TPU v7x, 512 devices: a whole 4x4x16 slice. The times are simulated.
512 devices in a mesh: replica: 4 (over x), fsdp: 128 (over y, z, core).
Axes of the slice: x: 4, y: 4, z: 16, core: 2. Of those that a mesh axis runs over, the one named last changes fastest.
Arguments:
- pseudo_grads: bfloat16 [4, 6144, 16384], P('replica', 'fsdp')
- outer_params: float32 [6144, 16384], P('replica', 'fsdp'), may hold values from -6 to 6
- momentum: float32 [6144, 16384], P('replica', 'fsdp'), may hold values from -0.6 to 0.6
- clip_level: float32 [1], replicated, may hold values from 0.05 to 0.2
- block_picks: int32 [4, 128, 4, 6], P(None, 'fsdp'), may hold values from -1 to 11, as said below
- cutoffs: int32 [4, 128, 4, 6], P(None, 'fsdp'), may hold values from 104 to 254
Outputs:
- new_params: float32 [6144, 16384], P('replica', 'fsdp')
- new_momentum: float32 [6144, 16384], P('replica', 'fsdp')
Inputs may be any that keep to these rules, and one draw needn't show every extreme that they name: block_picks[r, o, q, :] holds 1 to 6 different block indices followed by -1 in the remaining slots; in every draw some o and q have 6 indices from every worker r.
All inputs are finite; a program needn't handle non-finite values.
Results may differ from a plain program's by a relative error of at most 0.004.
Values may be sent and summed in bfloat16 or wider, within the bound.
No kernel may reach another device: no remote copies, remote signals or barrier semaphores. Data moves between devices by JAX's collectives and lax.ppermute only.
A program may use at most 64 MiB of HBM per device.

v0:
```python
import math

import jax
import jax.numpy as jnp
from jax import lax
from jax.sharding import PartitionSpec as P

BS = 128
D = 6144
FF = 16384


OUTER_RATE = 0.7
NESTEROV = 0.9
EPSILON = 1e-06
HIGH = lax.Precision.HIGHEST


def cosine_table(length):
    rows_idx = jnp.arange(length, dtype=jnp.float32)[:, None]
    cols_idx = jnp.arange(length, dtype=jnp.float32)[None, :]
    table = jnp.cos(math.pi * (2.0 * cols_idx + 1.0) * rows_idx / (2.0 * length)) * math.sqrt(
        2.0 / length
    )
    return jnp.where(rows_idx == 0.0, table * math.sqrt(0.5), table)


def forward_transform(table, blocks):
    halfway = jnp.einsum("uk,nbkl->nbul", table, blocks, precision=HIGH)
    return jnp.einsum("nbul,vl->nbuv", halfway, table, precision=HIGH)


def inverse_transform(table, blocks):
    halfway = jnp.einsum("uk,buv->bkv", table, blocks, precision=HIGH)
    return jnp.einsum("bkv,vl->bkl", halfway, table, precision=HIGH)


def per_device(pseudo_grads, outer_params, momentum, clip_level, block_picks, cutoffs):
    replicas = lax.axis_size("replica")
    owners = lax.axis_size("fsdp")
    replica_index = lax.axis_index("replica")
    table = cosine_table(BS)
    own_rows = pseudo_grads[0]
    rows_dev = own_rows.shape[0]
    col_width = own_rows.shape[1] // owners
    by_owner = own_rows.reshape(rows_dev, owners, col_width)
    frequency = jnp.arange(BS, dtype=jnp.int32)[:, None] + jnp.arange(BS, dtype=jnp.int32)[None, :]
    block_cols = col_width // BS
    landed = lax.all_to_all(by_owner, "fsdp", split_axis=1, concat_axis=0, tiled=True)
    block_rows = landed.shape[0] // (BS * replicas)
    owned = block_rows * block_cols
    blocks = landed.reshape(replicas, block_rows, BS, block_cols, BS)
    blocks = blocks.transpose(0, 1, 3, 2, 4).reshape(replicas, owned, BS, BS)
    block_ids = jnp.arange(owned, dtype=jnp.int32)
    sent_picks = lax.dynamic_index_in_dim(block_picks[:, 0], replica_index, 0, keepdims=False)
    sent_cuts = lax.dynamic_index_in_dim(cutoffs[:, 0], replica_index, 0, keepdims=False)
    pick_hit = sent_picks[..., None] == block_ids
    dense_coef = None
    coefficients = forward_transform(table, blocks.astype(jnp.float32))
    block_cut = jnp.max(jnp.where(pick_hit, sent_cuts[..., None], -1), axis=1)
    dense_coef = jnp.where(frequency <= block_cut[..., None, None], coefficients, jnp.float32(0.0))
    summed = lax.psum_scatter(dense_coef, "replica", scatter_dimension=0, tiled=True)[0]
    square_total = lax.psum(jnp.sum(summed * summed), ("replica", "fsdp"))
    factor = jnp.minimum(
        jnp.float32(1.0), clip_level[0] * math.sqrt(D * FF) / (jnp.sqrt(square_total) + EPSILON)
    )
    spatial = inverse_transform(table, summed * factor)
    update = (
        spatial.reshape(block_rows, block_cols, BS, BS)
        .transpose(0, 2, 1, 3)
        .reshape(block_rows * BS, block_cols * BS)
    )
    new_momentum = NESTEROV * momentum + update
    new_params = outer_params - OUTER_RATE * (update + NESTEROV * new_momentum)
    return (new_params, new_momentum)


def solution(mesh):
    in_specs = (
        P("replica", "fsdp", None),
        P("replica", "fsdp"),
        P("replica", "fsdp"),
        P(),
        P(None, "fsdp", None, None),
        P(None, "fsdp", None, None),
    )
    out_specs = (P("replica", "fsdp"), P("replica", "fsdp"))
    return jax.shard_map(
        per_device, mesh=mesh, in_specs=in_specs, out_specs=out_specs, check_vma=False
    )
```

profile of v0, /device:TPU:1, one launch (start us, length us, event | category | flops | bytes accessed | tf_op | source)
XLA Modules:
  0.0 273.7 jit_solution(4376459166112878310)
XLA Ops:
  7.2 1.8 copy.22
  9.0 2.2 copy.16
  11.1 20.6 %all-to-all-start = ((bf16[48,128,128]{2,0,1:T(8,128)(2,1)}), bf16[48,128,128]{2,0,1:T(8,128)(2,1)S(1)}, u32[]{:S(2)}, u32[]{:S(2)}) async-start(bf16[48,128,128]{2,0,1:T(8,128)(2,1)} %copy.16), calls=%async_computation | async-start | bytes 3145728 | tf_op jit(solution)/shard_map/all_to_all | solution.py:49
  31.7 0.0 reduce-scatter.2.cloned.1.call-start
  31.8 0.7 dynamic-slice_bitcast_fusion
  32.5 0.1 copy.14
  32.6 0.1 copy.15
  32.7 0.1 select_reduce_fusion
  32.8 75.7 %all-to-all-done = bf16[48,128,128]{2,0,1:T(8,128)(2,1)S(1)} async-done(((bf16[48,128,128]{2,0,1:T(8,128)(2,1)}), bf16[48,128,128]{2,0,1:T(8,128)(2,1)S(1)}, u32[]{:S(2)}, u32[]{:S(2)}) %all-to-all-start) | async-done | bytes 1572896 | tf_op jit(solution)/shard_map/all_to_all | solution.py:49
  108.5 1.7 fusion.10
  110.2 4.5 %compare_select_fusion = f32[4,12,128,128]{3,2,1,0:T(8,128)} fusion(f32[128,4,12,128]{3,0,2,1:T(8,128)S(1)} %fusion.10, s32[4,12]{1,0:T(4,128)S(1)} %select_reduce_fusion, s32[128,128]{1,0:T(8,128)S(1)} %iota_add_fusion, f32[128]{0:T(128)S(1)} %add_multiply_fusion, pred[128]{0:T(512)(128)(4,1)S(1)} %iota_compare_fusion.1), kind=kOutput, calls=%fused_computation.2 | convolution fusion | flops 1209614336 | bytes 6357824 | tf_op jit(solution)/shard_map/nbul,vl->nbuv/dot_general | solution.py:30
  114.7 0.0 copy-start
  114.7 0.0 copy-start.1
  114.7 0.0 reduce-scatter.2.cloned.1.call-update
  115.5 38.6 %reduce-scatter.2.cloned.1.call-done = f32[1,12,128,128]{3,2,1,0:T(8,128)} async-done(((f32[4,12,128,128]{3,2,1,0:T(8,128)}), f32[1,12,128,128]{3,2,1,0:T(8,128)}) %reduce-scatter.2.cloned.1.call-update) | async-done | bytes 786448 | tf_op jit(solution)/shard_map/reduce_scatter | solution.py:62
  154.2 1.9 multiply_reduce_fusion
  156.1 104.4 %psum.7 = f32[]{:T(128)} all-reduce(f32[]{:T(128)} %multiply_reduce_fusion), channel_id=1, replica_groups=mesh['replica'=4,'fsdp'=128] {'replica','fsdp'}, use_global_device_ids=true, to_apply=%region_3.4 | all-reduce | flops 1 | bytes 8 | tf_op jit(solution)/shard_map/psum | solution.py:63
  261.2 2.7 convolution_bitcast_fusion
  263.9 1.5 fusion.12
  265.5 0.0 copy-done
  265.5 0.0 copy-done.1
  265.5 1.3 fusion.5
  (3 shorter events, 0.0 us)
Async XLA Ops:
  11.1 97.3 %all-to-all-start = ((bf16[48,128,128]{2,0,1:T(8,128)(2,1)}), bf16[48,128,128]{2,0,1:T(8,128)(2,1)S(1)}, u32[]{:S(2)}, u32[]{:S(2)}) async-start(bf16[48,128,128]{2,0,1:T(8,128)(2,1)} %copy.16), calls=%async_computation | async-start | bytes 3145728 | tf_op jit(solution)/shard_map/all_to_all | solution.py:49
  31.7 122.4 %reduce-scatter.2.cloned.1.call-start = ((), (), s32[]{:S(2)}) async-start(), calls=%async_computation.2 | async-start | bytes 3932160 | tf_op jit(solution)/shard_map/reduce_scatter | solution.py:62
  114.7 150.7 %copy-start = (f32[1536,128]{1,0:T(8,128)S(1)}, f32[1536,128]{1,0:T(8,128)}, u32[]{:S(2)}) copy-start(f32[1536,128]{1,0:T(8,128)} %param.7) | copy-start | bytes 2359300
  114.7 150.8 %copy-start.1 = (f32[1536,128]{1,0:T(8,128)S(1)}, f32[1536,128]{1,0:T(8,128)}, u32[]{:S(2)}) copy-start(f32[1536,128]{1,0:T(8,128)} %param.8) | copy-start | bytes 2359300
Sparse Core Ops, SparseCore 0:
  114.9 39.2 reduce-scatter.1
where the time goes:
time: 274 us
  waiting for transfers between devices  114 us (42%)
  blocking collectives  104 us (38%)
  starting transfers between devices  20.6 us (8%)
  between operations  15.6 us (6%)
  matrix products  10.5 us (4%)
  local copies, waits for them, and re-layouts  4.88 us (2%)
  other arithmetic  3.38 us (1%)
    psum x1, blocking collectives, per_device(): square_total = lax.psum(jnp.sum(summed * summed), ('replica', 'fsdp'))  104 us
    all_to_all x1, waiting for transfers between devices, per_device(): lax.all_to_all(by_owner, 'fsdp', split_axis=1, concat_axis=0, tiled=True)  75.7 us
    reduce_scatter x1, waiting for transfers between devices, per_device(): lax.psum_scatter(dense_coef, 'replica', scatter_dimension=0, tiled=True)[0]  38.6 us
    all_to_all x1, starting transfers between devices, per_device(): lax.all_to_all(by_owner, 'fsdp', split_axis=1, concat_axis=0, tiled=True)  20.6 us
  transfers between devices with their start and end apart: 2, of which 2 were waited for; matrix products, arithmetic and copies ran while one was open for 0% of the time, Pallas kernels for 0%

commit v1 on v0

v1 whole, which is shorter than its diff:
```python
import math

import jax
import jax.numpy as jnp
import ml_dtypes
import numpy as np
from jax import lax
from jax.experimental import pallas as pl
from jax.experimental.pallas import tpu as pltpu
from jax.sharding import Mesh, PartitionSpec as P

BS = 128
D = 6144
FF = 16384
OUTER_RATE = 0.7
NESTEROV = 0.9
EPSILON = 1e-06
NX, NY, NZ, NC = 4, 4, 16, 2
BPO = 12
TAIL = 16
F32 = jnp.float32
BF16 = jnp.bfloat16


def table_parts():
    u = np.arange(BS, dtype=np.float64)[:, None]
    k = np.arange(BS, dtype=np.float64)[None, :]
    c = np.cos(math.pi * (2.0 * k + 1.0) * u / (2.0 * BS)) * math.sqrt(2.0 / BS)
    c[0] *= math.sqrt(0.5)
    hi = c.astype(ml_dtypes.bfloat16)
    lo = (c - hi.astype(np.float64)).astype(ml_dtypes.bfloat16)
    return hi, lo


def dot(a, b):
    return lax.dot_general(a, b, (((1,), (0,)), ((), ())), preferred_element_type=F32)


def split(v):
    hi = v.astype(BF16)
    return hi, (v - hi.astype(F32)).astype(BF16)


def times_wide(v, wide):
    hi, lo = split(v)
    both = dot(hi, wide)
    return both[:, :BS] + both[:, BS:] + dot(lo, wide[:, :BS])


def tall_times(tall, v):
    hi, lo = split(v)
    both = dot(tall, hi)
    return both[:BS] + both[BS:] + dot(tall[:BS], lo)


def pack_kernel(pos, g, out):
    c = pos[1]
    for cc in range(2):
        core = c if cc == 0 else 1 - c
        for m in range(4):
            for w in range(4):
                start = pl.multiple_of((2 * (4 * w + m) + core) * BS, BS)
                out[0, cc, 4 * m + w] = g[:, pl.ds(start, BS)]


def by_place(pos, mine, other, body):
    for p in range(4):
        for c in range(2):

            @pl.when((pos[0] == p) & (pos[1] == c))
            def _(p=p, c=c):
                if c == 0:
                    body(p, mine, other)
                else:
                    body(p, other, mine)


def exchange_kernel(pos, mine, other, a, b):
    def body(p, lo, hi):
        if p in (0, 3):
            s = slice(0, 4) if p == 0 else slice(12, 16)
            a[:, :, 0:48] = lo[:, s]
            a[:, :, 48:96] = hi[:, s]
            return
        for k in range(3):
            if p == 1:
                a[:, :, 32 * k : 32 * k + 32] = lo[:, 4 * k + 4 : 4 * k + 8, 0:32]
            else:
                a[:, :, 32 * k : 32 * k + 32] = hi[:, 4 * k : 4 * k + 4, 16:48]
        if p == 1:
            b[:, :, 0:16] = lo[:, 0:8, 32:48]
            b[:, :, 16:64] = hi[:, 0:8]
        else:
            b[:, :, 0:48] = lo[:, 8:16]
            b[:, :, 48:64] = hi[:, 8:16, 0:16]

    by_place(pos, mine, other, body)


def assemble(pos, mine, other, a, b, x):
    def body(p, lo, hi):
        for k in range(3):
            m = k + (k >= p)
            d = slice(4 * k, 4 * k + 4)
            s = slice(4 * m, 4 * m + 4)
            third = slice(32 * k, 32 * k + 32)
            if p == 0:
                x[:, d, 0:48] = lo[:, s]
                x[:, d, 48:96] = hi[:, s]
                x[:, d, 96:128] = a[:, :, third]
            elif p == 3:
                x[:, d, 0:32] = a[:, :, third]
                x[:, d, 32:80] = lo[:, s]
                x[:, d, 80:128] = hi[:, s]
            elif p == 1 and m == 0:
                x[:, d, 0:96] = a[:, :, :]
                x[:, d, 96:128] = lo[:, s, 0:32]
            elif p == 1:
                x[:, d, 0:16] = lo[:, s, 32:48]
                x[:, d, 16:64] = hi[:, s]
                x[:, d, 64:128] = b[:, 4 * (m - 2) : 4 * (m - 2) + 4]
            elif m == 3:
                x[:, d, 0:32] = hi[:, s, 16:48]
                x[:, d, 32:128] = a[:, :, :]
            else:
                x[:, d, 0:64] = b[:, s]
                x[:, d, 64:112] = lo[:, s]
                x[:, d, 112:128] = hi[:, s, 0:16]

    by_place(pos, mine, other, body)


def exponent(size):
    return jnp.clip(jnp.floor(jnp.log2(jnp.maximum(size, F32(1e-30)))) + 1.0, -100.0, 200.0)


def forward_kernel(pos, cut, mine, other, a, b, tall, wide, out, x, exps):
    assemble(pos, mine, other, a, b, x)
    p = pos[0]
    freq = lax.broadcasted_iota(jnp.int32, (BS, BS), 0) + lax.broadcasted_iota(jnp.int32, (BS, BS), 1)
    exps[...] = jnp.zeros_like(exps)
    for w in range(4):
        out[4 * w + p, 0:BS] = jnp.zeros((BS, BS), jnp.int16)

    def step(i, square):
        k = i // 4
        m = k + (k >= p).astype(jnp.int32)
        blk = p - (p > m).astype(jnp.int32)
        zq = 4 * (i % 4) + m
        total = jnp.zeros((BS, BS), F32)
        for r in range(NX):
            both = dot(x[r, i], wide[...])
            coef = tall_times(tall[...], both[:, :BS] + both[:, BS:])
            total += jnp.where(freq <= cut[zq, 4 * blk + r], coef, 0.0)
        e = exponent(jnp.max(jnp.abs(total), axis=0, keepdims=True))
        code = jnp.clip(jnp.floor(total * jnp.exp2(15.0 - e) + 0.5), -32767.0, 32767.0)
        out[zq, 0:BS] = code.astype(jnp.int32).astype(jnp.int16)
        exps[pl.ds(zq, 1), :] = e
        return square + jnp.sum(total * total, axis=0, keepdims=True)

    square = lax.fori_loop(0, BPO, step, jnp.zeros((1, BS), F32))
    e = exponent(square)
    scaled = jnp.minimum(square, F32(3e38)) * jnp.exp2(-0.5 * e) * jnp.exp2(-0.5 * e) * 16384.0
    d1 = jnp.floor(scaled)
    d2 = jnp.floor((scaled - d1) * 16384.0)
    e = jnp.where(square > F32(3e38), 200.0, e)
    row = lax.broadcasted_iota(jnp.int32, (TAIL, BS), 0)
    tail = jnp.where(row == 1, e, jnp.where(row == 2, d1, jnp.where(row == 3, d2, 0.0)))
    for s in range(NZ):
        mix = jnp.where(row == 0, exps[s : s + 1, :], tail)
        out[s, BS : BS + TAIL] = mix.astype(jnp.int32).astype(jnp.int16)


def compact_kernel(pos, z, out, norm):
    p = pos[0]
    row = lax.broadcasted_iota(jnp.int32, (TAIL, BS), 0)
    tail = jnp.zeros((TAIL, BS), F32)
    for g in range(4):
        for blk in range(3):
            src = 4 * g + blk + (p <= blk).astype(jnp.int32)
            n = 3 * g + blk
            out[BS * n : BS * n + BS] = z[src, 0:BS]
            e = z[src, BS : BS + TAIL].astype(jnp.int32).astype(F32)[0:1]
            tail = jnp.where(row == n, e, tail)
    out[BS * BPO : BS * BPO + TAIL] = tail.astype(jnp.int32).astype(jnp.int16)
    total = jnp.zeros((1, BS), F32)
    for s in range(NZ):
        t = z[s, BS : BS + TAIL].astype(jnp.int32).astype(F32)
        part = t[2:3] * F32(1.0 / 16384.0) + t[3:4] * F32(1.0 / 16384.0**2)
        total += part * jnp.exp2(0.5 * t[1:2]) * jnp.exp2(0.5 * t[1:2])
    norm[...] = jnp.broadcast_to(total[None], norm.shape)


def update_kernel(code, tail, norm, clip, params, mom, tall, wide, new_p, new_m):
    i = pl.program_id(0)
    total = jnp.sum(jnp.sum(norm[...], axis=0), axis=1, keepdims=True)
    factor = jnp.minimum(F32(1.0), clip[0] * F32(math.sqrt(D * FF)) / (jnp.sqrt(total) + F32(EPSILON)))
    row = lax.broadcasted_iota(jnp.int32, (TAIL, BS), 0)
    exps = tail[...].astype(jnp.int32).astype(F32)
    per = code.shape[0] // BS
    for n in range(per):
        e = jnp.sum(jnp.where(row == per * i + n, exps, 0.0), axis=0, keepdims=True)
        d = slice(BS * n, BS * n + BS)
        coef = code[d].astype(jnp.int32).astype(F32) * (jnp.exp2(e - 15.0) * factor)
        upd = tall_times(tall[...], times_wide(coef, wide[...]))
        nm = NESTEROV * mom[d] + upd
        new_m[d] = nm
        new_p[d] = params[d] - OUTER_RATE * (upd + NESTEROV * nm)


SMEM = pl.BlockSpec(memory_space=pltpu.SMEM)
VMEM = pl.BlockSpec(memory_space=pltpu.VMEM)
BIG = pltpu.CompilerParams(vmem_limit_bytes=40 * 1024 * 1024)


def per_device(pseudo_grads, outer_params, momentum, clip_level, block_picks, cutoffs):
    z = lax.axis_index("z")
    pos = jnp.stack([z % 4, lax.axis_index("c")]).astype(jnp.int32)
    hi, lo = table_parts()
    fwd_wide = jnp.asarray(np.concatenate([hi.T, lo.T], axis=1))
    fwd_tall = jnp.asarray(np.concatenate([hi, lo], axis=0))
    inv_wide = jnp.asarray(np.concatenate([hi, lo], axis=1))
    inv_tall = jnp.asarray(np.concatenate([hi.T, lo.T], axis=0))
    rows = pseudo_grads.shape[1]

    packed = pl.pallas_call(
        pack_kernel,
        out_shape=jax.ShapeDtypeStruct((NY, NC, NZ, rows, BS), BF16),
        grid=(NY,),
        in_specs=[SMEM, pl.BlockSpec((None, rows, FF // NY), lambda j: (0, 0, j))],
        out_specs=pl.BlockSpec((1, NC, NZ, rows, BS), lambda j: (j, 0, 0, 0, 0)),
        compiler_params=BIG,
        name="pack",
    )(pos, pseudo_grads)
    spread = lax.all_to_all(packed, "x", 0, 0, tiled=True)
    other = lax.ppermute(spread[:, 1], "c", [(0, 1), (1, 0)])

    half = pl.BlockSpec((NX, None, NZ, rows, BS), lambda i: (0, 0, 0, 0, 0))
    a, b = pl.pallas_call(
        exchange_kernel,
        out_shape=(
            jax.ShapeDtypeStruct((NX, 4, 96, BS), BF16),
            jax.ShapeDtypeStruct((NX, 8, 64, BS), BF16),
        ),
        grid=(1,),
        in_specs=[SMEM, half, VMEM],
        out_specs=(VMEM, VMEM),
        compiler_params=BIG,
        name="exchange",
    )(pos, spread, other)

    hit = block_picks[:, 0, :, :, None] == jnp.arange(BPO, dtype=jnp.int32)
    cut = jnp.max(jnp.where(hit, cutoffs[:, 0, :, :, None], -1), axis=2)
    cut = cut.transpose(1, 2, 0).reshape(NY, 4, 1, 12)
    cut = jnp.broadcast_to(cut, (NY, 4, 4, 12)).reshape(NY * NZ, 1, 12)
    cut = jnp.pad(cut, ((0, 0), (0, 0), (0, BS - 12)))
    cut, a, b = lax.optimization_barrier((cut, a, b))

    pair_a, pair_b = [], []
    for g in range(0, NZ, 4):
        pair_a += [(g, g + 1), (g + 1, g), (g + 2, g + 3), (g + 3, g + 2)]
        pair_b += [(g + 1, g + 2), (g + 2, g + 1)]
    a = lax.ppermute(a, "z", pair_a)
    b = lax.ppermute(b, "z", pair_b)
    cut = lax.all_to_all(cut, ("y", "z"), 0, 0, tiled=True)
    cut = lax.dynamic_slice_in_dim(cut[:, 0], lax.axis_index("x") * NZ, NZ, 0)

    coded = pl.pallas_call(
        forward_kernel,
        out_shape=jax.ShapeDtypeStruct((NZ, BS + TAIL, BS), jnp.int16),
        grid=(1,),
        in_specs=[SMEM, SMEM, half, VMEM, VMEM, VMEM, VMEM, VMEM],
        out_specs=VMEM,
        scratch_shapes=[
            pltpu.VMEM((NX, BPO, BS, BS), BF16),
            pltpu.VMEM((NZ, BS), F32),
        ],
        compiler_params=BIG,
        name="forward",
    )(pos, cut, spread, other, a, b, fwd_tall, fwd_wide)
    coded = lax.all_to_all(coded, "z", 0, 0, tiled=True)

    coded, norm = pl.pallas_call(
        compact_kernel,
        out_shape=(
            jax.ShapeDtypeStruct((BPO * BS + TAIL, BS), jnp.int16),
            jax.ShapeDtypeStruct((NX * NY * NC, 1, BS), F32),
        ),
        in_specs=[SMEM, VMEM],
        out_specs=(VMEM, VMEM),
        compiler_params=BIG,
        name="compact",
    )(pos, coded)
    swap = [(NY * i + j, NX * j + i) for i in range(NX) for j in range(NY)]
    coded = lax.ppermute(coded, ("x", "y"), swap)
    norm = lax.all_to_all(norm, ("x", "y", "c"), 0, 0, tiled=True)

    per = 3
    steps = BPO // per
    tile = pl.BlockSpec((per * BS, BS), lambda i: (i, 0))

    def whole(*shape):
        return pl.BlockSpec(shape, lambda i: (0,) * len(shape))

    return pl.pallas_call(
        update_kernel,
        out_shape=(
            jax.ShapeDtypeStruct(outer_params.shape, F32),
            jax.ShapeDtypeStruct(outer_params.shape, F32),
        ),
        grid=(steps,),
        in_specs=[
            tile,
            pl.BlockSpec((TAIL, BS), lambda i: (BPO * BS // TAIL, 0)),
            whole(NX * NY * NC, 1, BS),
            SMEM,
            tile,
            tile,
            whole(2 * BS, BS),
            whole(BS, 2 * BS),
        ],
        out_specs=(tile, tile),
        compiler_params=BIG,
        name="update",
    )(coded, coded, norm, clip_level, outer_params, momentum, inv_tall, inv_wide)


def solution(mesh):
    grid = Mesh(mesh.devices.reshape(NX, NY, NZ, NC), ("x", "y", "z", "c"))
    yzc = ("y", "z", "c")
    in_specs = (P("x", yzc, None), P("x", yzc), P("x", yzc), P(), P(None, yzc, None, None), P(None, yzc, None, None))
    out_specs = (P("x", yzc), P("x", yzc))
    return jax.shard_map(per_device, mesh=grid, in_specs=in_specs, out_specs=out_specs, check_vma=False)
```

time: 274 us -> 145 us (0.53)
  waiting for transfers between devices: 114 us -> 24.3 us
  blocking collectives: 104 us -> 55 us
  starting transfers between devices: 20.6 us -> 43.8 us
  Pallas kernels: 0 us -> 17.3 us
  between operations: 15.6 us -> 1.47 us
  matrix products: 10.5 us -> 0 us
  other arithmetic: 3.38 us -> 0.2 us
    psum x1 -> x0, blocking collectives: 104 us -> none  [per_device(): square_total = lax.psum(jnp.sum(summed * summed), ('replica', 'fsdp'))]
    all_to_all x0 -> x2, blocking collectives: none -> 55 us  [the longest x1 34.3 us: per_device(): coded = lax.all_to_all(coded, 'z', 0, 0, tiled=True)]
    all_to_all x1 -> x2, waiting for transfers between devices: 75.7 us -> 23.6 us  [the longest x1 13.1 us: per_device(): cut = lax.all_to_all(cut, ('y', 'z'), 0, 0, tiled=True)]
    reduce_scatter x1 -> x0, waiting for transfers between devices: 38.6 us -> none  [per_device(): lax.psum_scatter(dense_coef, 'replica', scatter_dimension=0, tiled=True)[0]]
    pallas_call x0 -> x5, Pallas kernels: none -> 17.3 us  [the longest x1 10.1 us: per_device(): pl.pallas_call(forward_kernel, out_shape=jax.ShapeDtypeStruct((NZ, BS + T...]
    ppermute x0 -> x4, starting transfers between devices: none -> 15.4 us  [the longest x1 7.64 us: per_device(): other = lax.ppermute(spread[:, 1], 'c', [(0, 1), (1, 0)])]
    dot_general x4 -> x0, matrix products: 10.5 us -> none  [the longest x1 4.52 us: forward_transform(): return jnp.einsum('nbul,vl->nbuv', halfway, table, precision=HIGH)]
    all_to_all x1 -> x2, starting transfers between devices: 20.6 us -> 28.4 us  [the longest x1 16.7 us: per_device(): cut = lax.all_to_all(cut, ('y', 'z'), 0, 0, tiled=True)]
  transfers between devices with their start and end apart: 2 -> 6, of which waited for: 2 -> 3; matrix products, arithmetic and copies ran while one was open for 0% -> 1% of each run, Pallas kernels for 0% -> 0%
where the time goes in v1:
time: 145 us
  blocking collectives  55 us (38%)
  starting transfers between devices  43.8 us (30%)
  waiting for transfers between devices  24.3 us (17%)
  Pallas kernels  17.3 us (12%)
  local copies, waits for them, and re-layouts  2.57 us (2%)
  between operations  1.47 us (1%)
    all_to_all x1, blocking collectives, per_device(): coded = lax.all_to_all(coded, 'z', 0, 0, tiled=True)  34.3 us
    all_to_all x1, blocking collectives, per_device(): spread = lax.all_to_all(packed, 'x', 0, 0, tiled=True)  20.7 us
    all_to_all x1, starting transfers between devices, per_device(): cut = lax.all_to_all(cut, ('y', 'z'), 0, 0, tiled=True)  16.7 us
    all_to_all x1, waiting for transfers between devices, per_device(): cut = lax.all_to_all(cut, ('y', 'z'), 0, 0, tiled=True)  13.1 us
    all_to_all x1, starting transfers between devices, per_device(): norm = lax.all_to_all(norm, ('x', 'y', 'c'), 0, 0, tiled=True)  11.7 us
    all_to_all x1, waiting for transfers between devices, per_device(): norm = lax.all_to_all(norm, ('x', 'y', 'c'), 0, 0, tiled=True)  10.5 us
    pallas_call x1, Pallas kernels, per_device(): pl.pallas_call(forward_kernel, out_shape=jax.ShapeDtypeStruct((NZ, BS + T...  10.1 us
    ppermute x1, starting transfers between devices, per_device(): other = lax.ppermute(spread[:, 1], 'c', [(0, 1), (1, 0)])  7.64 us
  transfers between devices with their start and end apart: 6, of which 3 were waited for; matrix products, arithmetic and copies ran while one was open for 1% of the time, Pallas kernels for 0%

profile of v1, /device:TPU:1, one launch (start us, length us, event | category | flops | bytes accessed | tf_op | source)
XLA Modules:
  0.0 144.7 jit_solution(2433568707209133151)
XLA Ops:
  0.6 0.1 pad_add_fusion.pos
  0.7 0.0 copy-start
  0.7 1.4 copy-done
  2.1 1.2 pack.1
  3.3 20.7 %all_to_all.20.mine = bf16[4,2,16,48,128]{4,3,2,1,0:T(8,128)(2,1)S(1)} all-to-all(bf16[4,2,16,48,128]{4,3,2,1,0:T(8,128)(2,1)S(1)} %pack.1), channel_id=1, replica_groups=mesh['x'=4,'y'=4,'z'=16,'c'=2] {'x'}, dimensions={0} | all-to-all | bytes 3145728 | tf_op jit(solution)/shard_map/all_to_all | solution.py:235
  24.0 0.0 copy-start.7
  24.0 0.0 copy-start.8
  24.0 0.1 slice_bitcast_fusion
  24.1 0.0 copy-start.3
  24.1 0.0 copy-start.4
  24.1 7.6 %collective-permute-start = (bf16[4,16,48,128]{3,2,1,0:T(8,128)(2,1)S(1)}, bf16[4,16,48,128]{3,2,1,0:T(8,128)(2,1)S(1)}, u32[]{:S(2)}, u32[]{:S(2)}) collective-permute-start(bf16[4,16,48,128]{3,2,1,0:T(8,128)(2,1)S(1)} %slice_bitcast_fusion), channel_id=1, source_target_pairs={{0,1},{1,0},{2,3},{3,2},{4,5},{5,4},{6,7},{7,6},{8,9},{9,8},{10,11... | collective-permute-start | bytes 2359304 | tf_op jit(solution)/shard_map/ppermute | solution.py:236
  31.7 0.0 copy-done.7
  31.7 0.1 copy.19
  31.9 0.0 copy-done.8
  31.9 0.1 copy.20
  32.0 0.1 select_reduce_fusion
  32.1 0.1 copy.21
  32.2 0.1 broadcast_in_dim.25
  32.3 0.6 pad.4
  32.9 0.7 collective-permute-done.other
  33.6 1.6 %exchange.1 = (bf16[4,4,96,128]{3,2,1,0:T(8,128)(2,1)}, bf16[4,8,64,128]{3,2,1,0:T(8,128)(2,1)}) custom-call(s32[2]{0:T(128)S(1)} %pad_add_fusion.pos, bf16[4,2,16,48,128]{4,3,2,1,0:T(8,128)(2,1)S(1)} %all_to_all.20.mine, bf16[4,16,48,128]{3,2,1,0:T(8,128)(2,1)S(1)} %collective-permute-done.other), custom_call_target="tpu_custom_call" | custom-call | tf_op jit(solution)/shard_map/exchange/pallas_call | solution.py:239
  35.2 0.7 collective-permute-start.2
  35.9 6.4 %collective-permute-start.1 = (bf16[4,4,96,128]{3,2,1,0:T(8,128)(2,1)}, bf16[4,4,96,128]{3,2,1,0:T(8,128)(2,1)S(1)}, u32[]{:S(2)}, u32[]{:S(2)}) collective-permute-start(bf16[4,4,96,128]{3,2,1,0:T(8,128)(2,1)} %get-tuple-element.12), channel_id=1, source_target_pairs={{0,2},{2,0},{4,6},{6,4},{8,10},{10,8},{12,14},{14,12},{16,18},{18,... | collective-permute-start | bytes 1179656 | tf_op jit(solution)/shard_map/ppermute | solution.py:263
  42.3 16.7 %all-to-all-start.1 = ((s32[64,1,128]{2,1,0:T(1,128)}), s32[64,1,128]{2,1,0:T(1,128)S(1)}, u32[]{:S(2)}, u32[]{:S(2)}) async-start(s32[64,1,128]{2,1,0:T(1,128)} %pad.4), calls=%async_computation.1 | async-start | bytes 65536 | tf_op jit(solution)/shard_map/all_to_all | solution.py:265
  59.0 13.1 %all-to-all-done.1 = s32[64,1,128]{2,1,0:T(1,128)S(1)} async-done(((s32[64,1,128]{2,1,0:T(1,128)}), s32[64,1,128]{2,1,0:T(1,128)S(1)}, u32[]{:S(2)}, u32[]{:S(2)}) %all-to-all-start.1) | async-done | bytes 32800 | tf_op jit(solution)/shard_map/all_to_all | solution.py:265
  72.1 0.0 collective-permute-done.1.a
  72.1 0.0 collective-permute-done.2.b
  72.1 0.0 copy-done.3
  72.1 0.0 copy-done.4
  72.1 10.1 %forward.1 = s16[16,144,128]{2,1,0:T(8,128)(2,1)S(1)} custom-call(s32[2]{0:T(128)S(1)} %pad_add_fusion.pos, s32[16,128]{1,0:T(8,128)S(1)} %bitcast.11, bf16[4,2,16,48,128]{4,3,2,1,0:T(8,128)(2,1)S(1)} %all_to_all.20.mine, bf16[4,16,48,128]{3,2,1,0:T(8,128)(2,1)S(1)} %collective-permute-done.other, bf16[4,4,96,128]{3,2,1,0:T(8,128)(2,1)S(1)} %collective-permute-done.1.a, ...), custom_call_target="tpu_custom_call" | custom-call | tf_op jit(solution)/shard_map/forward/pallas_call | solution.py:268
  82.3 0.0 copy-start.1
  82.3 0.0 copy-start.2
  82.3 0.0 copy-start.5
  82.3 0.0 copy-start.6
  82.3 34.3 %all_to_all.21.z = s16[16,144,128]{2,1,0:T(8,128)(2,1)S(1)} all-to-all(s16[16,144,128]{2,1,0:T(8,128)(2,1)S(1)} %forward.1), channel_id=1, replica_groups=mesh['x'=4,'y'=4,'z'=16,'c'=2] {'z'}, dimensions={0} | all-to-all | bytes 1179648 | tf_op jit(solution)/shard_map/all_to_all | solution.py:281
  116.7 1.2 compact.1
  117.8 0.7 collective-permute-start.3
  118.5 11.7 %all-to-all-start.3 = ((f32[32,1,128]{2,1,0:T(1,128)}), f32[32,1,128]{2,1,0:T(1,128)S(1)}, u32[]{:S(2)}, u32[]{:S(2)}) async-start(f32[32,1,128]{2,1,0:T(1,128)} %get-tuple-element.15), calls=%async_computation.3 | async-start | bytes 32768 | tf_op jit(solution)/shard_map/all_to_all | solution.py:296
  130.9 10.5 %all-to-all-done.3.norm = f32[32,1,128]{2,1,0:T(1,128)S(1)} async-done(((f32[32,1,128]{2,1,0:T(1,128)}), f32[32,1,128]{2,1,0:T(1,128)S(1)}, u32[]{:S(2)}, u32[]{:S(2)}) %all-to-all-start.3) | async-done | bytes 16416 | tf_op jit(solution)/shard_map/all_to_all | solution.py:296
  141.4 0.0 collective-permute-done.3.code.tail
  141.4 0.0 copy-done.1
  141.4 0.0 copy-done.2
  141.4 0.0 copy-done.5
  141.4 0.0 copy-done.6
  141.4 3.2 %update.1 = (f32[1536,128]{1,0:T(8,128)}, f32[1536,128]{1,0:T(8,128)}) custom-call(s16[1552,128]{1,0:T(8,128)(2,1)S(1)} %collective-permute-done.3.code.tail, s16[1552,128]{1,0:T(8,128)(2,1)S(1)} %collective-permute-done.3.code.tail, f32[32,1,128]{2,1,0:T(1,128)S(1)} %all-to-all-done.3.norm, f32[1]{0:T(128)S(6)} %copy.24.clip, f32[1536,128]{1,0:T(8,128)S(1)} %copy-done.1, ...), custom_call_target="tpu_custom_call" | custom-call | tf_op jit(solution)/shard_map/update/pallas_call | solution.py:305
  (2 shorter events, 0.0 us)
Async XLA Ops:
  0.7 1.4 copy-start
  24.0 7.7 %copy-start.7 = (s32[4,1,4,6]{3,2,1,0:T(4,128)S(1)}, s32[4,1,4,6]{3,2,1,0:T(4,128)}, u32[]{:S(2)}) copy-start(s32[4,1,4,6]{3,2,1,0:T(4,128)} %param.14) | copy-start | bytes 1156
  24.0 7.9 %copy-start.8 = (s32[4,1,4,6]{3,2,1,0:T(4,128)S(1)}, s32[4,1,4,6]{3,2,1,0:T(4,128)}, u32[]{:S(2)}) copy-start(s32[4,1,4,6]{3,2,1,0:T(4,128)} %param.15) | copy-start | bytes 1156
  24.1 48.1 %copy-start.3 = (bf16[128,256]{1,0:T(8,128)(2,1)S(1)}, bf16[128,256]{1,0:T(8,128)(2,1)}, u32[]{:S(2)}) copy-start(bf16[128,256]{1,0:T(8,128)(2,1)} %constant.45.clone.wide) | copy-start | bytes 196612
  24.1 48.1 %copy-start.4 = (bf16[256,128]{1,0:T(8,128)(2,1)S(1)}, bf16[256,128]{1,0:T(8,128)(2,1)}, u32[]{:S(2)}) copy-start(bf16[256,128]{1,0:T(8,128)(2,1)} %constant.46.clone.tall) | copy-start | bytes 196612
  24.1 9.5 %collective-permute-start = (bf16[4,16,48,128]{3,2,1,0:T(8,128)(2,1)S(1)}, bf16[4,16,48,128]{3,2,1,0:T(8,128)(2,1)S(1)}, u32[]{:S(2)}, u32[]{:S(2)}) collective-permute-start(bf16[4,16,48,128]{3,2,1,0:T(8,128)(2,1)S(1)} %slice_bitcast_fusion), channel_id=1, source_target_pairs={{0,1},{1,0},{2,3},{3,2},{4,5},{5,4},{6,7},{7,6},{8,9},{9,8},{10,11... | collective-permute-start | bytes 2359304 | tf_op jit(solution)/shard_map/ppermute | solution.py:236
  35.2 36.9 %collective-permute-start.2 = (bf16[4,8,64,128]{3,2,1,0:T(8,128)(2,1)}, bf16[4,8,64,128]{3,2,1,0:T(8,128)(2,1)S(1)}, u32[]{:S(2)}, u32[]{:S(2)}) collective-permute-start(bf16[4,8,64,128]{3,2,1,0:T(8,128)(2,1)} %get-tuple-element.13), channel_id=1, source_target_pairs={{2,4},{4,2},{10,12},{12,10},{18,20},{20,18},{26,28},{28,26},{3,5},... | collective-permute-start | bytes 1572872 | tf_op jit(solution)/shard_map/ppermute | solution.py:264
  35.9 36.2 %collective-permute-start.1 = (bf16[4,4,96,128]{3,2,1,0:T(8,128)(2,1)}, bf16[4,4,96,128]{3,2,1,0:T(8,128)(2,1)S(1)}, u32[]{:S(2)}, u32[]{:S(2)}) collective-permute-start(bf16[4,4,96,128]{3,2,1,0:T(8,128)(2,1)} %get-tuple-element.12), channel_id=1, source_target_pairs={{0,2},{2,0},{4,6},{6,4},{8,10},{10,8},{12,14},{14,12},{16,18},{18,... | collective-permute-start | bytes 1179656 | tf_op jit(solution)/shard_map/ppermute | solution.py:263
  42.3 29.8 %all-to-all-start.1 = ((s32[64,1,128]{2,1,0:T(1,128)}), s32[64,1,128]{2,1,0:T(1,128)S(1)}, u32[]{:S(2)}, u32[]{:S(2)}) async-start(s32[64,1,128]{2,1,0:T(1,128)} %pad.4), calls=%async_computation.1 | async-start | bytes 65536 | tf_op jit(solution)/shard_map/all_to_all | solution.py:265
  82.3 59.1 %copy-start.1 = (f32[1536,128]{1,0:T(8,128)S(1)}, f32[1536,128]{1,0:T(8,128)}, u32[]{:S(2)}) copy-start(f32[1536,128]{1,0:T(8,128)} %params.1) | copy-start | bytes 2359300
  82.3 59.1 %copy-start.2 = (f32[1536,128]{1,0:T(8,128)S(1)}, f32[1536,128]{1,0:T(8,128)}, u32[]{:S(2)}) copy-start(f32[1536,128]{1,0:T(8,128)} %mom.1) | copy-start | bytes 2359300
  82.3 59.1 %copy-start.5 = (bf16[128,256]{1,0:T(8,128)(2,1)S(1)}, bf16[128,256]{1,0:T(8,128)(2,1)}, u32[]{:S(2)}) copy-start(bf16[128,256]{1,0:T(8,128)(2,1)} %constant.47.clone.wide) | copy-start | bytes 196612
  82.3 59.1 %copy-start.6 = (bf16[256,128]{1,0:T(8,128)(2,1)S(1)}, bf16[256,128]{1,0:T(8,128)(2,1)}, u32[]{:S(2)}) copy-start(bf16[256,128]{1,0:T(8,128)(2,1)} %constant.48.clone.tall) | copy-start | bytes 196612
  117.8 23.6 %collective-permute-start.3 = (s16[1552,128]{1,0:T(8,128)(2,1)S(1)}, s16[1552,128]{1,0:T(8,128)(2,1)S(1)}, u32[]{:S(2)}, u32[]{:S(2)}) collective-permute-start(s16[1552,128]{1,0:T(8,128)(2,1)S(1)} %get-tuple-element.14), channel_id=1, source_target_pairs={{0,0},{32,128},{64,256},{96,384},{128,32},{160,160},{192,288},{224... | collective-permute-start | bytes 1191944 | tf_op jit(solution)/shard_map/ppermute | solution.py:295
  118.5 22.9 %all-to-all-start.3 = ((f32[32,1,128]{2,1,0:T(1,128)}), f32[32,1,128]{2,1,0:T(1,128)S(1)}, u32[]{:S(2)}, u32[]{:S(2)}) async-start(f32[32,1,128]{2,1,0:T(1,128)} %get-tuple-element.15), calls=%async_computation.3 | async-start | bytes 32768 | tf_op jit(solution)/shard_map/all_to_all | solution.py:296

commit v2 on v1

v2 whole, which is shorter than its diff:
```python
import functools
import math

import jax
import jax.numpy as jnp
import ml_dtypes
import numpy as np
from jax import lax
from jax.experimental import pallas as pl
from jax.experimental.pallas import tpu as pltpu
from jax.sharding import Mesh, PartitionSpec as P

BS = 128
D = 6144
FF = 16384
OUTER_RATE = 0.7
NESTEROV = 0.9
EPSILON = 1e-06
NX, NY, NZ, NC = 4, 4, 16, 2
BPO = 12
TAIL = 16
F32 = jnp.float32
BF16 = jnp.bfloat16


def table_parts():
    u = np.arange(BS, dtype=np.float64)[:, None]
    k = np.arange(BS, dtype=np.float64)[None, :]
    c = np.cos(math.pi * (2.0 * k + 1.0) * u / (2.0 * BS)) * math.sqrt(2.0 / BS)
    c[0] *= math.sqrt(0.5)
    hi = c.astype(ml_dtypes.bfloat16)
    lo = (c - hi.astype(np.float64)).astype(ml_dtypes.bfloat16)
    return hi, lo


def dot(a, b):
    return lax.dot_general(a, b, (((1,), (0,)), ((), ())), preferred_element_type=F32)


def split(v):
    hi = v.astype(BF16)
    return hi, (v - hi.astype(F32)).astype(BF16)


def times_wide(v, wide):
    hi, lo = split(v)
    both = dot(hi, wide)
    return both[:, :BS] + both[:, BS:] + dot(lo, wide[:, :BS])


def tall_times(tall, v):
    hi, lo = split(v)
    both = dot(tall, hi)
    return both[:BS] + both[BS:] + dot(tall[:BS], lo)


def pack_kernel(pos, g, out):
    c = pos[1]
    for cc in range(2):
        core = c if cc == 0 else 1 - c
        for m in range(4):
            for w in range(4):
                start = pl.multiple_of((2 * (4 * w + m) + core) * BS, BS)
                out[0, cc, 4 * m + w] = g[:, pl.ds(start, BS)]


def by_place(pos, mine, other, body):
    mine = mine.at[:, 0]
    for p in range(4):
        for c in range(2):

            @pl.when((pos[0] == p) & (pos[1] == c))
            def _(p=p, c=c):
                if c == 0:
                    body(p, mine, other)
                else:
                    body(p, other, mine)


def exchange_kernel(pos, mine, other, a, b):
    def body(p, lo, hi):
        if p in (0, 3):
            s = slice(0, 4) if p == 0 else slice(12, 16)
            a[:, :, 0:48] = lo[:, s]
            a[:, :, 48:96] = hi[:, s]
            return
        for k in range(3):
            if p == 1:
                a[:, :, 32 * k : 32 * k + 32] = lo[:, 4 * k + 4 : 4 * k + 8, 0:32]
            else:
                a[:, :, 32 * k : 32 * k + 32] = hi[:, 4 * k : 4 * k + 4, 16:48]
        if p == 1:
            b[:, :, 0:16] = lo[:, 0:8, 32:48]
            b[:, :, 16:64] = hi[:, 0:8]
        else:
            b[:, :, 0:48] = lo[:, 8:16]
            b[:, :, 48:64] = hi[:, 8:16, 0:16]

    by_place(pos, mine, other, body)


def assemble(k, pos, mine, other, a, b, x):
    def body(p, lo, hi):
        m = k + (k >= p)
        s = slice(4 * m, 4 * m + 4)
        third = slice(32 * k, 32 * k + 32)
        if p == 0:
            x[:, :, 0:48] = lo[:, s]
            x[:, :, 48:96] = hi[:, s]
            x[:, :, 96:128] = a[:, :, third]
        elif p == 3:
            x[:, :, 0:32] = a[:, :, third]
            x[:, :, 32:80] = lo[:, s]
            x[:, :, 80:128] = hi[:, s]
        elif p == 1 and m == 0:
            x[:, :, 0:96] = a[:, :, :]
            x[:, :, 96:128] = lo[:, s, 0:32]
        elif p == 1:
            x[:, :, 0:16] = lo[:, s, 32:48]
            x[:, :, 16:64] = hi[:, s]
            x[:, :, 64:128] = b[:, 4 * (m - 2) : 4 * (m - 2) + 4]
        elif m == 3:
            x[:, :, 0:32] = hi[:, s, 16:48]
            x[:, :, 32:128] = a[:, :, :]
        else:
            x[:, :, 0:64] = b[:, s]
            x[:, :, 64:112] = lo[:, s]
            x[:, :, 112:128] = hi[:, s, 0:16]

    by_place(pos, mine, other, body)


def exponent(size):
    return jnp.clip(jnp.floor(jnp.log2(jnp.maximum(size, F32(1e-30)))) + 1.0, -100.0, 200.0)


def forward_kernel(k, pos, cut, mine, other, a, b, tall, wide, out, square, x):
    assemble(k, pos, mine, other, a, b, x)
    p = pos[0]
    m = k + (k >= p).astype(jnp.int32)
    blk = p - (p > m).astype(jnp.int32)
    freq = lax.broadcasted_iota(jnp.int32, (BS, BS), 0) + lax.broadcasted_iota(jnp.int32, (BS, BS), 1)
    row = lax.broadcasted_iota(jnp.int32, (TAIL, BS), 0)
    tail = jnp.zeros((TAIL, BS), F32)
    squares = jnp.zeros((1, BS), F32)
    for w in range(4):
        total = jnp.zeros((BS, BS), F32)
        for r in range(NX):
            both = dot(x[r, w], wide[...])
            hi, lo = split(both[:, :BS] + both[:, BS:])
            four = dot(tall[...], jnp.concatenate([hi, lo], axis=1))
            coef = four[:BS, :BS] + (four[BS:, :BS] + four[:BS, BS:])
            total += jnp.where(freq <= cut[4 * w + m, 4 * blk + r], coef, 0.0)
        e = exponent(jnp.max(jnp.abs(total), axis=0, keepdims=True))
        code = jnp.clip(jnp.floor(total * jnp.exp2(15.0 - e) + 0.5), -32767.0, 32767.0)
        out[BS * w : BS * w + BS] = code.astype(jnp.int32).astype(jnp.int16)
        tail = jnp.where(row == w, e, tail)
        squares += jnp.sum(total * total, axis=0, keepdims=True)
    out[4 * BS : 4 * BS + TAIL] = tail.astype(jnp.int32).astype(jnp.int16)
    square[...] = squares


def slots_kernel(pos, c0, c1, c2, norm, out):
    p = pos[0]
    square = jnp.sum(norm[...], axis=0)
    e = exponent(square)
    scaled = jnp.minimum(square, F32(3e38)) * jnp.exp2(-0.5 * e) * jnp.exp2(-0.5 * e) * 16384.0
    d1 = jnp.floor(scaled)
    d2 = jnp.floor((scaled - d1) * 16384.0)
    e = jnp.where(square > F32(3e38), 200.0, e)
    row = lax.broadcasted_iota(jnp.int32, (TAIL, BS), 0)
    tail = jnp.where(row == 1, e, jnp.where(row == 2, d1, jnp.where(row == 3, d2, 0.0)))
    for k in range(3):
        code = (c0, c1, c2)[k]
        m = k + (k >= p).astype(jnp.int32)
        exps = code[4 * BS : 4 * BS + TAIL].astype(jnp.int32).astype(F32)
        for w in range(4):
            out[4 * w + m, 0:BS] = code[BS * w : BS * w + BS]
            mix = jnp.where(row == 0, exps[w : w + 1], tail)
            out[4 * w + m, BS : BS + TAIL] = mix.astype(jnp.int32).astype(jnp.int16)
    tail = tail.astype(jnp.int32).astype(jnp.int16)
    for w in range(4):
        out[4 * w + p, 0:BS] = jnp.zeros((BS, BS), jnp.int16)
        out[4 * w + p, BS : BS + TAIL] = tail


def update_kernel(pos, z, clip, params, mom, tall, wide, new_p, new_m):
    g = pl.program_id(0)
    p = pos[0]
    total = jnp.zeros((1, BS), F32)
    for s in range(NZ):
        t = z[s, BS : BS + TAIL].astype(jnp.int32).astype(F32)
        part = t[2:3] * F32(1.0 / 16384.0) + t[3:4] * F32(1.0 / 16384.0**2)
        total += part * jnp.exp2(0.5 * t[1:2]) * jnp.exp2(0.5 * t[1:2])
    total = jnp.sum(total, axis=1, keepdims=True)
    factor = jnp.minimum(F32(1.0), clip[0] * F32(math.sqrt(D * FF)) / (jnp.sqrt(total) + F32(EPSILON)))
    for n in range(3):
        src = 4 * g + n + (p <= n).astype(jnp.int32)
        e = z[src, BS : BS + TAIL].astype(jnp.int32).astype(F32)[0:1]
        d = slice(BS * n, BS * n + BS)
        coef = z[src, 0:BS].astype(jnp.int32).astype(F32) * (jnp.exp2(e - 15.0) * factor)
        upd = tall_times(tall[...], times_wide(coef, wide[...]))
        nm = NESTEROV * mom[d] + upd
        new_m[d] = nm
        new_p[d] = params[d] - OUTER_RATE * (upd + NESTEROV * nm)


SMEM = pl.BlockSpec(memory_space=pltpu.SMEM)
VMEM = pl.BlockSpec(memory_space=pltpu.VMEM)
BIG = pltpu.CompilerParams(vmem_limit_bytes=40 * 1024 * 1024)


def call(kernel, out_shape, inputs, name, scratch=()):
    return pl.pallas_call(
        kernel,
        out_shape=out_shape,
        in_specs=[SMEM if i.dtype == jnp.int32 else VMEM for i in inputs],
        out_specs=jax.tree.map(lambda _: VMEM, out_shape),
        scratch_shapes=scratch,
        compiler_params=BIG,
        name=name,
    )(*inputs)


def per_device(pseudo_grads, outer_params, momentum, clip_level, block_picks, cutoffs):
    z = lax.axis_index("z")
    pos = jnp.stack([z % 4, lax.axis_index("c")]).astype(jnp.int32)
    hi, lo = table_parts()
    fwd_wide = jnp.asarray(np.concatenate([hi.T, lo.T], axis=1))
    fwd_tall = jnp.asarray(np.concatenate([hi, lo], axis=0))
    inv_wide = jnp.asarray(np.concatenate([hi, lo], axis=1))
    inv_tall = jnp.asarray(np.concatenate([hi.T, lo.T], axis=0))
    rows = pseudo_grads.shape[1]
    swap = [(NY * i + j, NX * j + i) for i in range(NX) for j in range(NY)]
    shape = jax.ShapeDtypeStruct

    picks, cuts = (
        lax.dynamic_index_in_dim(v[:, 0], lax.axis_index("x"), 1, keepdims=False) for v in (block_picks, cutoffs)
    )
    hit = picks[:, :, None] == jnp.arange(BPO, dtype=jnp.int32)
    cut = jnp.max(jnp.where(hit, cuts[:, :, None], -1), axis=1)
    cut = jnp.pad(cut.T.reshape(4, BPO), ((0, 4), (0, BS - BPO)))
    cut = lax.ppermute(cut, ("x", "y"), swap)

    packed = pl.pallas_call(
        pack_kernel,
        out_shape=shape((NY, NC, NZ, rows, BS), BF16),
        grid=(NY,),
        in_specs=[SMEM, pl.BlockSpec((None, rows, FF // NY), lambda j: (0, 0, j))],
        out_specs=pl.BlockSpec((1, NC, NZ, rows, BS), lambda j: (j, 0, 0, 0, 0)),
        compiler_params=BIG,
        name="pack",
    )(pos, pseudo_grads)
    spread = lax.all_to_all(packed, "x", 0, 0, tiled=True)
    other = lax.ppermute(spread[:, 1], "c", [(0, 1), (1, 0)])

    a, b = call(
        exchange_kernel,
        (shape((NX, 4, 96, BS), BF16), shape((NX, 8, 64, BS), BF16)),
        (pos, spread, other),
        "exchange",
    )
    cut = jnp.broadcast_to(cut[:4, None], (4, 4, BS)).reshape(NZ, 1, BS)
    cut, a, b = lax.optimization_barrier((cut, a, b))
    pair_a, pair_b = [], []
    for g in range(0, NZ, 4):
        pair_a += [(g, g + 1), (g + 1, g), (g + 2, g + 3), (g + 3, g + 2)]
        pair_b += [(g + 1, g + 2), (g + 2, g + 1)]
    a = lax.ppermute(a, "z", pair_a)
    b = lax.ppermute(b, "z", pair_b)
    cut = lax.all_to_all(cut, "z", 0, 0, tiled=True)[:, 0]

    parts, squares = [], []
    for k in range(3):
        code, square = call(
            functools.partial(forward_kernel, k),
            (shape((4 * BS + TAIL, BS), jnp.int16), shape((1, BS), F32)),
            (pos, cut, spread, other, a, b, fwd_tall, fwd_wide),
            "forward",
            [pltpu.VMEM((NX, 4, BS, BS), BF16)],
        )
        parts.append(lax.ppermute(code, ("x", "y"), swap))
        squares.append(square)
    norm = jnp.broadcast_to(sum(squares)[None], (NX * NY * NC, 1, BS))
    norm = lax.all_to_all(norm, ("x", "y", "c"), 0, 0, tiled=True)
    coded = call(slots_kernel, shape((NZ, BS + TAIL, BS), jnp.int16), (pos, *parts, norm), "slots")
    coded = lax.all_to_all(coded, "z", 0, 0, tiled=True)

    tile = pl.BlockSpec((3 * BS, BS), lambda i: (i, 0))
    return pl.pallas_call(
        update_kernel,
        out_shape=(shape(outer_params.shape, F32), shape(outer_params.shape, F32)),
        grid=(4,),
        in_specs=[SMEM, VMEM, SMEM, tile, tile, VMEM, VMEM],
        out_specs=(tile, tile),
        compiler_params=BIG,
        name="update",
    )(pos, coded, clip_level, outer_params, momentum, inv_tall, inv_wide)


def solution(mesh):
    grid = Mesh(mesh.devices.reshape(NX, NY, NZ, NC), ("x", "y", "z", "c"))
    yzc = ("y", "z", "c")
    in_specs = (P("x", yzc, None), P("x", yzc), P("x", yzc), P(), P(None, yzc, None, None), P(None, yzc, None, None))
    out_specs = (P("x", yzc), P("x", yzc))
    return jax.shard_map(per_device, mesh=grid, in_specs=in_specs, out_specs=out_specs, check_vma=False)
```

time: 145 us -> 152 us (1.048)
  the two profiles are of different devices: /device:TPU:1 before, /device:TPU:32 now
where the time goes in v2:
time: 152 us; the launch traced here: 151 us
  blocking collectives  84 us (55%)
  waiting for transfers between devices  31.7 us (21%)
  Pallas kernels  15.7 us (10%)
  starting transfers between devices  15.4 us (10%)
  local copies, waits for them, and re-layouts  2.61 us (2%)
  between operations  1.52 us (1%)
    all_to_all x1, blocking collectives, per_device(): norm = lax.all_to_all(norm, ('x', 'y', 'c'), 0, 0, tiled=True)  33 us
    all_to_all x1, waiting for transfers between devices, per_device(): coded = lax.all_to_all(coded, 'z', 0, 0, tiled=True)  31.3 us
    all_to_all x1, blocking collectives, per_device(): cut = lax.all_to_all(cut, 'z', 0, 0, tiled=True)[:, 0]  26.2 us
    all_to_all x1, blocking collectives, per_device(): spread = lax.all_to_all(packed, 'x', 0, 0, tiled=True)  24.8 us
    pallas_call x5, Pallas kernels, call(): pl.pallas_call(kernel, out_shape=out_shape, in_specs=[SMEM if i.dtype ==...  10.7 us
    all_to_all x1, starting transfers between devices, per_device(): coded = lax.all_to_all(coded, 'z', 0, 0, tiled=True)  4.8 us
    ppermute x1, starting transfers between devices, per_device(): b = lax.ppermute(b, 'z', pair_b)  3.82 us
    pallas_call x1, Pallas kernels, per_device(): pl.pallas_call(update_kernel, out_shape=(shape(outer_params.shape, F32),...  3.79 us
  transfers between devices with their start and end apart: 8, of which 2 were waited for; matrix products, arithmetic and copies ran while one was open for 1% of the time, Pallas kernels for 4%

profile of v2, /device:TPU:32, one launch (start us, length us, event | category | flops | bytes accessed | tf_op | source)
XLA Modules:
  0.0 151.1 jit_solution(11999686857095476181)
XLA Ops:
  0.6 0.1 pad_add_fusion.pos
  0.7 0.0 copy-start
  0.7 1.4 copy-done
  2.1 1.2 pack.1
  3.3 24.8 %all_to_all.20.mine = bf16[4,2,16,48,128]{4,3,2,1,0:T(8,128)(2,1)S(1)} all-to-all(bf16[4,2,16,48,128]{4,3,2,1,0:T(8,128)(2,1)S(1)} %pack.1), channel_id=1, replica_groups=mesh['x'=4,'y'=4,'z'=16,'c'=2] {'x'}, dimensions={0} | all-to-all | bytes 3145728 | tf_op jit(solution)/shard_map/all_to_all | solution.py:254
  28.1 0.1 slice_bitcast_fusion
  28.1 0.0 copy-start.3
  28.2 0.0 copy-start.4
  28.2 2.1 %collective-permute-start.1 = (bf16[4,16,48,128]{3,2,1,0:T(8,128)(2,1)S(1)}, bf16[4,16,48,128]{3,2,1,0:T(8,128)(2,1)S(1)}, u32[]{:S(2)}, u32[]{:S(2)}) collective-permute-start(bf16[4,16,48,128]{3,2,1,0:T(8,128)(2,1)S(1)} %slice_bitcast_fusion), channel_id=1, source_target_pairs={{0,1},{1,0},{2,3},{3,2},{4,5},{5,4},{6,7},{7,6},{8,9},{9,8},{10,11... | collective-permute-start | bytes 2359304 | tf_op jit(solution)/shard_map/ppermute | solution.py:255
  30.2 0.7 constant_dynamic-slice_fusion
  31.0 0.1 copy.24
  31.1 0.1 copy.23
  31.2 0.1 select_reduce_fusion
  31.2 0.1 copy.25
  31.3 0.1 reshape.22
  31.4 0.7 collective-permute-start
  32.1 0.0 collective-permute-done
  32.1 0.4 collective-permute-done.1.other
  32.5 0.7 exchange.1
  33.2 3.8 %collective-permute-start.3 = (bf16[4,8,64,128]{3,2,1,0:T(8,128)(2,1)S(1)}, bf16[4,8,64,128]{3,2,1,0:T(8,128)(2,1)S(1)}, u32[]{:S(2)}, u32[]{:S(2)}) collective-permute-start(bf16[4,8,64,128]{3,2,1,0:T(8,128)(2,1)S(1)} %get-tuple-element.17), channel_id=1, source_target_pairs={{2,4},{4,2},{10,12},{12,10},{18,20},{20,18},{26,28},{28,26},{3,5},... | collective-permute-start | bytes 1572872 | tf_op jit(solution)/shard_map/ppermute | solution.py:270
  37.0 1.9 %collective-permute-start.2 = (bf16[4,4,96,128]{3,2,1,0:T(8,128)(2,1)S(1)}, bf16[4,4,96,128]{3,2,1,0:T(8,128)(2,1)S(1)}, u32[]{:S(2)}, u32[]{:S(2)}) collective-permute-start(bf16[4,4,96,128]{3,2,1,0:T(8,128)(2,1)S(1)} %get-tuple-element.16), channel_id=1, source_target_pairs={{0,2},{2,0},{4,6},{6,4},{8,10},{10,8},{12,14},{14,12},{16,18},{18,... | collective-permute-start | bytes 1179656 | tf_op jit(solution)/shard_map/ppermute | solution.py:269
  38.9 26.2 %all_to_all.21 = s32[16,1,128]{2,1,0:T(1,128)S(1)} all-to-all(s32[16,1,128]{2,1,0:T(1,128)S(1)} %bitcast.16), channel_id=1, replica_groups=mesh['x'=4,'y'=4,'z'=16,'c'=2] {'z'}, dimensions={0} | all-to-all | bytes 16384 | tf_op jit(solution)/shard_map/all_to_all | solution.py:271
  65.2 0.0 collective-permute-done.2.a
  65.2 0.0 collective-permute-done.3.b
  65.2 0.0 copy-done.3
  65.2 0.0 copy-done.4
  65.2 2.9 %forward.3 = (s16[528,128]{1,0:T(8,128)(2,1)S(1)}, f32[1,128]{1,0:T(1,128)S(1)}) custom-call(s32[2]{0:T(128)S(1)} %pad_add_fusion.pos, s32[16,128]{1,0:T(8,128)S(1)} %bitcast.13, bf16[4,2,16,48,128]{4,3,2,1,0:T(8,128)(2,1)S(1)} %all_to_all.20.mine, bf16[4,16,48,128]{3,2,1,0:T(8,128)(2,1)S(1)} %collective-permute-done.1.other, ...), custom_call_target="tpu_custom_call" | custom-call | tf_op jit(solution)/shard_map/forward/pallas_call | solution.py:214
  68.1 0.7 collective-permute-start.4
  68.7 2.9 %forward.4 = (s16[528,128]{1,0:T(8,128)(2,1)S(1)}, f32[1,128]{1,0:T(1,128)S(1)}) custom-call(s32[2]{0:T(128)S(1)} %pad_add_fusion.pos, s32[16,128]{1,0:T(8,128)S(1)} %bitcast.14, bf16[4,2,16,48,128]{4,3,2,1,0:T(8,128)(2,1)S(1)} %all_to_all.20.mine, bf16[4,16,48,128]{3,2,1,0:T(8,128)(2,1)S(1)} %collective-permute-done.1.other, ...), custom_call_target="tpu_custom_call" | custom-call | tf_op jit(solution)/shard_map/forward/pallas_call | solution.py:214
  71.6 0.7 collective-permute-start.5
  72.3 2.9 %forward.5 = (s16[528,128]{1,0:T(8,128)(2,1)S(1)}, f32[1,128]{1,0:T(1,128)S(1)}) custom-call(s32[2]{0:T(128)S(1)} %pad_add_fusion.pos, s32[16,128]{1,0:T(8,128)S(1)} %bitcast.15, bf16[4,2,16,48,128]{4,3,2,1,0:T(8,128)(2,1)S(1)} %all_to_all.20.mine, bf16[4,16,48,128]{3,2,1,0:T(8,128)(2,1)S(1)} %collective-permute-done.1.other, ...), custom_call_target="tpu_custom_call" | custom-call | tf_op jit(solution)/shard_map/forward/pallas_call | solution.py:214
  75.2 0.0 copy-start.1
  75.2 0.0 copy-start.2
  75.2 0.0 copy-start.5
  75.2 0.0 copy-start.6
  75.2 0.8 collective-permute-start.6
  76.1 33.0 %all_to_all.22.norm = f32[32,1,128]{2,1,0:T(1,128)S(1)} all-to-all(f32[32,1,128]{2,1,0:T(1,128)S(1)} %broadcast_in_dim.36), channel_id=1, replica_groups=mesh['x'=4,'y'=4,'z'=16,'c'=2] {'x','y','c'}, dimensions={0} | all-to-all | bytes 32768 | tf_op jit(solution)/shard_map/all_to_all | solution.py:285
  109.1 0.0 collective-permute-done.4.c0
  109.1 0.0 collective-permute-done.5.c1
  109.1 0.0 collective-permute-done.6.c2
  109.1 1.5 slots.1
  110.5 4.8 %all-to-all-start.3 = ((s16[16,144,128]{2,1,0:T(8,128)(2,1)}), s16[16,144,128]{2,1,0:T(8,128)(2,1)S(1)}, u32[]{:S(2)}, u32[]{:S(2)}) async-start(s16[16,144,128]{2,1,0:T(8,128)(2,1)} %slots.1), calls=%async_computation.3 | async-start | bytes 1179648 | tf_op jit(solution)/shard_map/all_to_all | solution.py:287
  116.0 31.3 %all-to-all-done.3.z = s16[16,144,128]{2,1,0:T(8,128)(2,1)S(1)} async-done(((s16[16,144,128]{2,1,0:T(8,128)(2,1)}), s16[16,144,128]{2,1,0:T(8,128)(2,1)S(1)}, u32[]{:S(2)}, u32[]{:S(2)}) %all-to-all-start.3) | async-done | bytes 589856 | tf_op jit(solution)/shard_map/all_to_all | solution.py:287
  147.3 0.0 copy-done.1
  147.3 0.0 copy-done.2
  147.3 0.0 copy-done.5
  147.3 0.0 copy-done.6
  147.3 3.8 %update.1 = (f32[1536,128]{1,0:T(8,128)}, f32[1536,128]{1,0:T(8,128)}) custom-call(s32[2]{0:T(128)S(1)} %pad_add_fusion.pos, s16[16,144,128]{2,1,0:T(8,128)(2,1)S(1)} %all-to-all-done.3.z, f32[1]{0:T(128)S(6)} %copy.28.clip, f32[1536,128]{1,0:T(8,128)S(1)} %copy-done.1, f32[1536,128]{1,0:T(8,128)S(1)} %copy-done.2, bf16[256,128]{1,0:T(8,128)(2,1)S(1)} %copy-done.5, ...), custom_call_target="tpu_custom_call" | custom-call | tf_op jit(solution)/shard_map/update/pallas_call | solution.py:290
  (5 shorter events, 0.0 us)
Async XLA Ops:
  0.7 1.4 copy-start
  28.1 37.0 %copy-start.3 = (bf16[256,128]{1,0:T(8,128)(2,1)S(1)}, bf16[256,128]{1,0:T(8,128)(2,1)}, u32[]{:S(2)}) copy-start(bf16[256,128]{1,0:T(8,128)(2,1)} %constant.49.clone.tall) | copy-start | bytes 196612
  28.2 37.0 %copy-start.4 = (bf16[128,256]{1,0:T(8,128)(2,1)S(1)}, bf16[128,256]{1,0:T(8,128)(2,1)}, u32[]{:S(2)}) copy-start(bf16[128,256]{1,0:T(8,128)(2,1)} %constant.48.clone.wide) | copy-start | bytes 196612
  28.2 4.3 %collective-permute-start.1 = (bf16[4,16,48,128]{3,2,1,0:T(8,128)(2,1)S(1)}, bf16[4,16,48,128]{3,2,1,0:T(8,128)(2,1)S(1)}, u32[]{:S(2)}, u32[]{:S(2)}) collective-permute-start(bf16[4,16,48,128]{3,2,1,0:T(8,128)(2,1)S(1)} %slice_bitcast_fusion), channel_id=1, source_target_pairs={{0,1},{1,0},{2,3},{3,2},{4,5},{5,4},{6,7},{7,6},{8,9},{9,8},{10,11... | collective-permute-start | bytes 2359304 | tf_op jit(solution)/shard_map/ppermute | solution.py:255
  31.4 0.7 collective-permute-start
  33.2 32.0 %collective-permute-start.3 = (bf16[4,8,64,128]{3,2,1,0:T(8,128)(2,1)S(1)}, bf16[4,8,64,128]{3,2,1,0:T(8,128)(2,1)S(1)}, u32[]{:S(2)}, u32[]{:S(2)}) collective-permute-start(bf16[4,8,64,128]{3,2,1,0:T(8,128)(2,1)S(1)} %get-tuple-element.17), channel_id=1, source_target_pairs={{2,4},{4,2},{10,12},{12,10},{18,20},{20,18},{26,28},{28,26},{3,5},... | collective-permute-start | bytes 1572872 | tf_op jit(solution)/shard_map/ppermute | solution.py:270
  37.0 28.2 %collective-permute-start.2 = (bf16[4,4,96,128]{3,2,1,0:T(8,128)(2,1)S(1)}, bf16[4,4,96,128]{3,2,1,0:T(8,128)(2,1)S(1)}, u32[]{:S(2)}, u32[]{:S(2)}) collective-permute-start(bf16[4,4,96,128]{3,2,1,0:T(8,128)(2,1)S(1)} %get-tuple-element.16), channel_id=1, source_target_pairs={{0,2},{2,0},{4,6},{6,4},{8,10},{10,8},{12,14},{14,12},{16,18},{18,... | collective-permute-start | bytes 1179656 | tf_op jit(solution)/shard_map/ppermute | solution.py:269
  68.1 41.0 %collective-permute-start.4 = (s16[528,128]{1,0:T(8,128)(2,1)S(1)}, s16[528,128]{1,0:T(8,128)(2,1)S(1)}, u32[]{:S(2)}, u32[]{:S(2)}) collective-permute-start(s16[528,128]{1,0:T(8,128)(2,1)S(1)} %get-tuple-element.18), channel_id=1, source_target_pairs={{0,0},{32,128},{64,256},{96,384},{128,32},{160,160},{192,288},{224... | collective-permute-start | bytes 405512 | tf_op jit(solution)/shard_map/ppermute | solution.py:282
  71.6 37.4 %collective-permute-start.5 = (s16[528,128]{1,0:T(8,128)(2,1)S(1)}, s16[528,128]{1,0:T(8,128)(2,1)S(1)}, u32[]{:S(2)}, u32[]{:S(2)}) collective-permute-start(s16[528,128]{1,0:T(8,128)(2,1)S(1)} %get-tuple-element.19), channel_id=1, source_target_pairs={{0,0},{32,128},{64,256},{96,384},{128,32},{160,160},{192,288},{224... | collective-permute-start | bytes 405512 | tf_op jit(solution)/shard_map/ppermute | solution.py:282
  75.2 72.1 %copy-start.1 = (f32[1536,128]{1,0:T(8,128)S(1)}, f32[1536,128]{1,0:T(8,128)}, u32[]{:S(2)}) copy-start(f32[1536,128]{1,0:T(8,128)} %params.1) | copy-start | bytes 2359300
  75.2 72.1 %copy-start.2 = (f32[1536,128]{1,0:T(8,128)S(1)}, f32[1536,128]{1,0:T(8,128)}, u32[]{:S(2)}) copy-start(f32[1536,128]{1,0:T(8,128)} %mom.1) | copy-start | bytes 2359300
  75.2 72.1 %copy-start.5 = (bf16[256,128]{1,0:T(8,128)(2,1)S(1)}, bf16[256,128]{1,0:T(8,128)(2,1)}, u32[]{:S(2)}) copy-start(bf16[256,128]{1,0:T(8,128)(2,1)} %constant.51.clone.tall) | copy-start | bytes 196612
  75.2 72.1 %copy-start.6 = (bf16[128,256]{1,0:T(8,128)(2,1)S(1)}, bf16[128,256]{1,0:T(8,128)(2,1)}, u32[]{:S(2)}) copy-start(bf16[128,256]{1,0:T(8,128)(2,1)} %constant.50.clone.wide) | copy-start | bytes 196612
  75.2 33.8 %collective-permute-start.6 = (s16[528,128]{1,0:T(8,128)(2,1)S(1)}, s16[528,128]{1,0:T(8,128)(2,1)S(1)}, u32[]{:S(2)}, u32[]{:S(2)}) collective-permute-start(s16[528,128]{1,0:T(8,128)(2,1)S(1)} %get-tuple-element.20), channel_id=1, source_target_pairs={{0,0},{32,128},{64,256},{96,384},{128,32},{160,160},{192,288},{224... | collective-permute-start | bytes 405512 | tf_op jit(solution)/shard_map/ppermute | solution.py:282
  110.5 36.7 %all-to-all-start.3 = ((s16[16,144,128]{2,1,0:T(8,128)(2,1)}), s16[16,144,128]{2,1,0:T(8,128)(2,1)S(1)}, u32[]{:S(2)}, u32[]{:S(2)}) async-start(s16[16,144,128]{2,1,0:T(8,128)(2,1)} %slots.1), calls=%async_computation.3 | async-start | bytes 1179648 | tf_op jit(solution)/shard_map/all_to_all | solution.py:287

commit v3 on v2

--- a/solution.py
+++ b/solution.py
@@ -99,8 +99,8 @@
     by_place(pos, mine, other, body)
 
 
-def assemble(k, pos, mine, other, a, b, x):
-    def body(p, lo, hi):
+def assemble(pos, mine, other, a, b, whole):
+    def place(p, k, lo, hi, x):
         m = k + (k >= p)
         s = slice(4 * m, 4 * m + 4)
         third = slice(32 * k, 32 * k + 32)
@@ -127,6 +127,10 @@
             x[:, :, 64:112] = lo[:, s]
             x[:, :, 112:128] = hi[:, s, 0:16]
 
+    def body(p, lo, hi):
+        for k in range(3):
+            place(p, k, lo, hi, whole.at[:, 4 * k : 4 * k + 4])
+
     by_place(pos, mine, other, body)
 
 
@@ -134,71 +138,76 @@
     return jnp.clip(jnp.floor(jnp.log2(jnp.maximum(size, F32(1e-30)))) + 1.0, -100.0, 200.0)
 
 
-def forward_kernel(k, pos, cut, mine, other, a, b, tall, wide, out, square, x):
-    assemble(k, pos, mine, other, a, b, x)
-    p = pos[0]
-    m = k + (k >= p).astype(jnp.int32)
-    blk = p - (p > m).astype(jnp.int32)
+def forward_kernel(pos, cut, mine, other, a, b, tall, wide, out, x, exps):
+    assemble(pos, mine, other, a, b, x)
+    p, grp = pos[0], pos[2]
     freq = lax.broadcasted_iota(jnp.int32, (BS, BS), 0) + lax.broadcasted_iota(jnp.int32, (BS, BS), 1)
     row = lax.broadcasted_iota(jnp.int32, (TAIL, BS), 0)
-    tail = jnp.zeros((TAIL, BS), F32)
-    squares = jnp.zeros((1, BS), F32)
+    exps[...] = jnp.zeros_like(exps)
     for w in range(4):
-        total = jnp.zeros((BS, BS), F32)
-        for r in range(NX):
-            both = dot(x[r, w], wide[...])
-            hi, lo = split(both[:, :BS] + both[:, BS:])
-            four = dot(tall[...], jnp.concatenate([hi, lo], axis=1))
-            coef = four[:BS, :BS] + (four[BS:, :BS] + four[:BS, BS:])
-            total += jnp.where(freq <= cut[4 * w + m, 4 * blk + r], coef, 0.0)
-        e = exponent(jnp.max(jnp.abs(total), axis=0, keepdims=True))
-        code = jnp.clip(jnp.floor(total * jnp.exp2(15.0 - e) + 0.5), -32767.0, 32767.0)
-        out[BS * w : BS * w + BS] = code.astype(jnp.int32).astype(jnp.int16)
-        tail = jnp.where(row == w, e, tail)
-        squares += jnp.sum(total * total, axis=0, keepdims=True)
-    out[4 * BS : 4 * BS + TAIL] = tail.astype(jnp.int32).astype(jnp.int16)
-    square[...] = squares
-
-
-def slots_kernel(pos, c0, c1, c2, norm, out):
-    p = pos[0]
-    square = jnp.sum(norm[...], axis=0)
+        out[4 * w + p, 0:BS] = jnp.zeros((BS, BS), jnp.int16)
+
+    def step(w, square):
+        for k in range(3):
+            m = k + (k >= p).astype(jnp.int32)
+            blk = p - (p > m).astype(jnp.int32)
+            src = 4 * ((grp + 4 - w) % 4) + (p + 4 - m) % 4
+            total = jnp.zeros((BS, BS), F32)
+            for r in range(NX):
+                both = dot(x[r, 4 * k + w], wide[...])
+                hi, lo = split(both[:, :BS] + both[:, BS:])
+                four = dot(tall[...], jnp.concatenate([hi, lo], axis=1))
+                coef = four[:BS, :BS] + (four[BS:, :BS] + four[:BS, BS:])
+                total += jnp.where(freq <= cut[src, 4 * blk + r], coef, 0.0)
+            e = exponent(jnp.max(jnp.abs(total), axis=0, keepdims=True))
+            code = jnp.clip(jnp.floor(total * jnp.exp2(15.0 - e) + 0.5), -32767.0, 32767.0)
+            out[4 * w + m, 0:BS] = code.astype(jnp.int32).astype(jnp.int16)
+            exps[pl.ds(4 * w + m, 1), :] = e
+            square += jnp.sum(total * total, axis=0, keepdims=True)
+        return square
+
+    square = lax.fori_loop(0, 4, step, jnp.zeros((1, BS), F32))
     e = exponent(square)
     scaled = jnp.minimum(square, F32(3e38)) * jnp.exp2(-0.5 * e) * jnp.exp2(-0.5 * e) * 16384.0
     d1 = jnp.floor(scaled)
     d2 = jnp.floor((scaled - d1) * 16384.0)
     e = jnp.where(square > F32(3e38), 200.0, e)
+    tail = jnp.where(row == 1, e, jnp.where(row == 2, d1, jnp.where(row == 3, d2, 0.0)))
+    for s in range(NZ):
+        mix = jnp.where(row == 0, exps[s : s + 1, :], tail)
+        out[s, BS : BS + TAIL] = mix.astype(jnp.int32).astype(jnp.int16)
+
+
+def compact_kernel(pos, z, out, norm):
+    p = pos[0]
     row = lax.broadcasted_iota(jnp.int32, (TAIL, BS), 0)
-    tail = jnp.where(row == 1, e, jnp.where(row == 2, d1, jnp.where(row == 3, d2, 0.0)))
-    for k in range(3):
-        code = (c0, c1, c2)[k]
-        m = k + (k >= p).astype(jnp.int32)
-        exps = code[4 * BS : 4 * BS + TAIL].astype(jnp.int32).astype(F32)
-        for w in range(4):
-            out[4 * w + m, 0:BS] = code[BS * w : BS * w + BS]
-            mix = jnp.where(row == 0, exps[w : w + 1], tail)
-            out[4 * w + m, BS : BS + TAIL] = mix.astype(jnp.int32).astype(jnp.int16)
-    tail = tail.astype(jnp.int32).astype(jnp.int16)
-    for w in range(4):
-        out[4 * w + p, 0:BS] = jnp.zeros((BS, BS), jnp.int16)
-        out[4 * w + p, BS : BS + TAIL] = tail
-
-
-def update_kernel(pos, z, clip, params, mom, tall, wide, new_p, new_m):
-    g = pl.program_id(0)
-    p = pos[0]
+    tail = jnp.zeros((TAIL, BS), F32)
+    for g in range(4):
+        for blk in range(3):
+            src = 4 * g + blk + (p <= blk).astype(jnp.int32)
+            n = 3 * g + blk
+            out[BS * n : BS * n + BS] = z[src, 0:BS]
+            e = z[src, BS : BS + TAIL].astype(jnp.int32).astype(F32)[0:1]
+            tail = jnp.where(row == n, e, tail)
+    out[BS * BPO : BS * BPO + TAIL] = tail.astype(jnp.int32).astype(jnp.int16)
     total = jnp.zeros((1, BS), F32)
     for s in range(NZ):
         t = z[s, BS : BS + TAIL].astype(jnp.int32).astype(F32)
         part = t[2:3] * F32(1.0 / 16384.0) + t[3:4] * F32(1.0 / 16384.0**2)
         total += part * jnp.exp2(0.5 * t[1:2]) * jnp.exp2(0.5 * t[1:2])
-    total = jnp.sum(total, axis=1, keepdims=True)
+    norm[...] = jnp.broadcast_to(total[None], norm.shape)
+
+
+def update_kernel(code, tail, norm, clip, params, mom, tall, wide, new_p, new_m):
+    i = pl.program_id(0)
+    total = jnp.sum(jnp.sum(norm[...], axis=0), axis=1, keepdims=True)
     factor = jnp.minimum(F32(1.0), clip[0] * F32(math.sqrt(D * FF)) / (jnp.sqrt(total) + F32(EPSILON)))
+    row = lax.broadcasted_iota(jnp.int32, (TAIL, BS), 0)
+    exps = tail[...].astype(jnp.int32).astype(F32)
     for n in range(3):
-        src = 4 * g + n + (p <= n).astype(jnp.int32)
-        e = z[src, BS : BS + TAIL].astype(jnp.int32).astype(F32)[0:1]
+        e = jnp.sum(jnp.where(row == 3 * i + n, exps, 0.0), axis=0, keepdims=True)
         d = slice(BS * n, BS * n + BS)
-        coef = z[src, 0:BS].astype(jnp.int32).astype(F32) * (jnp.exp2(e - 15.0) * factor)
+        coef = code[d].astype(jnp.int32).astype(F32) * (jnp.exp2(e - 15.0) * factor)
         upd = tall_times(tall[...], times_wide(coef, wide[...]))
         nm = NESTEROV * mom[d] + upd
         new_m[d] = nm
@@ -224,7 +233,7 @@
 
 def per_device(pseudo_grads, outer_params, momentum, clip_level, block_picks, cutoffs):
     z = lax.axis_index("z")
-    pos = jnp.stack([z % 4, lax.axis_index("c")]).astype(jnp.int32)
+    pos = jnp.stack([z % 4, lax.axis_index("c"), z // 4]).astype(jnp.int32)
     hi, lo = table_parts()
     fwd_wide = jnp.asarray(np.concatenate([hi.T, lo.T], axis=1))
     fwd_tall = jnp.asarray(np.concatenate([hi, lo], axis=0))
@@ -240,7 +249,25 @@
     hit = picks[:, :, None] == jnp.arange(BPO, dtype=jnp.int32)
     cut = jnp.max(jnp.where(hit, cuts[:, :, None], -1), axis=1)
     cut = jnp.pad(cut.T.reshape(4, BPO), ((0, 4), (0, BS - BPO)))
-    cut = lax.ppermute(cut, ("x", "y"), swap)
+    cut, pseudo_grads = lax.optimization_barrier((cut, pseudo_grads))
+    near = []
+    for n in range(4):
+        near.append(
+            lax.ppermute(
+                cut,
+                ("x", "y", "z"),
+                [
+                    ((NY * i + j) * NZ + 4 * g + q, (NX * j + i) * NZ + 4 * g + (q + n) % 4)
+                    for i in range(NX)
+                    for j in range(NY)
+                    for g in range(4)
+                    for q in range(4)
+                ],
+            )
+        )
+    near = jnp.stack(near)
+    far = [near] + [lax.ppermute(near, "z", [(i, (i + 4 * n) % NZ) for i in range(NZ)]) for n in range(1, 4)]
+    cut = lax.dynamic_index_in_dim(jnp.concatenate(far), z // 4, 1, keepdims=False)
 
     packed = pl.pallas_call(
         pack_kernel,
@@ -252,6 +279,7 @@
         name="pack",
     )(pos, pseudo_grads)
     spread = lax.all_to_all(packed, "x", 0, 0, tiled=True)
+    spread, cut = lax.optimization_barrier((spread, cut))
     other = lax.ppermute(spread[:, 1], "c", [(0, 1), (1, 0)])
 
     a, b = call(
@@ -260,42 +288,49 @@
         (pos, spread, other),
         "exchange",
     )
-    cut = jnp.broadcast_to(cut[:4, None], (4, 4, BS)).reshape(NZ, 1, BS)
-    cut, a, b = lax.optimization_barrier((cut, a, b))
     pair_a, pair_b = [], []
     for g in range(0, NZ, 4):
         pair_a += [(g, g + 1), (g + 1, g), (g + 2, g + 3), (g + 3, g + 2)]
         pair_b += [(g + 1, g + 2), (g + 2, g + 1)]
     a = lax.ppermute(a, "z", pair_a)
     b = lax.ppermute(b, "z", pair_b)
-    cut = lax.all_to_all(cut, "z", 0, 0, tiled=True)[:, 0]
-
-    parts, squares = [], []
-    for k in range(3):
-        code, square = call(
-            functools.partial(forward_kernel, k),
-            (shape((4 * BS + TAIL, BS), jnp.int16), shape((1, BS), F32)),
-            (pos, cut, spread, other, a, b, fwd_tall, fwd_wide),
-            "forward",
-            [pltpu.VMEM((NX, 4, BS, BS), BF16)],
-        )
-        parts.append(lax.ppermute(code, ("x", "y"), swap))
-        squares.append(square)
-    norm = jnp.broadcast_to(sum(squares)[None], (NX * NY * NC, 1, BS))
+
+    coded = call(
+        forward_kernel,
+        shape((NZ, BS + TAIL, BS), jnp.int16),
+        (pos, cut, spread, other, a, b, fwd_tall, fwd_wide),
+        "forward",
+        [pltpu.VMEM((NX, BPO, BS, BS), BF16), pltpu.VMEM((NZ, BS), F32)],
+    )
+    coded = lax.all_to_all(coded, "z", 0, 0, tiled=True)
+    coded, norm = call(
+        compact_kernel,
+        (shape((BPO * BS + TAIL, BS), jnp.int16), shape((NX * NY * NC, 1, BS), F32)),
+        (pos, coded),
+        "compact",
+    )
+    coded = lax.ppermute(coded, ("x", "y"), swap)
     norm = lax.all_to_all(norm, ("x", "y", "c"), 0, 0, tiled=True)
-    coded = call(slots_kernel, shape((NZ, BS + TAIL, BS), jnp.int16), (pos, *parts, norm), "slots")
-    coded = lax.all_to_all(coded, "z", 0, 0, tiled=True)
 
     tile = pl.BlockSpec((3 * BS, BS), lambda i: (i, 0))
     return pl.pallas_call(
         update_kernel,
         out_shape=(shape(outer_params.shape, F32), shape(outer_params.shape, F32)),
         grid=(4,),
-        in_specs=[SMEM, VMEM, SMEM, tile, tile, VMEM, VMEM],
+        in_specs=[
+            tile,
+            pl.BlockSpec((TAIL, BS), lambda i: (BPO * BS // TAIL, 0)),
+            VMEM,
+            SMEM,
+            tile,
+            tile,
+            VMEM,
+            VMEM,
+        ],
         out_specs=(tile, tile),
         compiler_params=BIG,
         name="update",
-    )(pos, coded, clip_level, outer_params, momentum, inv_tall, inv_wide)
+    )(coded, coded, norm, clip_level, outer_params, momentum, inv_tall, inv_wide)
 
 
 def solution(mesh):

time: 152 us -> 158 us (1.039)
  the two profiles are of different devices: /device:TPU:32 before, /device:TPU:1 now
where the time goes in v3:
time: 158 us; the launch traced here: 156 us
  starting transfers between devices  76.2 us (48%)
  blocking collectives  36.9 us (23%)
  waiting for transfers between devices  24 us (15%)
  Pallas kernels  15 us (9%)
  local copies, waits for them, and re-layouts  2.63 us (2%)
  between operations  1.61 us (1%)
    all_to_all x1, blocking collectives, per_device(): coded = lax.all_to_all(coded, 'z', 0, 0, tiled=True)  36.9 us
    ppermute x3, starting transfers between devices, per_device(): lax.ppermute(near, 'z', [(i, (i + 4 * n) % NZ) for i in range(NZ)])  22.8 us
    all_to_all x1, starting transfers between devices, per_device(): spread = lax.all_to_all(packed, 'x', 0, 0, tiled=True)  15.2 us
    all_to_all x1, starting transfers between devices, per_device(): norm = lax.all_to_all(norm, ('x', 'y', 'c'), 0, 0, tiled=True)  13.8 us
    ppermute x4, starting transfers between devices, per_device(): lax.ppermute(cut, ('x', 'y', 'z'), [((NY * i + j) * NZ + 4 * g + q, (NX *...  12.6 us
    all_to_all x1, waiting for transfers between devices, per_device(): norm = lax.all_to_all(norm, ('x', 'y', 'c'), 0, 0, tiled=True)  10.1 us
    pallas_call x3, Pallas kernels, call(): pl.pallas_call(kernel, out_shape=out_shape, in_specs=[SMEM if i.dtype ==...  9.24 us
    ppermute x1, waiting for transfers between devices, per_device(): a = lax.ppermute(a, 'z', pair_a)  8.85 us
  transfers between devices with their start and end apart: 13, of which 4 were waited for; matrix products, arithmetic and copies ran while one was open for 0% of the time, Pallas kernels for 2%

profile of v3, /device:TPU:1, one launch (start us, length us, event | category | flops | bytes accessed | tf_op | source)
XLA Modules:
  0.0 156.4 jit_solution(17341273385334171848)
XLA Ops:
  0.6 0.7 constant_dynamic-slice_fusion.1
  1.4 0.1 copy.19
  1.5 0.1 copy.20
  1.5 0.1 select_reduce_fusion
  1.6 0.1 copy.21
  1.7 0.1 reshape.15
  1.8 0.7 collective-permute-start
  2.5 4.4 %collective-permute-start.1 = (s32[8,128]{1,0:T(8,128)S(1)}, s32[8,128]{1,0:T(8,128)S(1)}, u32[]{:S(2)}, u32[]{:S(2)}) collective-permute-start(s32[8,128]{1,0:T(8,128)S(1)} %pad.4), channel_id=1, source_target_pairs={{0,2},{2,4},{4,6},{6,0},{8,10},{10,12},{12,14},{14,8},{16,18},{18,... | collective-permute-start | bytes 12296 | tf_op jit(solution)/shard_map/ppermute | solution.py:256
  6.9 4.9 %collective-permute-start.2 = (s32[8,128]{1,0:T(8,128)S(1)}, s32[8,128]{1,0:T(8,128)S(1)}, u32[]{:S(2)}, u32[]{:S(2)}) collective-permute-start(s32[8,128]{1,0:T(8,128)S(1)} %pad.4), channel_id=1, source_target_pairs={{0,4},{2,6},{4,0},{6,2},{8,12},{10,14},{12,8},{14,10},{16,20},{18,... | collective-permute-start | bytes 12296 | tf_op jit(solution)/shard_map/ppermute | solution.py:256
  11.8 2.6 %collective-permute-start.3 = (s32[8,128]{1,0:T(8,128)S(1)}, s32[8,128]{1,0:T(8,128)S(1)}, u32[]{:S(2)}, u32[]{:S(2)}) collective-permute-start(s32[8,128]{1,0:T(8,128)S(1)} %pad.4), channel_id=1, source_target_pairs={{0,6},{2,0},{4,2},{6,4},{8,14},{10,8},{12,10},{14,12},{16,22},{18,... | collective-permute-start | bytes 12296 | tf_op jit(solution)/shard_map/ppermute | solution.py:256
  14.4 0.1 pad_add_fusion.1.pos
  14.5 0.0 copy-start
  14.5 1.4 copy-done
  15.9 2.5 %pack.1 = bf16[4,2,16,48,128]{4,3,2,1,0:T(8,128)(2,1)} custom-call(s32[3]{0:T(128)S(1)} %pad_add_fusion.1.pos, bf16[1,48,16384]{2,1,0:T(8,128)(2,1)S(1)} %copy-done), custom_call_target="tpu_custom_call" | custom-call | tf_op jit(solution)/shard_map/pack/pallas_call | solution.py:272
  18.4 15.2 %all-to-all-start = ((bf16[4,2,16,48,128]{4,3,2,1,0:T(8,128)(2,1)}), bf16[4,2,16,48,128]{4,3,2,1,0:T(8,128)(2,1)S(1)}, u32[]{:S(2)}, u32[]{:S(2)}) async-start(bf16[4,2,16,48,128]{4,3,2,1,0:T(8,128)(2,1)} %pack.1), calls=%async_computation | async-start | bytes 3145728 | tf_op jit(solution)/shard_map/all_to_all | solution.py:281
  33.6 0.0 collective-permute-done
  33.6 0.0 collective-permute-done.1
  33.6 0.0 collective-permute-done.2
  33.6 0.0 collective-permute-done.3
  33.6 8.8 %collective-permute-start.4 = (s32[4,8,128]{2,1,0:T(8,128)S(1)}, s32[4,8,128]{2,1,0:T(8,128)S(1)}, u32[]{:S(2)}, u32[]{:S(2)}) collective-permute-start(s32[4,8,128]{2,1,0:T(8,128)S(1)} %pad_add_fusion), channel_id=1, source_target_pairs={{0,8},{2,10},{4,12},{6,14},{8,16},{10,18},{12,20},{14,22},{16,24},... | collective-permute-start | bytes 49160 | tf_op jit(solution)/shard_map/ppermute | solution.py:269
  42.4 8.8 %collective-permute-start.5 = (s32[4,8,128]{2,1,0:T(8,128)S(1)}, s32[4,8,128]{2,1,0:T(8,128)S(1)}, u32[]{:S(2)}, u32[]{:S(2)}) collective-permute-start(s32[4,8,128]{2,1,0:T(8,128)S(1)} %pad_add_fusion), channel_id=1, source_target_pairs={{0,16},{2,18},{4,20},{6,22},{8,24},{10,26},{12,28},{14,30},{16,0},... | collective-permute-start | bytes 49160 | tf_op jit(solution)/shard_map/ppermute | solution.py:269
  51.3 5.2 %collective-permute-start.6 = (s32[4,8,128]{2,1,0:T(8,128)S(1)}, s32[4,8,128]{2,1,0:T(8,128)S(1)}, u32[]{:S(2)}, u32[]{:S(2)}) collective-permute-start(s32[4,8,128]{2,1,0:T(8,128)S(1)} %pad_add_fusion), channel_id=1, source_target_pairs={{0,24},{2,26},{4,28},{6,30},{8,0},{10,2},{12,4},{14,6},{16,8},{18,... | collective-permute-start | bytes 49160 | tf_op jit(solution)/shard_map/ppermute | solution.py:269
  56.5 0.0 collective-permute-done.4
  56.5 0.0 collective-permute-done.5
  56.6 3.1 %collective-permute-done.6 = s32[4,8,128]{2,1,0:T(8,128)S(1)} collective-permute-done((s32[4,8,128]{2,1,0:T(8,128)S(1)}, s32[4,8,128]{2,1,0:T(8,128)S(1)}, u32[]{:S(2)}, u32[]{:S(2)}) %collective-permute-start.6) | collective-permute-done | bytes 16416 | tf_op jit(solution)/shard_map/ppermute | solution.py:269
  59.7 0.0 all-to-all-done.mine
  59.7 0.1 slice_bitcast_fusion
  59.8 0.0 copy-start.3
  59.8 0.0 copy-start.4
  59.8 5.8 %collective-permute-start.7 = (bf16[4,16,48,128]{3,2,1,0:T(8,128)(2,1)S(1)}, bf16[4,16,48,128]{3,2,1,0:T(8,128)(2,1)S(1)}, u32[]{:S(2)}, u32[]{:S(2)}) collective-permute-start(bf16[4,16,48,128]{3,2,1,0:T(8,128)(2,1)S(1)} %slice_bitcast_fusion), channel_id=1, source_target_pairs={{0,1},{1,0},{2,3},{3,2},{4,5},{5,4},{6,7},{7,6},{8,9},{9,8},{10,11... | collective-permute-start | bytes 2359304 | tf_op jit(solution)/shard_map/ppermute | solution.py:283
  65.6 1.9 %collective-permute-done.7.other = bf16[4,16,48,128]{3,2,1,0:T(8,128)(2,1)S(1)} collective-permute-done((bf16[4,16,48,128]{3,2,1,0:T(8,128)(2,1)S(1)}, bf16[4,16,48,128]{3,2,1,0:T(8,128)(2,1)S(1)}, u32[]{:S(2)}, u32[]{:S(2)}) %collective-permute-start.7) | collective-permute-done | bytes 786464 | tf_op jit(solution)/shard_map/ppermute | solution.py:283
  67.5 0.6 exchange.1
  68.2 0.7 collective-permute-start.9
  68.9 4.6 %collective-permute-start.8 = (bf16[4,4,96,128]{3,2,1,0:T(8,128)(2,1)S(1)}, bf16[4,4,96,128]{3,2,1,0:T(8,128)(2,1)S(1)}, u32[]{:S(2)}, u32[]{:S(2)}) collective-permute-start(bf16[4,4,96,128]{3,2,1,0:T(8,128)(2,1)S(1)} %get-tuple-element.14), channel_id=1, source_target_pairs={{0,2},{2,0},{4,6},{6,4},{8,10},{10,8},{12,14},{14,12},{16,18},{18,... | collective-permute-start | bytes 1179656 | tf_op jit(solution)/shard_map/ppermute | solution.py:295
  73.5 8.9 %collective-permute-done.8.a = bf16[4,4,96,128]{3,2,1,0:T(8,128)(2,1)S(1)} collective-permute-done((bf16[4,4,96,128]{3,2,1,0:T(8,128)(2,1)S(1)}, bf16[4,4,96,128]{3,2,1,0:T(8,128)(2,1)S(1)}, u32[]{:S(2)}, u32[]{:S(2)}) %collective-permute-start.8) | collective-permute-done | bytes 393248 | tf_op jit(solution)/shard_map/ppermute | solution.py:295
  82.3 0.0 collective-permute-done.9.b
  82.3 0.0 copy-done.3
  82.3 0.0 copy-done.4
  82.3 7.4 %forward.1 = s16[16,144,128]{2,1,0:T(8,128)(2,1)S(1)} custom-call(s32[3]{0:T(128)S(1)} %pad_add_fusion.1.pos, s32[16,128]{1,0:T(8,128)S(1)} %bitcast.17, bf16[4,2,16,48,128]{4,3,2,1,0:T(8,128)(2,1)S(1)} %all-to-all-done.mine, bf16[4,16,48,128]{3,2,1,0:T(8,128)(2,1)S(1)} %collective-permute-done.7.other, ...), custom_call_target="tpu_custom_call" | custom-call | tf_op jit(solution)/shard_map/forward/pallas_call | solution.py:223
  89.8 0.0 copy-start.1
  89.8 0.0 copy-start.2
  89.8 0.0 copy-start.5
  89.8 0.0 copy-start.6
  89.8 36.9 %all_to_all.15.z = s16[16,144,128]{2,1,0:T(8,128)(2,1)S(1)} all-to-all(s16[16,144,128]{2,1,0:T(8,128)(2,1)S(1)} %forward.1), channel_id=1, replica_groups=mesh['x'=4,'y'=4,'z'=16,'c'=2] {'z'}, dimensions={0} | all-to-all | bytes 1179648 | tf_op jit(solution)/shard_map/all_to_all | solution.py:305
  126.8 1.2 compact.1
  127.9 0.7 collective-permute-start.10
  128.6 13.8 %all-to-all-start.2 = ((f32[32,1,128]{2,1,0:T(1,128)}), f32[32,1,128]{2,1,0:T(1,128)S(1)}, u32[]{:S(2)}, u32[]{:S(2)}) async-start(f32[32,1,128]{2,1,0:T(1,128)} %get-tuple-element.17), calls=%async_computation.2 | async-start | bytes 32768 | tf_op jit(solution)/shard_map/all_to_all | solution.py:313
  143.1 10.1 %all-to-all-done.2.norm = f32[32,1,128]{2,1,0:T(1,128)S(1)} async-done(((f32[32,1,128]{2,1,0:T(1,128)}), f32[32,1,128]{2,1,0:T(1,128)S(1)}, u32[]{:S(2)}, u32[]{:S(2)}) %all-to-all-start.2) | async-done | bytes 16416 | tf_op jit(solution)/shard_map/all_to_all | solution.py:313
  153.2 0.0 collective-permute-done.10.code.tail
  153.2 0.0 copy-done.1
  153.2 0.0 copy-done.2
  153.2 0.0 copy-done.5
  153.2 0.0 copy-done.6
  153.2 3.2 %update.1 = (f32[1536,128]{1,0:T(8,128)}, f32[1536,128]{1,0:T(8,128)}) custom-call(s16[1552,128]{1,0:T(8,128)(2,1)S(1)} %collective-permute-done.10.code.tail, s16[1552,128]{1,0:T(8,128)(2,1)S(1)} %collective-permute-done.10.code.tail, f32[32,1,128]{2,1,0:T(1,128)S(1)} %all-to-all-done.2.norm, f32[1]{0:T(128)S(6)} %copy.31.clip, f32[1536,128]{1,0:T(8,128)S(1)} %copy-done.1, ...), custom_call_target="tpu_custom_call" | custom-call | tf_op jit(solution)/shard_map/update/pallas_call | solution.py:316
  (10 shorter events, 0.0 us)
Async XLA Ops:
  1.8 31.8 %collective-permute-start = (s32[8,128]{1,0:T(8,128)S(1)}, s32[8,128]{1,0:T(8,128)S(1)}, u32[]{:S(2)}, u32[]{:S(2)}) collective-permute-start(s32[8,128]{1,0:T(8,128)S(1)} %pad.4), channel_id=1, source_target_pairs={{0,0},{2,2},{4,4},{6,6},{8,8},{10,10},{12,12},{14,14},{16,16},{18,... | collective-permute-start | bytes 12296 | tf_op jit(solution)/shard_map/ppermute | solution.py:256
  2.5 31.1 %collective-permute-start.1 = (s32[8,128]{1,0:T(8,128)S(1)}, s32[8,128]{1,0:T(8,128)S(1)}, u32[]{:S(2)}, u32[]{:S(2)}) collective-permute-start(s32[8,128]{1,0:T(8,128)S(1)} %pad.4), channel_id=1, source_target_pairs={{0,2},{2,4},{4,6},{6,0},{8,10},{10,12},{12,14},{14,8},{16,18},{18,... | collective-permute-start | bytes 12296 | tf_op jit(solution)/shard_map/ppermute | solution.py:256
  6.9 26.7 %collective-permute-start.2 = (s32[8,128]{1,0:T(8,128)S(1)}, s32[8,128]{1,0:T(8,128)S(1)}, u32[]{:S(2)}, u32[]{:S(2)}) collective-permute-start(s32[8,128]{1,0:T(8,128)S(1)} %pad.4), channel_id=1, source_target_pairs={{0,4},{2,6},{4,0},{6,2},{8,12},{10,14},{12,8},{14,10},{16,20},{18,... | collective-permute-start | bytes 12296 | tf_op jit(solution)/shard_map/ppermute | solution.py:256
  11.8 21.8 %collective-permute-start.3 = (s32[8,128]{1,0:T(8,128)S(1)}, s32[8,128]{1,0:T(8,128)S(1)}, u32[]{:S(2)}, u32[]{:S(2)}) collective-permute-start(s32[8,128]{1,0:T(8,128)S(1)} %pad.4), channel_id=1, source_target_pairs={{0,6},{2,0},{4,2},{6,4},{8,14},{10,8},{12,10},{14,12},{16,22},{18,... | collective-permute-start | bytes 12296 | tf_op jit(solution)/shard_map/ppermute | solution.py:256
  14.5 1.4 copy-start
  18.4 41.3 %all-to-all-start = ((bf16[4,2,16,48,128]{4,3,2,1,0:T(8,128)(2,1)}), bf16[4,2,16,48,128]{4,3,2,1,0:T(8,128)(2,1)S(1)}, u32[]{:S(2)}, u32[]{:S(2)}) async-start(bf16[4,2,16,48,128]{4,3,2,1,0:T(8,128)(2,1)} %pack.1), calls=%async_computation | async-start | bytes 3145728 | tf_op jit(solution)/shard_map/all_to_all | solution.py:281
  33.6 22.9 %collective-permute-start.4 = (s32[4,8,128]{2,1,0:T(8,128)S(1)}, s32[4,8,128]{2,1,0:T(8,128)S(1)}, u32[]{:S(2)}, u32[]{:S(2)}) collective-permute-start(s32[4,8,128]{2,1,0:T(8,128)S(1)} %pad_add_fusion), channel_id=1, source_target_pairs={{0,8},{2,10},{4,12},{6,14},{8,16},{10,18},{12,20},{14,22},{16,24},... | collective-permute-start | bytes 49160 | tf_op jit(solution)/shard_map/ppermute | solution.py:269
  42.4 14.1 %collective-permute-start.5 = (s32[4,8,128]{2,1,0:T(8,128)S(1)}, s32[4,8,128]{2,1,0:T(8,128)S(1)}, u32[]{:S(2)}, u32[]{:S(2)}) collective-permute-start(s32[4,8,128]{2,1,0:T(8,128)S(1)} %pad_add_fusion), channel_id=1, source_target_pairs={{0,16},{2,18},{4,20},{6,22},{8,24},{10,26},{12,28},{14,30},{16,0},... | collective-permute-start | bytes 49160 | tf_op jit(solution)/shard_map/ppermute | solution.py:269
  51.3 8.4 %collective-permute-start.6 = (s32[4,8,128]{2,1,0:T(8,128)S(1)}, s32[4,8,128]{2,1,0:T(8,128)S(1)}, u32[]{:S(2)}, u32[]{:S(2)}) collective-permute-start(s32[4,8,128]{2,1,0:T(8,128)S(1)} %pad_add_fusion), channel_id=1, source_target_pairs={{0,24},{2,26},{4,28},{6,30},{8,0},{10,2},{12,4},{14,6},{16,8},{18,... | collective-permute-start | bytes 49160 | tf_op jit(solution)/shard_map/ppermute | solution.py:269
  59.8 22.6 %copy-start.3 = (bf16[128,256]{1,0:T(8,128)(2,1)S(1)}, bf16[128,256]{1,0:T(8,128)(2,1)}, u32[]{:S(2)}) copy-start(bf16[128,256]{1,0:T(8,128)(2,1)} %constant.67.clone.wide) | copy-start | bytes 196612
  59.8 22.6 %copy-start.4 = (bf16[256,128]{1,0:T(8,128)(2,1)S(1)}, bf16[256,128]{1,0:T(8,128)(2,1)}, u32[]{:S(2)}) copy-start(bf16[256,128]{1,0:T(8,128)(2,1)} %constant.68.clone.tall) | copy-start | bytes 196612
  59.8 7.7 %collective-permute-start.7 = (bf16[4,16,48,128]{3,2,1,0:T(8,128)(2,1)S(1)}, bf16[4,16,48,128]{3,2,1,0:T(8,128)(2,1)S(1)}, u32[]{:S(2)}, u32[]{:S(2)}) collective-permute-start(bf16[4,16,48,128]{3,2,1,0:T(8,128)(2,1)S(1)} %slice_bitcast_fusion), channel_id=1, source_target_pairs={{0,1},{1,0},{2,3},{3,2},{4,5},{5,4},{6,7},{7,6},{8,9},{9,8},{10,11... | collective-permute-start | bytes 2359304 | tf_op jit(solution)/shard_map/ppermute | solution.py:283
  68.2 14.2 %collective-permute-start.9 = (bf16[4,8,64,128]{3,2,1,0:T(8,128)(2,1)S(1)}, bf16[4,8,64,128]{3,2,1,0:T(8,128)(2,1)S(1)}, u32[]{:S(2)}, u32[]{:S(2)}) collective-permute-start(bf16[4,8,64,128]{3,2,1,0:T(8,128)(2,1)S(1)} %get-tuple-element.15), channel_id=1, source_target_pairs={{2,4},{4,2},{10,12},{12,10},{18,20},{20,18},{26,28},{28,26},{3,5},... | collective-permute-start | bytes 1572872 | tf_op jit(solution)/shard_map/ppermute | solution.py:296
  68.9 13.5 %collective-permute-start.8 = (bf16[4,4,96,128]{3,2,1,0:T(8,128)(2,1)S(1)}, bf16[4,4,96,128]{3,2,1,0:T(8,128)(2,1)S(1)}, u32[]{:S(2)}, u32[]{:S(2)}) collective-permute-start(bf16[4,4,96,128]{3,2,1,0:T(8,128)(2,1)S(1)} %get-tuple-element.14), channel_id=1, source_target_pairs={{0,2},{2,0},{4,6},{6,4},{8,10},{10,8},{12,14},{14,12},{16,18},{18,... | collective-permute-start | bytes 1179656 | tf_op jit(solution)/shard_map/ppermute | solution.py:295
  89.8 63.4 %copy-start.1 = (f32[1536,128]{1,0:T(8,128)S(1)}, f32[1536,128]{1,0:T(8,128)}, u32[]{:S(2)}) copy-start(f32[1536,128]{1,0:T(8,128)} %params.1) | copy-start | bytes 2359300
  89.8 63.4 %copy-start.2 = (f32[1536,128]{1,0:T(8,128)S(1)}, f32[1536,128]{1,0:T(8,128)}, u32[]{:S(2)}) copy-start(f32[1536,128]{1,0:T(8,128)} %mom.1) | copy-start | bytes 2359300
  89.8 63.4 %copy-start.5 = (bf16[128,256]{1,0:T(8,128)(2,1)S(1)}, bf16[128,256]{1,0:T(8,128)(2,1)}, u32[]{:S(2)}) copy-start(bf16[128,256]{1,0:T(8,128)(2,1)} %constant.69.clone.wide) | copy-start | bytes 196612
  89.8 63.4 %copy-start.6 = (bf16[256,128]{1,0:T(8,128)(2,1)S(1)}, bf16[256,128]{1,0:T(8,128)(2,1)}, u32[]{:S(2)}) copy-start(bf16[256,128]{1,0:T(8,128)(2,1)} %constant.70.clone.tall) | copy-start | bytes 196612
  127.9 25.2 %collective-permute-start.10 = (s16[1552,128]{1,0:T(8,128)(2,1)S(1)}, s16[1552,128]{1,0:T(8,128)(2,1)S(1)}, u32[]{:S(2)}, u32[]{:S(2)}) collective-permute-start(s16[1552,128]{1,0:T(8,128)(2,1)S(1)} %get-tuple-element.16), channel_id=1, source_target_pairs={{0,0},{32,128},{64,256},{96,384},{128,32},{160,160},{192,288},{224... | collective-permute-start | bytes 1191944 | tf_op jit(solution)/shard_map/ppermute | solution.py:312
  128.6 24.5 %all-to-all-start.2 = ((f32[32,1,128]{2,1,0:T(1,128)}), f32[32,1,128]{2,1,0:T(1,128)S(1)}, u32[]{:S(2)}, u32[]{:S(2)}) async-start(f32[32,1,128]{2,1,0:T(1,128)} %get-tuple-element.17), calls=%async_computation.2 | async-start | bytes 32768 | tf_op jit(solution)/shard_map/all_to_all | solution.py:313

commit v4 on v3

--- a/solution.py
+++ b/solution.py
@@ -54,18 +54,17 @@
     return both[:BS] + both[BS:] + dot(tall[:BS], lo)
 
 
-def pack_kernel(pos, g, out):
+def pack_kernel(pos, g, keep, give):
     c = pos[1]
-    for cc in range(2):
-        core = c if cc == 0 else 1 - c
+    for out, core in ((keep, c), (give, 1 - c)):
         for m in range(4):
             for w in range(4):
                 start = pl.multiple_of((2 * (4 * w + m) + core) * BS, BS)
-                out[0, cc, 4 * m + w] = g[:, pl.ds(start, BS)]
-
-
-def by_place(pos, mine, other, body):
-    mine = mine.at[:, 0]
+                out[0, 4 * m + w] = g[:, pl.ds(start, BS)]
+
+
+def by_place(pos, spread, body):
+    mine, other = spread.at[:, 0], spread.at[:, 1]
     for p in range(4):
         for c in range(2):
 
@@ -77,7 +76,7 @@
                     body(p, other, mine)
 
 
-def exchange_kernel(pos, mine, other, a, b):
+def exchange_kernel(pos, spread, a, b):
     def body(p, lo, hi):
         if p in (0, 3):
             s = slice(0, 4) if p == 0 else slice(12, 16)
@@ -96,10 +95,10 @@
             b[:, :, 0:48] = lo[:, 8:16]
             b[:, :, 48:64] = hi[:, 8:16, 0:16]
 
-    by_place(pos, mine, other, body)
-
-
-def assemble(pos, mine, other, a, b, whole):
+    by_place(pos, spread, body)
+
+
+def assemble(pos, spread, a, b, whole):
     def place(p, k, lo, hi, x):
         m = k + (k >= p)
         s = slice(4 * m, 4 * m + 4)
@@ -131,16 +130,16 @@
         for k in range(3):
             place(p, k, lo, hi, whole.at[:, 4 * k : 4 * k + 4])
 
-    by_place(pos, mine, other, body)
+    by_place(pos, spread, body)
 
 
 def exponent(size):
     return jnp.clip(jnp.floor(jnp.log2(jnp.maximum(size, F32(1e-30)))) + 1.0, -100.0, 200.0)
 
 
-def forward_kernel(pos, cut, mine, other, a, b, tall, wide, out, x, exps):
-    assemble(pos, mine, other, a, b, x)
-    p, grp = pos[0], pos[2]
+def forward_kernel(pos, cut, spread, a, b, left, wide, out, x, exps):
+    assemble(pos, spread, a, b, x)
+    p = pos[0]
     freq = lax.broadcasted_iota(jnp.int32, (BS, BS), 0) + lax.broadcasted_iota(jnp.int32, (BS, BS), 1)
     row = lax.broadcasted_iota(jnp.int32, (TAIL, BS), 0)
     exps[...] = jnp.zeros_like(exps)
@@ -151,14 +150,20 @@
         for k in range(3):
             m = k + (k >= p).astype(jnp.int32)
             blk = p - (p > m).astype(jnp.int32)
-            src = 4 * ((grp + 4 - w) % 4) + (p + 4 - m) % 4
             total = jnp.zeros((BS, BS), F32)
             for r in range(NX):
                 both = dot(x[r, 4 * k + w], wide[...])
                 hi, lo = split(both[:, :BS] + both[:, BS:])
-                four = dot(tall[...], jnp.concatenate([hi, lo], axis=1))
-                coef = four[:BS, :BS] + (four[BS:, :BS] + four[:BS, BS:])
-                total += jnp.where(freq <= cut[src, 4 * blk + r], coef, 0.0)
+                pairs = jnp.concatenate(
+                    [
+                        jnp.concatenate([hi, lo], axis=1),
+                        jnp.concatenate([hi, jnp.zeros_like(lo)], axis=1),
+                    ],
+                    axis=0,
+                )
+                both = dot(left[...], pairs)
+                coef = both[:, :BS] + both[:, BS:]
+                total += jnp.where(freq <= cut[4 * w + m, 4 * blk + r], coef, 0.0)
             e = exponent(jnp.max(jnp.abs(total), axis=0, keepdims=True))
             code = jnp.clip(jnp.floor(total * jnp.exp2(15.0 - e) + 0.5), -32767.0, 32767.0)
             out[4 * w + m, 0:BS] = code.astype(jnp.int32).astype(jnp.int16)
@@ -166,7 +171,9 @@
             square += jnp.sum(total * total, axis=0, keepdims=True)
         return square
 
-    square = lax.fori_loop(0, 4, step, jnp.zeros((1, BS), F32))
+    square = jnp.zeros((1, BS), F32)
+    for w in range(4):
+        square = step(w, square)
     e = exponent(square)
     scaled = jnp.minimum(square, F32(3e38)) * jnp.exp2(-0.5 * e) * jnp.exp2(-0.5 * e) * 16384.0
     d1 = jnp.floor(scaled)
@@ -233,59 +240,42 @@
 
 def per_device(pseudo_grads, outer_params, momentum, clip_level, block_picks, cutoffs):
     z = lax.axis_index("z")
-    pos = jnp.stack([z % 4, lax.axis_index("c"), z // 4]).astype(jnp.int32)
+    pos = jnp.stack([z % 4, lax.axis_index("c")]).astype(jnp.int32)
     hi, lo = table_parts()
     fwd_wide = jnp.asarray(np.concatenate([hi.T, lo.T], axis=1))
-    fwd_tall = jnp.asarray(np.concatenate([hi, lo], axis=0))
     inv_wide = jnp.asarray(np.concatenate([hi, lo], axis=1))
     inv_tall = jnp.asarray(np.concatenate([hi.T, lo.T], axis=0))
     rows = pseudo_grads.shape[1]
     swap = [(NY * i + j, NX * j + i) for i in range(NX) for j in range(NY)]
     shape = jax.ShapeDtypeStruct
 
-    picks, cuts = (
-        lax.dynamic_index_in_dim(v[:, 0], lax.axis_index("x"), 1, keepdims=False) for v in (block_picks, cutoffs)
-    )
-    hit = picks[:, :, None] == jnp.arange(BPO, dtype=jnp.int32)
-    cut = jnp.max(jnp.where(hit, cuts[:, :, None], -1), axis=1)
-    cut = jnp.pad(cut.T.reshape(4, BPO), ((0, 4), (0, BS - BPO)))
-    cut, pseudo_grads = lax.optimization_barrier((cut, pseudo_grads))
-    near = []
-    for n in range(4):
-        near.append(
-            lax.ppermute(
-                cut,
-                ("x", "y", "z"),
-                [
-                    ((NY * i + j) * NZ + 4 * g + q, (NX * j + i) * NZ + 4 * g + (q + n) % 4)
-                    for i in range(NX)
-                    for j in range(NY)
-                    for g in range(4)
-                    for q in range(4)
-                ],
-            )
-        )
-    near = jnp.stack(near)
-    far = [near] + [lax.ppermute(near, "z", [(i, (i + 4 * n) % NZ) for i in range(NZ)]) for n in range(1, 4)]
-    cut = lax.dynamic_index_in_dim(jnp.concatenate(far), z // 4, 1, keepdims=False)
-
-    packed = pl.pallas_call(
+    hit = block_picks[:, 0, :, :, None] == jnp.arange(BPO, dtype=jnp.int32)
+    cut = jnp.max(jnp.where(hit, cutoffs[:, 0, :, :, None], -1), axis=2)
+    cut = cut.transpose(1, 2, 0).reshape(NY, 4, 1, BPO)
+    cut = jnp.broadcast_to(cut, (NY, 4, 4, BPO)).reshape(NY * NZ, 1, BPO)
+    cut = jnp.pad(cut, ((0, 0), (0, 0), (0, BS - BPO)))
+    cut = lax.all_to_all(cut, ("y", "z"), 0, 0, tiled=True)
+    cut = lax.dynamic_slice_in_dim(cut[:, 0], lax.axis_index("x") * NZ, NZ, 0)
+
+    part = pl.BlockSpec((1, NZ, rows, BS), lambda j: (j, 0, 0, 0))
+    keep, give = pl.pallas_call(
         pack_kernel,
-        out_shape=shape((NY, NC, NZ, rows, BS), BF16),
+        out_shape=[shape((NY, NZ, rows, BS), BF16)] * 2,
         grid=(NY,),
         in_specs=[SMEM, pl.BlockSpec((None, rows, FF // NY), lambda j: (0, 0, j))],
-        out_specs=pl.BlockSpec((1, NC, NZ, rows, BS), lambda j: (j, 0, 0, 0, 0)),
+        out_specs=[part, part],
         compiler_params=BIG,
         name="pack",
     )(pos, pseudo_grads)
-    spread = lax.all_to_all(packed, "x", 0, 0, tiled=True)
-    spread, cut = lax.optimization_barrier((spread, cut))
-    other = lax.ppermute(spread[:, 1], "c", [(0, 1), (1, 0)])
+    got = lax.ppermute(give, "c", [(0, 1), (1, 0)])
+    chip = jnp.stack([keep, got], axis=1)
+    chip, cut = lax.optimization_barrier((chip, cut))
+    spread = lax.all_to_all(chip, "x", 0, 0, tiled=True)
 
     a, b = call(
         exchange_kernel,
         (shape((NX, 4, 96, BS), BF16), shape((NX, 8, 64, BS), BF16)),
-        (pos, spread, other),
+        (pos, spread),
         "exchange",
     )
     pair_a, pair_b = [], []
@@ -298,7 +288,7 @@
     coded = call(
         forward_kernel,
         shape((NZ, BS + TAIL, BS), jnp.int16),
-        (pos, cut, spread, other, a, b, fwd_tall, fwd_wide),
+        (pos, cut, spread, a, b, inv_wide, fwd_wide),
         "forward",
         [pltpu.VMEM((NX, BPO, BS, BS), BF16), pltpu.VMEM((NZ, BS), F32)],
     )

time: 158 us -> 141 us (0.89)
  the two profiles are of different devices: /device:TPU:1 before, /device:TPU:39 now
where the time goes in v4:
time: 141 us; the launch traced here: 140 us
  blocking collectives  57.1 us (40%)
  starting transfers between devices  37.4 us (27%)
  waiting for transfers between devices  32.3 us (23%)
  Pallas kernels  9.14 us (6%)
  local copies, waits for them, and re-layouts  2.51 us (2%)
  between operations  1.45 us (1%)
    all_to_all x1, blocking collectives, per_device(): coded = lax.all_to_all(coded, 'z', 0, 0, tiled=True)  36 us
    all_to_all x1, blocking collectives, per_device(): spread = lax.all_to_all(chip, 'x', 0, 0, tiled=True)  21.1 us
    all_to_all x1, starting transfers between devices, per_device(): cut = lax.all_to_all(cut, ('y', 'z'), 0, 0, tiled=True)  17.8 us
    all_to_all x1, waiting for transfers between devices, per_device(): cut = lax.all_to_all(cut, ('y', 'z'), 0, 0, tiled=True)  12.4 us
    all_to_all x1, waiting for transfers between devices, per_device(): norm = lax.all_to_all(norm, ('x', 'y', 'c'), 0, 0, tiled=True)  11.8 us
    all_to_all x1, starting transfers between devices, per_device(): norm = lax.all_to_all(norm, ('x', 'y', 'c'), 0, 0, tiled=True)  8.44 us
    ppermute x1, waiting for transfers between devices, per_device(): a = lax.ppermute(a, 'z', pair_a)  7.58 us
    pallas_call x3, Pallas kernels, call(): pl.pallas_call(kernel, out_shape=out_shape, in_specs=[SMEM if i.dtype ==...  4.76 us
  transfers between devices with their start and end apart: 6, of which 4 were waited for; matrix products, arithmetic and copies ran while one was open for 1% of the time, Pallas kernels for 0%

profile of v4, /device:TPU:39, one launch (start us, length us, event | category | flops | bytes accessed | tf_op | source)
XLA Modules:
  0.0 140.3 jit_solution(13306056224759968198)
XLA Ops:
  0.6 0.0 copy-start.6
  0.6 0.0 copy-start.7
  0.7 0.1 pad_add_fusion.pos
  0.7 0.0 copy-start
  0.7 1.4 %copy-done = bf16[1,48,16384]{2,1,0:T(8,128)(2,1)S(1)} copy-done((bf16[1,48,16384]{2,1,0:T(8,128)(2,1)S(1)}, bf16[1,48,16384]{2,1,0:T(8,128)(2,1)}, u32[]{:S(2)}) %copy-start) | copy-done | bytes 1572888
  2.1 1.2 pack.1
  3.3 2.6 %collective-permute-start = (bf16[4,16,48,128]{3,2,1,0:T(8,128)(2,1)S(1)}, bf16[4,16,48,128]{3,2,1,0:T(8,128)(2,1)S(1)}, u32[]{:S(2)}, u32[]{:S(2)}) collective-permute-start(bf16[4,16,48,128]{3,2,1,0:T(8,128)(2,1)S(1)} %get-tuple-element.11), channel_id=1, source_target_pairs={{0,1},{1,0},{2,3},{3,2},{4,5},{5,4},{6,7},{7,6},{8,9},{9,8},{10,11... | collective-permute-start | bytes 2359304 | tf_op jit(solution)/shard_map/ppermute | solution.py:270
  5.9 0.0 copy-done.6
  5.9 0.1 copy.12
  6.0 0.0 copy-done.7
  6.0 0.1 copy.11
  6.1 0.1 select_reduce_fusion
  6.3 0.1 copy.13
  6.4 0.1 broadcast_in_dim.25
  6.5 0.6 pad.4
  7.1 17.8 %all-to-all-start = ((s32[64,1,128]{2,1,0:T(1,128)}), s32[64,1,128]{2,1,0:T(1,128)S(1)}, u32[]{:S(2)}, u32[]{:S(2)}) async-start(s32[64,1,128]{2,1,0:T(1,128)} %pad.4), calls=%async_computation | async-start | bytes 65536 | tf_op jit(solution)/shard_map/all_to_all | solution.py:257
  25.0 12.4 %all-to-all-done = s32[64,1,128]{2,1,0:T(1,128)S(1)} async-done(((s32[64,1,128]{2,1,0:T(1,128)}), s32[64,1,128]{2,1,0:T(1,128)S(1)}, u32[]{:S(2)}, u32[]{:S(2)}) %all-to-all-start) | async-done | bytes 32800 | tf_op jit(solution)/shard_map/all_to_all | solution.py:257
  37.3 0.0 collective-permute-done
  37.3 0.1 pad_maximum_fusion
  37.5 21.1 %all_to_all.20.spread = bf16[4,2,16,48,128]{4,3,2,1,0:T(8,128)(2,1)S(1)} all-to-all(bf16[4,2,16,48,128]{4,3,2,1,0:T(8,128)(2,1)S(1)} %pad_maximum_fusion), channel_id=1, replica_groups=mesh['x'=4,'y'=4,'z'=16,'c'=2] {'x'}, dimensions={0} | all-to-all | bytes 3145728 | tf_op jit(solution)/shard_map/all_to_all | solution.py:273
  58.6 0.0 copy-start.3
  58.6 0.0 copy-start.5
  58.6 0.7 exchange.1
  59.3 2.4 %collective-permute-start.2 = (bf16[4,8,64,128]{3,2,1,0:T(8,128)(2,1)S(1)}, bf16[4,8,64,128]{3,2,1,0:T(8,128)(2,1)S(1)}, u32[]{:S(2)}, u32[]{:S(2)}) collective-permute-start(bf16[4,8,64,128]{3,2,1,0:T(8,128)(2,1)S(1)} %get-tuple-element.15), channel_id=1, source_target_pairs={{2,4},{4,2},{10,12},{12,10},{18,20},{20,18},{26,28},{28,26},{3,5},... | collective-permute-start | bytes 1572872 | tf_op jit(solution)/shard_map/ppermute | solution.py:286
  61.7 1.9 %collective-permute-start.1 = (bf16[4,4,96,128]{3,2,1,0:T(8,128)(2,1)S(1)}, bf16[4,4,96,128]{3,2,1,0:T(8,128)(2,1)S(1)}, u32[]{:S(2)}, u32[]{:S(2)}) collective-permute-start(bf16[4,4,96,128]{3,2,1,0:T(8,128)(2,1)S(1)} %get-tuple-element.14), channel_id=1, source_target_pairs={{0,2},{2,0},{4,6},{6,4},{8,10},{10,8},{12,14},{14,12},{16,18},{18,... | collective-permute-start | bytes 1179656 | tf_op jit(solution)/shard_map/ppermute | solution.py:285
  63.6 7.6 %collective-permute-done.1.a = bf16[4,4,96,128]{3,2,1,0:T(8,128)(2,1)S(1)} collective-permute-done((bf16[4,4,96,128]{3,2,1,0:T(8,128)(2,1)S(1)}, bf16[4,4,96,128]{3,2,1,0:T(8,128)(2,1)S(1)}, u32[]{:S(2)}, u32[]{:S(2)}) %collective-permute-start.1) | collective-permute-done | bytes 393248 | tf_op jit(solution)/shard_map/ppermute | solution.py:285
  71.2 0.6 collective-permute-done.2.b
  71.8 0.0 copy-done.3
  71.8 0.0 copy-done.5
  71.8 2.9 %forward.1 = s16[16,144,128]{2,1,0:T(8,128)(2,1)S(1)} custom-call(s32[2]{0:T(128)S(1)} %pad_add_fusion.pos, s32[16,128]{1,0:T(8,128)S(1)} %bitcast.10, bf16[4,2,16,48,128]{4,3,2,1,0:T(8,128)(2,1)S(1)} %all_to_all.20.spread, bf16[4,4,96,128]{3,2,1,0:T(8,128)(2,1)S(1)} %collective-permute-done.1.a, bf16[4,8,64,128]{3,2,1,0:T(8,128)(2,1)S(1)} %collective-permute-done.2.b, ...), custom_call_target="tpu_custom_call" | custom-call | tf_op jit(solution)/shard_map/forward/pallas_call | solution.py:230
  74.7 0.0 copy-start.1
  74.7 0.0 copy-start.2
  74.7 0.0 copy-start.4
  74.8 36.0 %all_to_all.21.z = s16[16,144,128]{2,1,0:T(8,128)(2,1)S(1)} all-to-all(s16[16,144,128]{2,1,0:T(8,128)(2,1)S(1)} %forward.1), channel_id=1, replica_groups=mesh['x'=4,'y'=4,'z'=16,'c'=2] {'z'}, dimensions={0} | all-to-all | bytes 1179648 | tf_op jit(solution)/shard_map/all_to_all | solution.py:295
  110.8 1.2 compact.1
  111.9 4.2 %collective-permute-start.3 = (s16[1552,128]{1,0:T(8,128)(2,1)S(1)}, s16[1552,128]{1,0:T(8,128)(2,1)S(1)}, u32[]{:S(2)}, u32[]{:S(2)}) collective-permute-start(s16[1552,128]{1,0:T(8,128)(2,1)S(1)} %get-tuple-element.16), channel_id=1, source_target_pairs={{0,0},{32,128},{64,256},{96,384},{128,32},{160,160},{192,288},{224... | collective-permute-start | bytes 1191944 | tf_op jit(solution)/shard_map/ppermute | solution.py:302
  116.1 8.4 %all-to-all-start.3 = ((f32[32,1,128]{2,1,0:T(1,128)}), f32[32,1,128]{2,1,0:T(1,128)S(1)}, u32[]{:S(2)}, u32[]{:S(2)}) async-start(f32[32,1,128]{2,1,0:T(1,128)} %get-tuple-element.17), calls=%async_computation.3 | async-start | bytes 32768 | tf_op jit(solution)/shard_map/all_to_all | solution.py:303
  125.2 11.8 %all-to-all-done.3.norm = f32[32,1,128]{2,1,0:T(1,128)S(1)} async-done(((f32[32,1,128]{2,1,0:T(1,128)}), f32[32,1,128]{2,1,0:T(1,128)S(1)}, u32[]{:S(2)}, u32[]{:S(2)}) %all-to-all-start.3) | async-done | bytes 16416 | tf_op jit(solution)/shard_map/all_to_all | solution.py:303
  137.0 0.0 collective-permute-done.3.code.tail
  137.0 0.0 copy-done.1
  137.0 0.0 copy-done.2
  137.0 0.0 copy-done.4
  137.0 3.2 %update.1 = (f32[1536,128]{1,0:T(8,128)}, f32[1536,128]{1,0:T(8,128)}) custom-call(s16[1552,128]{1,0:T(8,128)(2,1)S(1)} %collective-permute-done.3.code.tail, s16[1552,128]{1,0:T(8,128)(2,1)S(1)} %collective-permute-done.3.code.tail, f32[32,1,128]{2,1,0:T(1,128)S(1)} %all-to-all-done.3.norm, f32[1]{0:T(128)S(6)} %copy.14.clip, f32[1536,128]{1,0:T(8,128)S(1)} %copy-done.1, ...), custom_call_target="tpu_custom_call" | custom-call | tf_op jit(solution)/shard_map/update/pallas_call | solution.py:306
  (2 shorter events, 0.0 us)
Async XLA Ops:
  0.6 5.3 %copy-start.6 = (s32[4,1,4,6]{3,2,1,0:T(4,128)S(1)}, s32[4,1,4,6]{3,2,1,0:T(4,128)}, u32[]{:S(2)}) copy-start(s32[4,1,4,6]{3,2,1,0:T(4,128)} %param.14) | copy-start | bytes 1156
  0.6 5.4 %copy-start.7 = (s32[4,1,4,6]{3,2,1,0:T(4,128)S(1)}, s32[4,1,4,6]{3,2,1,0:T(4,128)}, u32[]{:S(2)}) copy-start(s32[4,1,4,6]{3,2,1,0:T(4,128)} %param.13) | copy-start | bytes 1156
  0.7 1.4 %copy-start = (bf16[1,48,16384]{2,1,0:T(8,128)(2,1)S(1)}, bf16[1,48,16384]{2,1,0:T(8,128)(2,1)}, u32[]{:S(2)}) copy-start(bf16[1,48,16384]{2,1,0:T(8,128)(2,1)} %g.1) | copy-start | bytes 4718596
  3.3 34.0 %collective-permute-start = (bf16[4,16,48,128]{3,2,1,0:T(8,128)(2,1)S(1)}, bf16[4,16,48,128]{3,2,1,0:T(8,128)(2,1)S(1)}, u32[]{:S(2)}, u32[]{:S(2)}) collective-permute-start(bf16[4,16,48,128]{3,2,1,0:T(8,128)(2,1)S(1)} %get-tuple-element.11), channel_id=1, source_target_pairs={{0,1},{1,0},{2,3},{3,2},{4,5},{5,4},{6,7},{7,6},{8,9},{9,8},{10,11... | collective-permute-start | bytes 2359304 | tf_op jit(solution)/shard_map/ppermute | solution.py:270
  7.1 30.2 %all-to-all-start = ((s32[64,1,128]{2,1,0:T(1,128)}), s32[64,1,128]{2,1,0:T(1,128)S(1)}, u32[]{:S(2)}, u32[]{:S(2)}) async-start(s32[64,1,128]{2,1,0:T(1,128)} %pad.4), calls=%async_computation | async-start | bytes 65536 | tf_op jit(solution)/shard_map/all_to_all | solution.py:257
  58.6 13.2 %copy-start.3 = (bf16[128,256]{1,0:T(8,128)(2,1)S(1)}, bf16[128,256]{1,0:T(8,128)(2,1)}, u32[]{:S(2)}) copy-start(bf16[128,256]{1,0:T(8,128)(2,1)} %constant.44.clone.left.wide) | copy-start | bytes 196612
  58.6 13.2 %copy-start.5 = (bf16[128,256]{1,0:T(8,128)(2,1)S(1)}, bf16[128,256]{1,0:T(8,128)(2,1)}, u32[]{:S(2)}) copy-start(bf16[128,256]{1,0:T(8,128)(2,1)} %constant.43.clone.wide) | copy-start | bytes 196612
  59.3 12.5 %collective-permute-start.2 = (bf16[4,8,64,128]{3,2,1,0:T(8,128)(2,1)S(1)}, bf16[4,8,64,128]{3,2,1,0:T(8,128)(2,1)S(1)}, u32[]{:S(2)}, u32[]{:S(2)}) collective-permute-start(bf16[4,8,64,128]{3,2,1,0:T(8,128)(2,1)S(1)} %get-tuple-element.15), channel_id=1, source_target_pairs={{2,4},{4,2},{10,12},{12,10},{18,20},{20,18},{26,28},{28,26},{3,5},... | collective-permute-start | bytes 1572872 | tf_op jit(solution)/shard_map/ppermute | solution.py:286
  61.7 9.5 %collective-permute-start.1 = (bf16[4,4,96,128]{3,2,1,0:T(8,128)(2,1)S(1)}, bf16[4,4,96,128]{3,2,1,0:T(8,128)(2,1)S(1)}, u32[]{:S(2)}, u32[]{:S(2)}) collective-permute-start(bf16[4,4,96,128]{3,2,1,0:T(8,128)(2,1)S(1)} %get-tuple-element.14), channel_id=1, source_target_pairs={{0,2},{2,0},{4,6},{6,4},{8,10},{10,8},{12,14},{14,12},{16,18},{18,... | collective-permute-start | bytes 1179656 | tf_op jit(solution)/shard_map/ppermute | solution.py:285
  74.7 62.3 %copy-start.1 = (f32[1536,128]{1,0:T(8,128)S(1)}, f32[1536,128]{1,0:T(8,128)}, u32[]{:S(2)}) copy-start(f32[1536,128]{1,0:T(8,128)} %params.1) | copy-start | bytes 2359300
  74.7 62.3 %copy-start.2 = (f32[1536,128]{1,0:T(8,128)S(1)}, f32[1536,128]{1,0:T(8,128)}, u32[]{:S(2)}) copy-start(f32[1536,128]{1,0:T(8,128)} %mom.1) | copy-start | bytes 2359300
  74.7 62.3 %copy-start.4 = (bf16[256,128]{1,0:T(8,128)(2,1)S(1)}, bf16[256,128]{1,0:T(8,128)(2,1)}, u32[]{:S(2)}) copy-start(bf16[256,128]{1,0:T(8,128)(2,1)} %constant.45.clone.tall) | copy-start | bytes 196612
  111.9 25.1 %collective-permute-start.3 = (s16[1552,128]{1,0:T(8,128)(2,1)S(1)}, s16[1552,128]{1,0:T(8,128)(2,1)S(1)}, u32[]{:S(2)}, u32[]{:S(2)}) collective-permute-start(s16[1552,128]{1,0:T(8,128)(2,1)S(1)} %get-tuple-element.16), channel_id=1, source_target_pairs={{0,0},{32,128},{64,256},{96,384},{128,32},{160,160},{192,288},{224... | collective-permute-start | bytes 1191944 | tf_op jit(solution)/shard_map/ppermute | solution.py:302
  116.1 20.9 %all-to-all-start.3 = ((f32[32,1,128]{2,1,0:T(1,128)}), f32[32,1,128]{2,1,0:T(1,128)S(1)}, u32[]{:S(2)}, u32[]{:S(2)}) async-start(f32[32,1,128]{2,1,0:T(1,128)} %get-tuple-element.17), calls=%async_computation.3 | async-start | bytes 32768 | tf_op jit(solution)/shard_map/all_to_all | solution.py:303

commit v5 on v4

--- a/solution.py
+++ b/solution.py
@@ -54,26 +54,17 @@
     return both[:BS] + both[BS:] + dot(tall[:BS], lo)
 
 
-def pack_kernel(pos, g, keep, give):
-    c = pos[1]
-    for out, core in ((keep, c), (give, 1 - c)):
+def pack_kernel(g, out):
+    for core in range(NC):
         for m in range(4):
             for w in range(4):
-                start = pl.multiple_of((2 * (4 * w + m) + core) * BS, BS)
-                out[0, 4 * m + w] = g[:, pl.ds(start, BS)]
+                start = (2 * (4 * w + m) + core) * BS
+                out[0, core, 4 * m + w] = g[:, start : start + BS]
 
 
 def by_place(pos, spread, body):
-    mine, other = spread.at[:, 0], spread.at[:, 1]
     for p in range(4):
-        for c in range(2):
-
-            @pl.when((pos[0] == p) & (pos[1] == c))
-            def _(p=p, c=c):
-                if c == 0:
-                    body(p, mine, other)
-                else:
-                    body(p, other, mine)
+        pl.when(pos[0] == p)(functools.partial(body, p, spread.at[:, 0], spread.at[:, 1]))
 
 
 def exchange_kernel(pos, spread, a, b):
@@ -137,43 +128,43 @@
     return jnp.clip(jnp.floor(jnp.log2(jnp.maximum(size, F32(1e-30)))) + 1.0, -100.0, 200.0)
 
 
-def forward_kernel(pos, cut, spread, a, b, left, wide, out, x, exps):
+def forward_kernel(pos, spread, a, b, left, wide, out, x):
     assemble(pos, spread, a, b, x)
+    for i in range(BPO):
+        for r in range(NX):
+            both = dot(x[r, i], wide[...])
+            hi, lo = split(both[:, :BS] + both[:, BS:])
+            pairs = jnp.concatenate(
+                [
+                    jnp.concatenate([hi, lo], axis=1),
+                    jnp.concatenate([hi, jnp.zeros_like(lo)], axis=1),
+                ],
+                axis=0,
+            )
+            both = dot(left[...], pairs)
+            out[i, r] = both[:, :BS] + both[:, BS:]
+
+
+def mask_kernel(pos, cut, coef, out, exps):
     p = pos[0]
     freq = lax.broadcasted_iota(jnp.int32, (BS, BS), 0) + lax.broadcasted_iota(jnp.int32, (BS, BS), 1)
     row = lax.broadcasted_iota(jnp.int32, (TAIL, BS), 0)
     exps[...] = jnp.zeros_like(exps)
     for w in range(4):
         out[4 * w + p, 0:BS] = jnp.zeros((BS, BS), jnp.int16)
-
-    def step(w, square):
-        for k in range(3):
-            m = k + (k >= p).astype(jnp.int32)
-            blk = p - (p > m).astype(jnp.int32)
-            total = jnp.zeros((BS, BS), F32)
-            for r in range(NX):
-                both = dot(x[r, 4 * k + w], wide[...])
-                hi, lo = split(both[:, :BS] + both[:, BS:])
-                pairs = jnp.concatenate(
-                    [
-                        jnp.concatenate([hi, lo], axis=1),
-                        jnp.concatenate([hi, jnp.zeros_like(lo)], axis=1),
-                    ],
-                    axis=0,
-                )
-                both = dot(left[...], pairs)
-                coef = both[:, :BS] + both[:, BS:]
-                total += jnp.where(freq <= cut[4 * w + m, 4 * blk + r], coef, 0.0)
-            e = exponent(jnp.max(jnp.abs(total), axis=0, keepdims=True))
-            code = jnp.clip(jnp.floor(total * jnp.exp2(15.0 - e) + 0.5), -32767.0, 32767.0)
-            out[4 * w + m, 0:BS] = code.astype(jnp.int32).astype(jnp.int16)
-            exps[pl.ds(4 * w + m, 1), :] = e
-            square += jnp.sum(total * total, axis=0, keepdims=True)
-        return square
-
     square = jnp.zeros((1, BS), F32)
-    for w in range(4):
-        square = step(w, square)
+    for i in range(BPO):
+        k, w = divmod(i, 4)
+        m = k + (k >= p).astype(jnp.int32)
+        blk = p - (p > m).astype(jnp.int32)
+        total = jnp.zeros((BS, BS), F32)
+        for r in range(NX):
+            total += jnp.where(freq <= cut[4 * w + m, 4 * blk + r], coef[i, r], 0.0)
+        e = exponent(jnp.max(jnp.abs(total), axis=0, keepdims=True))
+        code = jnp.clip(jnp.floor(total * jnp.exp2(15.0 - e) + 0.5), -32767.0, 32767.0)
+        out[4 * w + m, 0:BS] = code.astype(jnp.int32).astype(jnp.int16)
+        exps[pl.ds(4 * w + m, 1), :] = e
+        square += jnp.sum(total * total, axis=0, keepdims=True)
     e = exponent(square)
     scaled = jnp.minimum(square, F32(3e38)) * jnp.exp2(-0.5 * e) * jnp.exp2(-0.5 * e) * 16384.0
     d1 = jnp.floor(scaled)
@@ -223,7 +214,7 @@
 
 SMEM = pl.BlockSpec(memory_space=pltpu.SMEM)
 VMEM = pl.BlockSpec(memory_space=pltpu.VMEM)
-BIG = pltpu.CompilerParams(vmem_limit_bytes=40 * 1024 * 1024)
+BIG = pltpu.CompilerParams(vmem_limit_bytes=16 * 1024 * 1024)
 
 
 def call(kernel, out_shape, inputs, name, scratch=()):
@@ -240,7 +231,7 @@
 
 def per_device(pseudo_grads, outer_params, momentum, clip_level, block_picks, cutoffs):
     z = lax.axis_index("z")
-    pos = jnp.stack([z % 4, lax.axis_index("c")]).astype(jnp.int32)
+    pos = (z % 4).astype(jnp.int32).reshape(1)
     hi, lo = table_parts()
     fwd_wide = jnp.asarray(np.concatenate([hi.T, lo.T], axis=1))
     inv_wide = jnp.asarray(np.concatenate([hi, lo], axis=1))
@@ -249,28 +240,27 @@
     swap = [(NY * i + j, NX * j + i) for i in range(NX) for j in range(NY)]
     shape = jax.ShapeDtypeStruct
 
-    hit = block_picks[:, 0, :, :, None] == jnp.arange(BPO, dtype=jnp.int32)
-    cut = jnp.max(jnp.where(hit, cutoffs[:, 0, :, :, None], -1), axis=2)
-    cut = cut.transpose(1, 2, 0).reshape(NY, 4, 1, BPO)
-    cut = jnp.broadcast_to(cut, (NY, 4, 4, BPO)).reshape(NY * NZ, 1, BPO)
-    cut = jnp.pad(cut, ((0, 0), (0, 0), (0, BS - BPO)))
-    cut = lax.all_to_all(cut, ("y", "z"), 0, 0, tiled=True)
-    cut = lax.dynamic_slice_in_dim(cut[:, 0], lax.axis_index("x") * NZ, NZ, 0)
-
-    part = pl.BlockSpec((1, NZ, rows, BS), lambda j: (j, 0, 0, 0))
-    keep, give = pl.pallas_call(
+    picks, cuts = (
+        lax.dynamic_index_in_dim(v[:, 0], lax.axis_index("x"), 1, keepdims=False) for v in (block_picks, cutoffs)
+    )
+    hit = picks[:, :, None] == jnp.arange(BPO, dtype=jnp.int32)
+    cut = jnp.max(jnp.where(hit, cuts[:, :, None], -1), axis=1)
+    cut = jnp.pad(cut.T.reshape(4, BPO), ((0, 4), (0, BS - BPO)))
+    cut, pseudo_grads = lax.optimization_barrier((cut, pseudo_grads))
+    cut = lax.ppermute(cut, ("x", "y"), swap)
+
+    chip = pl.pallas_call(
         pack_kernel,
-        out_shape=[shape((NY, NZ, rows, BS), BF16)] * 2,
+        out_shape=shape((NY, NC, NZ, rows, BS), BF16),
         grid=(NY,),
-        in_specs=[SMEM, pl.BlockSpec((None, rows, FF // NY), lambda j: (0, 0, j))],
-        out_specs=[part, part],
+        in_specs=[pl.BlockSpec((None, rows, FF // NY), lambda j: (0, 0, j))],
+        out_specs=pl.BlockSpec((1, NC, NZ, rows, BS), lambda j: (j, 0, 0, 0, 0)),
         compiler_params=BIG,
         name="pack",
-    )(pos, pseudo_grads)
-    got = lax.ppermute(give, "c", [(0, 1), (1, 0)])
-    chip = jnp.stack([keep, got], axis=1)
-    chip, cut = lax.optimization_barrier((chip, cut))
-    spread = lax.all_to_all(chip, "x", 0, 0, tiled=True)
+    )(pseudo_grads)
+    chip = lax.all_to_all(chip.reshape(NY * NC, NZ, rows, BS), ("x", "c"), 0, 0, tiled=True)
+    spread = chip.reshape(NX, NC, NZ, rows, BS)
+    spread, cut = lax.optimization_barrier((spread, cut))
 
     a, b = call(
         exchange_kernel,
@@ -285,12 +275,23 @@
     a = lax.ppermute(a, "z", pair_a)
     b = lax.ppermute(b, "z", pair_b)
 
+    cut = jnp.broadcast_to(cut[:4, None], (4, 4, BS)).reshape(NZ, 1, BS)
+    cut, a, b = lax.optimization_barrier((cut, a, b))
+    cut = lax.all_to_all(cut, "z", 0, 0, tiled=True)[:, 0]
+
+    coef = call(
+        forward_kernel,
+        shape((BPO, NX, BS, BS), F32),
+        (pos, spread, a, b, inv_wide, fwd_wide),
+        "forward",
+        [pltpu.VMEM((NX, BPO, BS, BS), BF16)],
+    )
     coded = call(
-        forward_kernel,
+        mask_kernel,
         shape((NZ, BS + TAIL, BS), jnp.int16),
-        (pos, cut, spread, a, b, inv_wide, fwd_wide),
-        "forward",
-        [pltpu.VMEM((NX, BPO, BS, BS), BF16), pltpu.VMEM((NZ, BS), F32)],
+        (pos, cut, coef),
+        "mask",
+        [pltpu.VMEM((NZ, BS), F32)],
     )
     coded = lax.all_to_all(coded, "z", 0, 0, tiled=True)
     coded, norm = call(

time: 141 us -> 141 us (level)
  the two profiles are of different devices: /device:TPU:39 before, /device:TPU:1 now
where the time goes in v5:
time: 141 us; the launch traced here: 140 us
  waiting for transfers between devices  47.2 us (33%)
  starting transfers between devices  40.1 us (28%)
  blocking collectives  35.4 us (25%)
  Pallas kernels  9.17 us (7%)
  local copies, waits for them, and re-layouts  6.67 us (5%)
  between operations  1.45 us (1%)
    all_to_all x1, blocking collectives, per_device(): coded = lax.all_to_all(coded, 'z', 0, 0, tiled=True)  35.4 us
    all_to_all x1, waiting for transfers between devices, per_device(): lax.all_to_all(chip.reshape(NY * NC, NZ, rows, BS), ('x', 'c'), 0, 0, til...  19.9 us
    all_to_all x1, starting transfers between devices, per_device(): norm = lax.all_to_all(norm, ('x', 'y', 'c'), 0, 0, tiled=True)  13.7 us
    all_to_all x1, starting transfers between devices, per_device(): cut = lax.all_to_all(cut, 'z', 0, 0, tiled=True)[:, 0]  12 us
    all_to_all x1, starting transfers between devices, per_device(): lax.all_to_all(chip.reshape(NY * NC, NZ, rows, BS), ('x', 'c'), 0, 0, til...  10.4 us
    all_to_all x1, waiting for transfers between devices, per_device(): norm = lax.all_to_all(norm, ('x', 'y', 'c'), 0, 0, tiled=True)  10.1 us
    ppermute x1, waiting for transfers between devices, per_device(): a = lax.ppermute(a, 'z', pair_a)  9.66 us
    all_to_all x1, waiting for transfers between devices, per_device(): cut = lax.all_to_all(cut, 'z', 0, 0, tiled=True)[:, 0]  7.49 us
  transfers between devices with their start and end apart: 7, of which 4 were waited for; matrix products, arithmetic and copies ran while one was open for 0% of the time, Pallas kernels for 1%

profile of v5, /device:TPU:1, one launch (start us, length us, event | category | flops | bytes accessed | tf_op | source)
XLA Modules:
  0.0 140.0 jit_solution(6644168459999954709)
XLA Ops:
  0.6 0.7 constant_dynamic-slice_fusion
  1.4 0.1 copy.12
  1.5 0.1 copy.11
  1.5 0.1 select_reduce_fusion
  1.6 0.1 copy.13
  1.7 0.1 reshape.29
  1.8 0.0 copy-start.2
  1.8 1.4 %copy-done.2 = bf16[1,48,16384]{2,1,0:T(8,128)(2,1)S(1)} copy-done((bf16[1,48,16384]{2,1,0:T(8,128)(2,1)S(1)}, bf16[1,48,16384]{2,1,0:T(8,128)(2,1)}, u32[]{:S(2)}) %copy-start.2) | copy-done | bytes 1572888
  3.2 1.9 %pack.1 = bf16[4,2,16,48,128]{4,3,2,1,0:T(8,128)(2,1)} custom-call(bf16[1,48,16384]{2,1,0:T(8,128)(2,1)S(1)} %copy-done.2), custom_call_target="tpu_custom_call" | custom-call | tf_op jit(solution)/shard_map/pack/pallas_call | solution.py:252
  5.1 10.4 %all-to-all-start = ((bf16[8,16,48,128]{3,2,1,0:T(8,128)(2,1)}), bf16[8,16,48,128]{3,2,1,0:T(8,128)(2,1)S(1)}, u32[]{:S(2)}, u32[]{:S(2)}) async-start(bf16[8,16,48,128]{3,2,1,0:T(8,128)(2,1)} %bitcast.4), calls=%async_computation | async-start | bytes 3145728 | tf_op jit(solution)/shard_map/all_to_all | solution.py:261
  15.5 0.0 copy-start.5
  15.5 0.0 copy-start.6
  15.5 0.8 collective-permute-start
  16.3 0.0 collective-permute-done
  16.3 19.9 %all-to-all-done = bf16[8,16,48,128]{3,2,1,0:T(8,128)(2,1)S(1)} async-done(((bf16[8,16,48,128]{3,2,1,0:T(8,128)(2,1)}), bf16[8,16,48,128]{3,2,1,0:T(8,128)(2,1)S(1)}, u32[]{:S(2)}, u32[]{:S(2)}) %all-to-all-start) | async-done | bytes 1572896 | tf_op jit(solution)/shard_map/all_to_all | solution.py:261
  36.3 0.7 collective-permute-start.2
  37.0 1.9 %collective-permute-start.1 = (bf16[4,4,96,128]{3,2,1,0:T(8,128)(2,1)S(1)}, bf16[4,4,96,128]{3,2,1,0:T(8,128)(2,1)S(1)}, u32[]{:S(2)}, u32[]{:S(2)}) collective-permute-start(bf16[4,4,96,128]{3,2,1,0:T(8,128)(2,1)S(1)} %get-tuple-element.17), channel_id=1, source_target_pairs={{0,2},{2,0},{4,6},{6,4},{8,10},{10,8},{12,14},{14,12},{16,18},{18,... | collective-permute-start | bytes 1179656 | tf_op jit(solution)/shard_map/ppermute | solution.py:275
  38.9 9.7 %collective-permute-done.1.a = bf16[4,4,96,128]{3,2,1,0:T(8,128)(2,1)S(1)} collective-permute-done((bf16[4,4,96,128]{3,2,1,0:T(8,128)(2,1)S(1)}, bf16[4,4,96,128]{3,2,1,0:T(8,128)(2,1)S(1)}, u32[]{:S(2)}, u32[]{:S(2)}) %collective-permute-start.1) | collective-permute-done | bytes 393248 | tf_op jit(solution)/shard_map/ppermute | solution.py:275
  48.6 0.0 collective-permute-done.2.b
  48.6 0.6 broadcast_in_dim.26
  49.2 12.0 %all-to-all-start.1 = ((s32[16,1,128]{2,1,0:T(1,128)}), s32[16,1,128]{2,1,0:T(1,128)S(1)}, u32[]{:S(2)}, u32[]{:S(2)}) async-start(s32[16,1,128]{2,1,0:T(1,128)} %bitcast.6), calls=%async_computation.1 | async-start | bytes 16384 | tf_op jit(solution)/shard_map/all_to_all | solution.py:280
  61.2 0.0 copy-done.5
  61.2 0.0 copy-done.6
  61.3 2.1 %forward.1.coef = f32[12,4,128,128]{3,2,1,0:T(8,128)S(1)} custom-call(s32[1]{0:T(128)} %bitcast.pos, bf16[4,2,16,48,128]{4,3,2,1,0:T(8,128)(2,1)S(1)} %bitcast.9, bf16[4,4,96,128]{3,2,1,0:T(8,128)(2,1)S(1)} %collective-permute-done.1.a, bf16[4,8,64,128]{3,2,1,0:T(8,128)(2,1)S(1)} %collective-permute-done.2.b, bf16[128,256]{1,0:T(8,128)(2,1)S(1)} %copy-done.5, ...), custom_call_target="tpu_custom_call" | custom-call | tf_op jit(solution)/shard_map/forward/pallas_call | solution.py:221
  63.3 0.0 copy-start
  63.3 1.6 %copy-done = f32[12,4,128,128]{3,2,1,0:T(8,128)} copy-done((f32[12,4,128,128]{3,2,1,0:T(8,128)}, f32[12,4,128,128]{3,2,1,0:T(8,128)S(1)}, u32[]{:S(2)}) %copy-start) | copy-done | bytes 3145752
  65.0 7.5 %all-to-all-done.1 = s32[16,1,128]{2,1,0:T(1,128)S(1)} async-done(((s32[16,1,128]{2,1,0:T(1,128)}), s32[16,1,128]{2,1,0:T(1,128)S(1)}, u32[]{:S(2)}, u32[]{:S(2)}) %all-to-all-start.1) | async-done | bytes 8224 | tf_op jit(solution)/shard_map/all_to_all | solution.py:280
  72.5 0.0 copy-start.1
  72.5 1.9 %copy-done.1 = f32[12,4,128,128]{3,2,1,0:T(8,128)S(1)} copy-done((f32[12,4,128,128]{3,2,1,0:T(8,128)S(1)}, f32[12,4,128,128]{3,2,1,0:T(8,128)}, u32[]{:S(2)}) %copy-start.1) | copy-done | bytes 3145752
  74.4 1.3 mask.1
  75.6 0.0 copy-start.3
  75.7 0.0 copy-start.4
  75.7 0.0 copy-start.7
  75.7 35.4 %all_to_all.20.z = s16[16,144,128]{2,1,0:T(8,128)(2,1)S(1)} all-to-all(s16[16,144,128]{2,1,0:T(8,128)(2,1)S(1)} %mask.1), channel_id=1, replica_groups=mesh['x'=4,'y'=4,'z'=16,'c'=2] {'z'}, dimensions={0} | all-to-all | bytes 1179648 | tf_op jit(solution)/shard_map/all_to_all | solution.py:296
  111.0 0.7 compact.1
  111.7 0.7 collective-permute-start.3
  112.4 13.7 %all-to-all-start.3 = ((f32[32,1,128]{2,1,0:T(1,128)}), f32[32,1,128]{2,1,0:T(1,128)S(1)}, u32[]{:S(2)}, u32[]{:S(2)}) async-start(f32[32,1,128]{2,1,0:T(1,128)} %get-tuple-element.23), calls=%async_computation.3 | async-start | bytes 32768 | tf_op jit(solution)/shard_map/all_to_all | solution.py:304
  126.7 10.1 %all-to-all-done.3.norm = f32[32,1,128]{2,1,0:T(1,128)S(1)} async-done(((f32[32,1,128]{2,1,0:T(1,128)}), f32[32,1,128]{2,1,0:T(1,128)S(1)}, u32[]{:S(2)}, u32[]{:S(2)}) %all-to-all-start.3) | async-done | bytes 16416 | tf_op jit(solution)/shard_map/all_to_all | solution.py:304
  136.8 0.0 collective-permute-done.3.code.tail
  136.8 0.0 copy-done.3
  136.8 0.0 copy-done.4
  136.8 0.0 copy-done.7
  136.8 3.2 %update.1 = (f32[1536,128]{1,0:T(8,128)}, f32[1536,128]{1,0:T(8,128)}) custom-call(s16[1552,128]{1,0:T(8,128)(2,1)S(1)} %collective-permute-done.3.code.tail, s16[1552,128]{1,0:T(8,128)(2,1)S(1)} %collective-permute-done.3.code.tail, f32[32,1,128]{2,1,0:T(1,128)S(1)} %all-to-all-done.3.norm, f32[1]{0:T(128)S(6)} %copy.14.clip, f32[1536,128]{1,0:T(8,128)S(1)} %copy-done.3, ...), custom_call_target="tpu_custom_call" | custom-call | tf_op jit(solution)/shard_map/update/pallas_call | solution.py:307
  (3 shorter events, 0.1 us)
Async XLA Ops:
  1.8 1.4 %copy-start.2 = (bf16[1,48,16384]{2,1,0:T(8,128)(2,1)S(1)}, bf16[1,48,16384]{2,1,0:T(8,128)(2,1)}, u32[]{:S(2)}) copy-start(bf16[1,48,16384]{2,1,0:T(8,128)(2,1)} %g) | copy-start | bytes 4718596
  5.1 31.1 %all-to-all-start = ((bf16[8,16,48,128]{3,2,1,0:T(8,128)(2,1)}), bf16[8,16,48,128]{3,2,1,0:T(8,128)(2,1)S(1)}, u32[]{:S(2)}, u32[]{:S(2)}) async-start(bf16[8,16,48,128]{3,2,1,0:T(8,128)(2,1)} %bitcast.4), calls=%async_computation | async-start | bytes 3145728 | tf_op jit(solution)/shard_map/all_to_all | solution.py:261
  15.5 45.7 %copy-start.5 = (bf16[128,256]{1,0:T(8,128)(2,1)S(1)}, bf16[128,256]{1,0:T(8,128)(2,1)}, u32[]{:S(2)}) copy-start(bf16[128,256]{1,0:T(8,128)(2,1)} %constant.45.clone.left.wide) | copy-start | bytes 196612
  15.5 45.7 %copy-start.6 = (bf16[128,256]{1,0:T(8,128)(2,1)S(1)}, bf16[128,256]{1,0:T(8,128)(2,1)}, u32[]{:S(2)}) copy-start(bf16[128,256]{1,0:T(8,128)(2,1)} %constant.44.clone.wide) | copy-start | bytes 196612
  15.5 0.8 collective-permute-start
  36.3 12.3 %collective-permute-start.2 = (bf16[4,8,64,128]{3,2,1,0:T(8,128)(2,1)S(1)}, bf16[4,8,64,128]{3,2,1,0:T(8,128)(2,1)S(1)}, u32[]{:S(2)}, u32[]{:S(2)}) collective-permute-start(bf16[4,8,64,128]{3,2,1,0:T(8,128)(2,1)S(1)} %get-tuple-element.18), channel_id=1, source_target_pairs={{2,4},{4,2},{10,12},{12,10},{18,20},{20,18},{26,28},{28,26},{3,5},... | collective-permute-start | bytes 1572872 | tf_op jit(solution)/shard_map/ppermute | solution.py:276
  37.0 11.6 %collective-permute-start.1 = (bf16[4,4,96,128]{3,2,1,0:T(8,128)(2,1)S(1)}, bf16[4,4,96,128]{3,2,1,0:T(8,128)(2,1)S(1)}, u32[]{:S(2)}, u32[]{:S(2)}) collective-permute-start(bf16[4,4,96,128]{3,2,1,0:T(8,128)(2,1)S(1)} %get-tuple-element.17), channel_id=1, source_target_pairs={{0,2},{2,0},{4,6},{6,4},{8,10},{10,8},{12,14},{14,12},{16,18},{18,... | collective-permute-start | bytes 1179656 | tf_op jit(solution)/shard_map/ppermute | solution.py:275
  49.2 23.3 %all-to-all-start.1 = ((s32[16,1,128]{2,1,0:T(1,128)}), s32[16,1,128]{2,1,0:T(1,128)S(1)}, u32[]{:S(2)}, u32[]{:S(2)}) async-start(s32[16,1,128]{2,1,0:T(1,128)} %bitcast.6), calls=%async_computation.1 | async-start | bytes 16384 | tf_op jit(solution)/shard_map/all_to_all | solution.py:280
  63.3 1.6 %copy-start = (f32[12,4,128,128]{3,2,1,0:T(8,128)}, f32[12,4,128,128]{3,2,1,0:T(8,128)S(1)}, u32[]{:S(2)}) copy-start(f32[12,4,128,128]{3,2,1,0:T(8,128)S(1)} %forward.1.coef) | copy-start | bytes 9437188
  72.5 1.9 %copy-start.1 = (f32[12,4,128,128]{3,2,1,0:T(8,128)S(1)}, f32[12,4,128,128]{3,2,1,0:T(8,128)}, u32[]{:S(2)}) copy-start(f32[12,4,128,128]{3,2,1,0:T(8,128)} %copy-done) | copy-start | bytes 9437188
  75.6 61.2 %copy-start.3 = (f32[1536,128]{1,0:T(8,128)S(1)}, f32[1536,128]{1,0:T(8,128)}, u32[]{:S(2)}) copy-start(f32[1536,128]{1,0:T(8,128)} %params.1) | copy-start | bytes 2359300
  75.7 61.1 %copy-start.4 = (f32[1536,128]{1,0:T(8,128)S(1)}, f32[1536,128]{1,0:T(8,128)}, u32[]{:S(2)}) copy-start(f32[1536,128]{1,0:T(8,128)} %mom.1) | copy-start | bytes 2359300
  75.7 61.1 %copy-start.7 = (bf16[256,128]{1,0:T(8,128)(2,1)S(1)}, bf16[256,128]{1,0:T(8,128)(2,1)}, u32[]{:S(2)}) copy-start(bf16[256,128]{1,0:T(8,128)(2,1)} %constant.46.clone.tall) | copy-start | bytes 196612
  111.7 25.1 %collective-permute-start.3 = (s16[1552,128]{1,0:T(8,128)(2,1)S(1)}, s16[1552,128]{1,0:T(8,128)(2,1)S(1)}, u32[]{:S(2)}, u32[]{:S(2)}) collective-permute-start(s16[1552,128]{1,0:T(8,128)(2,1)S(1)} %get-tuple-element.22), channel_id=1, source_target_pairs={{0,0},{32,128},{64,256},{96,384},{128,32},{160,160},{192,288},{224... | collective-permute-start | bytes 1191944 | tf_op jit(solution)/shard_map/ppermute | solution.py:303
  112.4 24.4 %all-to-all-start.3 = ((f32[32,1,128]{2,1,0:T(1,128)}), f32[32,1,128]{2,1,0:T(1,128)S(1)}, u32[]{:S(2)}, u32[]{:S(2)}) async-start(f32[32,1,128]{2,1,0:T(1,128)} %get-tuple-element.23), calls=%async_computation.3 | async-start | bytes 32768 | tf_op jit(solution)/shard_map/all_to_all | solution.py:304

commit v6 on v4

--- a/solution.py
+++ b/solution.py
@@ -54,26 +54,17 @@
     return both[:BS] + both[BS:] + dot(tall[:BS], lo)
 
 
-def pack_kernel(pos, g, keep, give):
-    c = pos[1]
-    for out, core in ((keep, c), (give, 1 - c)):
+def pack_kernel(g, out):
+    for core in range(NC):
         for m in range(4):
             for w in range(4):
-                start = pl.multiple_of((2 * (4 * w + m) + core) * BS, BS)
-                out[0, 4 * m + w] = g[:, pl.ds(start, BS)]
+                start = (2 * (4 * w + m) + core) * BS
+                out[0, core, 4 * m + w] = g[:, start : start + BS]
 
 
 def by_place(pos, spread, body):
-    mine, other = spread.at[:, 0], spread.at[:, 1]
     for p in range(4):
-        for c in range(2):
-
-            @pl.when((pos[0] == p) & (pos[1] == c))
-            def _(p=p, c=c):
-                if c == 0:
-                    body(p, mine, other)
-                else:
-                    body(p, other, mine)
+        pl.when(pos[0] == p)(functools.partial(body, p, spread.at[:, 0], spread.at[:, 1]))
 
 
 def exchange_kernel(pos, spread, a, b):
@@ -240,7 +231,7 @@
 
 def per_device(pseudo_grads, outer_params, momentum, clip_level, block_picks, cutoffs):
     z = lax.axis_index("z")
-    pos = jnp.stack([z % 4, lax.axis_index("c")]).astype(jnp.int32)
+    pos = (z % 4).astype(jnp.int32).reshape(1)
     hi, lo = table_parts()
     fwd_wide = jnp.asarray(np.concatenate([hi.T, lo.T], axis=1))
     inv_wide = jnp.asarray(np.concatenate([hi, lo], axis=1))
@@ -249,28 +240,29 @@
     swap = [(NY * i + j, NX * j + i) for i in range(NX) for j in range(NY)]
     shape = jax.ShapeDtypeStruct
 
-    hit = block_picks[:, 0, :, :, None] == jnp.arange(BPO, dtype=jnp.int32)
-    cut = jnp.max(jnp.where(hit, cutoffs[:, 0, :, :, None], -1), axis=2)
-    cut = cut.transpose(1, 2, 0).reshape(NY, 4, 1, BPO)
-    cut = jnp.broadcast_to(cut, (NY, 4, 4, BPO)).reshape(NY * NZ, 1, BPO)
+    picks, cuts = (
+        lax.dynamic_index_in_dim(v[:, 0], lax.axis_index("x"), 1, keepdims=False) for v in (block_picks, cutoffs)
+    )
+    hit = picks[:, :, None] == jnp.arange(BPO, dtype=jnp.int32)
+    cut = jnp.max(jnp.where(hit, cuts[:, :, None], -1), axis=1)
+    cut = jnp.broadcast_to(cut.T.reshape(4, 1, BPO), (4, 4, BPO)).reshape(NZ, 1, BPO)
     cut = jnp.pad(cut, ((0, 0), (0, 0), (0, BS - BPO)))
-    cut = lax.all_to_all(cut, ("y", "z"), 0, 0, tiled=True)
-    cut = lax.dynamic_slice_in_dim(cut[:, 0], lax.axis_index("x") * NZ, NZ, 0)
-
-    part = pl.BlockSpec((1, NZ, rows, BS), lambda j: (j, 0, 0, 0))
-    keep, give = pl.pallas_call(
+    cut = lax.all_to_all(cut, "z", 0, 0, tiled=True)[:, 0]
+
+    chip = pl.pallas_call(
         pack_kernel,
-        out_shape=[shape((NY, NZ, rows, BS), BF16)] * 2,
+        out_shape=shape((NY, NC, NZ, rows, BS), BF16),
         grid=(NY,),
-        in_specs=[SMEM, pl.BlockSpec((None, rows, FF // NY), lambda j: (0, 0, j))],
-        out_specs=[part, part],
+        in_specs=[pl.BlockSpec((None, rows, FF // NY), lambda j: (0, 0, j))],
+        out_specs=pl.BlockSpec((1, NC, NZ, rows, BS), lambda j: (j, 0, 0, 0, 0)),
         compiler_params=BIG,
         name="pack",
-    )(pos, pseudo_grads)
-    got = lax.ppermute(give, "c", [(0, 1), (1, 0)])
-    chip = jnp.stack([keep, got], axis=1)
+    )(pseudo_grads)
     chip, cut = lax.optimization_barrier((chip, cut))
-    spread = lax.all_to_all(chip, "x", 0, 0, tiled=True)
+    cut = lax.ppermute(cut, ("x", "y"), swap)
+    chip = lax.all_to_all(chip.reshape(NY * NC, NZ, rows, BS), ("x", "c"), 0, 0, tiled=True)
+    spread = chip.reshape(NX, NC, NZ, rows, BS)
+    spread, cut = lax.optimization_barrier((spread, cut))
 
     a, b = call(
         exchange_kernel,

time: 141 us -> 137 us (0.972)
  the two profiles are of different devices: /device:TPU:39 before, /device:TPU:1 now
where the time goes in v6:
time: 137 us; the launch traced here: 136 us
  waiting for transfers between devices  46.2 us (34%)
  starting transfers between devices  41.6 us (30%)
  blocking collectives  35.3 us (26%)
  Pallas kernels  8.7 us (6%)
  local copies, waits for them, and re-layouts  3.14 us (2%)
  between operations  1.43 us (1%)
    all_to_all x1, blocking collectives, per_device(): coded = lax.all_to_all(coded, 'z', 0, 0, tiled=True)  35.3 us
    all_to_all x1, waiting for transfers between devices, per_device(): lax.all_to_all(chip.reshape(NY * NC, NZ, rows, BS), ('x', 'c'), 0, 0, til...  19.9 us
    all_to_all x1, starting transfers between devices, per_device(): cut = lax.all_to_all(cut, 'z', 0, 0, tiled=True)[:, 0]  15.7 us
    all_to_all x1, starting transfers between devices, per_device(): norm = lax.all_to_all(norm, ('x', 'y', 'c'), 0, 0, tiled=True)  13.6 us
    all_to_all x1, waiting for transfers between devices, per_device(): norm = lax.all_to_all(norm, ('x', 'y', 'c'), 0, 0, tiled=True)  10.2 us
    ppermute x1, waiting for transfers between devices, per_device(): a = lax.ppermute(a, 'z', pair_a)  8.18 us
    all_to_all x1, waiting for transfers between devices, per_device(): cut = lax.all_to_all(cut, 'z', 0, 0, tiled=True)[:, 0]  7.9 us
    all_to_all x1, starting transfers between devices, per_device(): lax.all_to_all(chip.reshape(NY * NC, NZ, rows, BS), ('x', 'c'), 0, 0, til...  6.38 us
  transfers between devices with their start and end apart: 7, of which 4 were waited for; matrix products, arithmetic and copies ran while one was open for 0% of the time, Pallas kernels for 1%

profile of v6, /device:TPU:1, one launch (start us, length us, event | category | flops | bytes accessed | tf_op | source)
XLA Modules:
  0.0 136.3 jit_solution(5907616736093945390)
XLA Ops:
  0.6 0.7 constant_dynamic-slice_fusion
  1.4 0.1 copy.11
  1.5 0.1 copy.12
  1.5 0.1 select_reduce_fusion
  1.6 0.1 copy.13
  1.7 0.1 broadcast_in_dim.27
  1.8 0.6 pad.4
  2.4 15.7 %all-to-all-start = ((s32[16,1,128]{2,1,0:T(1,128)}), s32[16,1,128]{2,1,0:T(1,128)S(1)}, u32[]{:S(2)}, u32[]{:S(2)}) async-start(s32[16,1,128]{2,1,0:T(1,128)} %pad.4), calls=%async_computation | async-start | bytes 16384 | tf_op jit(solution)/shard_map/all_to_all | solution.py:250
  18.2 0.0 copy-start
  18.2 1.4 %copy-done = bf16[1,48,16384]{2,1,0:T(8,128)(2,1)S(1)} copy-done((bf16[1,48,16384]{2,1,0:T(8,128)(2,1)S(1)}, bf16[1,48,16384]{2,1,0:T(8,128)(2,1)}, u32[]{:S(2)}) %copy-start) | copy-done | bytes 1572888
  19.6 1.9 %pack.1 = bf16[4,2,16,48,128]{4,3,2,1,0:T(8,128)(2,1)} custom-call(bf16[1,48,16384]{2,1,0:T(8,128)(2,1)S(1)} %copy-done), custom_call_target="tpu_custom_call" | custom-call | tf_op jit(solution)/shard_map/pack/pallas_call | solution.py:252
  21.5 7.9 %all-to-all-done = s32[16,1,128]{2,1,0:T(1,128)S(1)} async-done(((s32[16,1,128]{2,1,0:T(1,128)}), s32[16,1,128]{2,1,0:T(1,128)S(1)}, u32[]{:S(2)}, u32[]{:S(2)}) %all-to-all-start) | async-done | bytes 8224 | tf_op jit(solution)/shard_map/all_to_all | solution.py:250
  29.4 6.4 %all-to-all-start.1 = ((bf16[8,16,48,128]{3,2,1,0:T(8,128)(2,1)}), bf16[8,16,48,128]{3,2,1,0:T(8,128)(2,1)S(1)}, u32[]{:S(2)}, u32[]{:S(2)}) async-start(bf16[8,16,48,128]{3,2,1,0:T(8,128)(2,1)} %bitcast.6), calls=%async_computation.1 | async-start | bytes 3145728 | tf_op jit(solution)/shard_map/all_to_all | solution.py:263
  35.8 0.0 copy-start.3
  35.8 0.0 copy-start.5
  35.8 0.8 collective-permute-start
  36.6 0.0 collective-permute-done.cut
  36.6 19.9 %all-to-all-done.1 = bf16[8,16,48,128]{3,2,1,0:T(8,128)(2,1)S(1)} async-done(((bf16[8,16,48,128]{3,2,1,0:T(8,128)(2,1)}), bf16[8,16,48,128]{3,2,1,0:T(8,128)(2,1)S(1)}, u32[]{:S(2)}, u32[]{:S(2)}) %all-to-all-start.1) | async-done | bytes 1572896 | tf_op jit(solution)/shard_map/all_to_all | solution.py:263
  56.6 0.7 collective-permute-start.2
  57.3 3.7 %collective-permute-start.1 = (bf16[4,4,96,128]{3,2,1,0:T(8,128)(2,1)S(1)}, bf16[4,4,96,128]{3,2,1,0:T(8,128)(2,1)S(1)}, u32[]{:S(2)}, u32[]{:S(2)}) collective-permute-start(bf16[4,4,96,128]{3,2,1,0:T(8,128)(2,1)S(1)} %get-tuple-element.14), channel_id=1, source_target_pairs={{0,2},{2,0},{4,6},{6,4},{8,10},{10,8},{12,14},{14,12},{16,18},{18,... | collective-permute-start | bytes 1179656 | tf_op jit(solution)/shard_map/ppermute | solution.py:277
  61.0 8.2 %collective-permute-done.1.a = bf16[4,4,96,128]{3,2,1,0:T(8,128)(2,1)S(1)} collective-permute-done((bf16[4,4,96,128]{3,2,1,0:T(8,128)(2,1)S(1)}, bf16[4,4,96,128]{3,2,1,0:T(8,128)(2,1)S(1)}, u32[]{:S(2)}, u32[]{:S(2)}) %collective-permute-start.1) | collective-permute-done | bytes 393248 | tf_op jit(solution)/shard_map/ppermute | solution.py:277
  69.1 0.0 collective-permute-done.2.b
  69.2 0.0 copy-done.3
  69.2 0.0 copy-done.5
  69.2 2.9 %forward.1 = s16[16,144,128]{2,1,0:T(8,128)(2,1)S(1)} custom-call(s32[1]{0:T(128)} %bitcast.pos, s32[16,128]{1,0:T(8,128)S(1)} %collective-permute-done.cut, bf16[4,2,16,48,128]{4,3,2,1,0:T(8,128)(2,1)S(1)} %bitcast.9, bf16[4,4,96,128]{3,2,1,0:T(8,128)(2,1)S(1)} %collective-permute-done.1.a, bf16[4,8,64,128]{3,2,1,0:T(8,128)(2,1)S(1)} %collective-permute-done.2.b, ...), custom_call_target="tpu_custom_call" | custom-call | tf_op jit(solution)/shard_map/forward/pallas_call | solution.py:221
  72.0 0.0 copy-start.1
  72.0 0.0 copy-start.2
  72.0 0.0 copy-start.4
  72.1 35.3 %all_to_all.20.z = s16[16,144,128]{2,1,0:T(8,128)(2,1)S(1)} all-to-all(s16[16,144,128]{2,1,0:T(8,128)(2,1)S(1)} %forward.1), channel_id=1, replica_groups=mesh['x'=4,'y'=4,'z'=16,'c'=2] {'z'}, dimensions={0} | all-to-all | bytes 1179648 | tf_op jit(solution)/shard_map/all_to_all | solution.py:287
  107.3 0.7 compact.1
  108.0 0.7 collective-permute-start.3
  108.7 13.6 %all-to-all-start.3 = ((f32[32,1,128]{2,1,0:T(1,128)}), f32[32,1,128]{2,1,0:T(1,128)S(1)}, u32[]{:S(2)}, u32[]{:S(2)}) async-start(f32[32,1,128]{2,1,0:T(1,128)} %get-tuple-element.17), calls=%async_computation.3 | async-start | bytes 32768 | tf_op jit(solution)/shard_map/all_to_all | solution.py:295
  122.9 10.2 %all-to-all-done.3.norm = f32[32,1,128]{2,1,0:T(1,128)S(1)} async-done(((f32[32,1,128]{2,1,0:T(1,128)}), f32[32,1,128]{2,1,0:T(1,128)S(1)}, u32[]{:S(2)}, u32[]{:S(2)}) %all-to-all-start.3) | async-done | bytes 16416 | tf_op jit(solution)/shard_map/all_to_all | solution.py:295
  133.1 0.0 collective-permute-done.3.code.tail
  133.1 0.0 copy-done.1
  133.1 0.0 copy-done.2
  133.1 0.0 copy-done.4
  133.1 3.2 %update.1 = (f32[1536,128]{1,0:T(8,128)}, f32[1536,128]{1,0:T(8,128)}) custom-call(s16[1552,128]{1,0:T(8,128)(2,1)S(1)} %collective-permute-done.3.code.tail, s16[1552,128]{1,0:T(8,128)(2,1)S(1)} %collective-permute-done.3.code.tail, f32[32,1,128]{2,1,0:T(1,128)S(1)} %all-to-all-done.3.norm, f32[1]{0:T(128)S(6)} %copy.14.clip, f32[1536,128]{1,0:T(8,128)S(1)} %copy-done.1, ...), custom_call_target="tpu_custom_call" | custom-call | tf_op jit(solution)/shard_map/update/pallas_call | solution.py:298
  (2 shorter events, 0.1 us)
Async XLA Ops:
  2.4 27.0 %all-to-all-start = ((s32[16,1,128]{2,1,0:T(1,128)}), s32[16,1,128]{2,1,0:T(1,128)S(1)}, u32[]{:S(2)}, u32[]{:S(2)}) async-start(s32[16,1,128]{2,1,0:T(1,128)} %pad.4), calls=%async_computation | async-start | bytes 16384 | tf_op jit(solution)/shard_map/all_to_all | solution.py:250
  18.2 1.4 %copy-start = (bf16[1,48,16384]{2,1,0:T(8,128)(2,1)S(1)}, bf16[1,48,16384]{2,1,0:T(8,128)(2,1)}, u32[]{:S(2)}) copy-start(bf16[1,48,16384]{2,1,0:T(8,128)(2,1)} %g.1) | copy-start | bytes 4718596
  29.4 27.1 %all-to-all-start.1 = ((bf16[8,16,48,128]{3,2,1,0:T(8,128)(2,1)}), bf16[8,16,48,128]{3,2,1,0:T(8,128)(2,1)S(1)}, u32[]{:S(2)}, u32[]{:S(2)}) async-start(bf16[8,16,48,128]{3,2,1,0:T(8,128)(2,1)} %bitcast.6), calls=%async_computation.1 | async-start | bytes 3145728 | tf_op jit(solution)/shard_map/all_to_all | solution.py:263
  35.8 33.4 %copy-start.3 = (bf16[128,256]{1,0:T(8,128)(2,1)S(1)}, bf16[128,256]{1,0:T(8,128)(2,1)}, u32[]{:S(2)}) copy-start(bf16[128,256]{1,0:T(8,128)(2,1)} %constant.45.clone.left.wide) | copy-start | bytes 196612
  35.8 33.4 %copy-start.5 = (bf16[128,256]{1,0:T(8,128)(2,1)S(1)}, bf16[128,256]{1,0:T(8,128)(2,1)}, u32[]{:S(2)}) copy-start(bf16[128,256]{1,0:T(8,128)(2,1)} %constant.44.clone.wide) | copy-start | bytes 196612
  35.8 0.8 collective-permute-start
  56.6 12.6 %collective-permute-start.2 = (bf16[4,8,64,128]{3,2,1,0:T(8,128)(2,1)S(1)}, bf16[4,8,64,128]{3,2,1,0:T(8,128)(2,1)S(1)}, u32[]{:S(2)}, u32[]{:S(2)}) collective-permute-start(bf16[4,8,64,128]{3,2,1,0:T(8,128)(2,1)S(1)} %get-tuple-element.15), channel_id=1, source_target_pairs={{2,4},{4,2},{10,12},{12,10},{18,20},{20,18},{26,28},{28,26},{3,5},... | collective-permute-start | bytes 1572872 | tf_op jit(solution)/shard_map/ppermute | solution.py:278
  57.3 11.9 %collective-permute-start.1 = (bf16[4,4,96,128]{3,2,1,0:T(8,128)(2,1)S(1)}, bf16[4,4,96,128]{3,2,1,0:T(8,128)(2,1)S(1)}, u32[]{:S(2)}, u32[]{:S(2)}) collective-permute-start(bf16[4,4,96,128]{3,2,1,0:T(8,128)(2,1)S(1)} %get-tuple-element.14), channel_id=1, source_target_pairs={{0,2},{2,0},{4,6},{6,4},{8,10},{10,8},{12,14},{14,12},{16,18},{18,... | collective-permute-start | bytes 1179656 | tf_op jit(solution)/shard_map/ppermute | solution.py:277
  72.0 61.1 %copy-start.1 = (f32[1536,128]{1,0:T(8,128)S(1)}, f32[1536,128]{1,0:T(8,128)}, u32[]{:S(2)}) copy-start(f32[1536,128]{1,0:T(8,128)} %params.1) | copy-start | bytes 2359300
  72.0 61.1 %copy-start.2 = (f32[1536,128]{1,0:T(8,128)S(1)}, f32[1536,128]{1,0:T(8,128)}, u32[]{:S(2)}) copy-start(f32[1536,128]{1,0:T(8,128)} %mom.1) | copy-start | bytes 2359300
  72.0 61.0 %copy-start.4 = (bf16[256,128]{1,0:T(8,128)(2,1)S(1)}, bf16[256,128]{1,0:T(8,128)(2,1)}, u32[]{:S(2)}) copy-start(bf16[256,128]{1,0:T(8,128)(2,1)} %constant.46.clone.tall) | copy-start | bytes 196612
  108.0 25.1 %collective-permute-start.3 = (s16[1552,128]{1,0:T(8,128)(2,1)S(1)}, s16[1552,128]{1,0:T(8,128)(2,1)S(1)}, u32[]{:S(2)}, u32[]{:S(2)}) collective-permute-start(s16[1552,128]{1,0:T(8,128)(2,1)S(1)} %get-tuple-element.16), channel_id=1, source_target_pairs={{0,0},{32,128},{64,256},{96,384},{128,32},{160,160},{192,288},{224... | collective-permute-start | bytes 1191944 | tf_op jit(solution)/shard_map/ppermute | solution.py:294
  108.7 24.4 %all-to-all-start.3 = ((f32[32,1,128]{2,1,0:T(1,128)}), f32[32,1,128]{2,1,0:T(1,128)S(1)}, u32[]{:S(2)}, u32[]{:S(2)}) async-start(f32[32,1,128]{2,1,0:T(1,128)} %get-tuple-element.17), calls=%async_computation.3 | async-start | bytes 32768 | tf_op jit(solution)/shard_map/all_to_all | solution.py:295

commit v7 on v6

--- a/solution.py
+++ b/solution.py
@@ -54,82 +54,95 @@
     return both[:BS] + both[BS:] + dot(tall[:BS], lo)
 
 
-def pack_kernel(g, out):
-    for core in range(NC):
-        for m in range(4):
-            for w in range(4):
-                start = (2 * (4 * w + m) + core) * BS
-                out[0, core, 4 * m + w] = g[:, start : start + BS]
-
-
-def by_place(pos, spread, body):
+def pack_kernel(pos, g, *outs):
+    c, x = pos[1], pos[2]
+    for s in range(NX):
+        for out, core in ((outs[s], c), (outs[NX + s], 1 - c)):
+            base = NZ * NC * ((x + s) % 4) + core
+            for m in range(4):
+                for w in range(4):
+                    start = pl.multiple_of((base + 2 * (4 * w + m)) * BS, BS)
+                    out[4 * m + w] = g[0, :, pl.ds(start, BS)]
+
+
+def by_place(pos, rows, body):
     for p in range(4):
-        pl.when(pos[0] == p)(functools.partial(body, p, spread.at[:, 0], spread.at[:, 1]))
-
-
-def exchange_kernel(pos, spread, a, b):
-    def body(p, lo, hi):
-        if p in (0, 3):
-            s = slice(0, 4) if p == 0 else slice(12, 16)
-            a[:, :, 0:48] = lo[:, s]
-            a[:, :, 48:96] = hi[:, s]
-            return
-        for k in range(3):
+        for c in range(2):
+            mine, other = rows[:NX], rows[NX:]
+            pair = (mine, other) if c == 0 else (other, mine)
+            pl.when((pos[0] == p) & (pos[1] == c))(functools.partial(body, p, *pair))
+
+
+def exchange_kernel(pos, *refs):
+    a, b = refs[-2:]
+
+    def body(p, los, his):
+        for r in range(NX):
+            lo, hi = los[r], his[r]
+            if p in (0, 3):
+                s = slice(0, 4) if p == 0 else slice(12, 16)
+                a[r, :, 0:48] = lo[s]
+                a[r, :, 48:96] = hi[s]
+                continue
+            for k in range(3):
+                if p == 1:
+                    a[r, :, 32 * k : 32 * k + 32] = lo[4 * k + 4 : 4 * k + 8, 0:32]
+                else:
+                    a[r, :, 32 * k : 32 * k + 32] = hi[4 * k : 4 * k + 4, 16:48]
             if p == 1:
-                a[:, :, 32 * k : 32 * k + 32] = lo[:, 4 * k + 4 : 4 * k + 8, 0:32]
+                b[r, :, 0:16] = lo[0:8, 32:48]
+                b[r, :, 16:64] = hi[0:8]
             else:
-                a[:, :, 32 * k : 32 * k + 32] = hi[:, 4 * k : 4 * k + 4, 16:48]
-        if p == 1:
-            b[:, :, 0:16] = lo[:, 0:8, 32:48]
-            b[:, :, 16:64] = hi[:, 0:8]
-        else:
-            b[:, :, 0:48] = lo[:, 8:16]
-            b[:, :, 48:64] = hi[:, 8:16, 0:16]
-
-    by_place(pos, spread, body)
-
-
-def assemble(pos, spread, a, b, whole):
-    def place(p, k, lo, hi, x):
+                b[r, :, 0:48] = lo[8:16]
+                b[r, :, 48:64] = hi[8:16, 0:16]
+
+    by_place(pos, refs[:-2], body)
+
+
+def assemble(pos, rows, a, b, whole):
+    def place(p, k, lo, hi, r):
         m = k + (k >= p)
+        d = slice(4 * k, 4 * k + 4)
         s = slice(4 * m, 4 * m + 4)
         third = slice(32 * k, 32 * k + 32)
         if p == 0:
-            x[:, :, 0:48] = lo[:, s]
-            x[:, :, 48:96] = hi[:, s]
-            x[:, :, 96:128] = a[:, :, third]
+            whole[r, d, 0:48] = lo[s]
+            whole[r, d, 48:96] = hi[s]
+            whole[r, d, 96:128] = a[r, :, third]
         elif p == 3:
-            x[:, :, 0:32] = a[:, :, third]
-            x[:, :, 32:80] = lo[:, s]
-            x[:, :, 80:128] = hi[:, s]
+            whole[r, d, 0:32] = a[r, :, third]
+            whole[r, d, 32:80] = lo[s]
+            whole[r, d, 80:128] = hi[s]
         elif p == 1 and m == 0:
-            x[:, :, 0:96] = a[:, :, :]
-            x[:, :, 96:128] = lo[:, s, 0:32]
+            whole[r, d, 0:96] = a[r]
+            whole[r, d, 96:128] = lo[s, 0:32]
         elif p == 1:
-            x[:, :, 0:16] = lo[:, s, 32:48]
-            x[:, :, 16:64] = hi[:, s]
-            x[:, :, 64:128] = b[:, 4 * (m - 2) : 4 * (m - 2) + 4]
+            whole[r, d, 0:16] = lo[s, 32:48]
+            whole[r, d, 16:64] = hi[s]
+            whole[r, d, 64:128] = b[r, 4 * (m - 2) : 4 * (m - 2) + 4]
         elif m == 3:
-            x[:, :, 0:32] = hi[:, s, 16:48]
-            x[:, :, 32:128] = a[:, :, :]
+            whole[r, d, 0:32] = hi[s, 16:48]
+            whole[r, d, 32:128] = a[r]
         else:
-            x[:, :, 0:64] = b[:, s]
-            x[:, :, 64:112] = lo[:, s]
-            x[:, :, 112:128] = hi[:, s, 0:16]
-
-    def body(p, lo, hi):
+            whole[r, d, 0:64] = b[r, s]
+            whole[r, d, 64:112] = lo[s]
+            whole[r, d, 112:128] = hi[s, 0:16]
+
+    def body(p, los, his):
         for k in range(3):
-            place(p, k, lo, hi, whole.at[:, 4 * k : 4 * k + 4])
-
-    by_place(pos, spread, body)
+            for r in range(NX):
+                place(p, k, los[r], his[r], r)
+
+    by_place(pos, rows, body)
 
 
 def exponent(size):
     return jnp.clip(jnp.floor(jnp.log2(jnp.maximum(size, F32(1e-30)))) + 1.0, -100.0, 200.0)
 
 
-def forward_kernel(pos, cut, spread, a, b, left, wide, out, x, exps):
-    assemble(pos, spread, a, b, x)
+def forward_kernel(pos, cut, *refs):
+    a, b, left, wide, out, x, exps = refs[2 * NX :]
+    assemble(pos, refs[: 2 * NX], a, b, x)
     p = pos[0]
     freq = lax.broadcasted_iota(jnp.int32, (BS, BS), 0) + lax.broadcasted_iota(jnp.int32, (BS, BS), 1)
     row = lax.broadcasted_iota(jnp.int32, (TAIL, BS), 0)
@@ -154,7 +167,7 @@
                 )
                 both = dot(left[...], pairs)
                 coef = both[:, :BS] + both[:, BS:]
-                total += jnp.where(freq <= cut[4 * w + m, 4 * blk + r], coef, 0.0)
+                total += jnp.where(freq <= cut[4 * w + m, 4 * blk + (pos[2] + 4 - r) % 4], coef, 0.0)
             e = exponent(jnp.max(jnp.abs(total), axis=0, keepdims=True))
             code = jnp.clip(jnp.floor(total * jnp.exp2(15.0 - e) + 0.5), -32767.0, 32767.0)
             out[4 * w + m, 0:BS] = code.astype(jnp.int32).astype(jnp.int16)
@@ -231,7 +244,7 @@
 
 def per_device(pseudo_grads, outer_params, momentum, clip_level, block_picks, cutoffs):
     z = lax.axis_index("z")
-    pos = (z % 4).astype(jnp.int32).reshape(1)
+    pos = jnp.stack([z % 4, lax.axis_index("c"), lax.axis_index("x")]).astype(jnp.int32)
     hi, lo = table_parts()
     fwd_wide = jnp.asarray(np.concatenate([hi.T, lo.T], axis=1))
     inv_wide = jnp.asarray(np.concatenate([hi, lo], axis=1))
@@ -247,27 +260,26 @@
     cut = jnp.max(jnp.where(hit, cuts[:, :, None], -1), axis=1)
     cut = jnp.broadcast_to(cut.T.reshape(4, 1, BPO), (4, 4, BPO)).reshape(NZ, 1, BPO)
     cut = jnp.pad(cut, ((0, 0), (0, 0), (0, BS - BPO)))
+    cut, pseudo_grads = lax.optimization_barrier((cut, pseudo_grads))
     cut = lax.all_to_all(cut, "z", 0, 0, tiled=True)[:, 0]
 
-    chip = pl.pallas_call(
-        pack_kernel,
-        out_shape=shape((NY, NC, NZ, rows, BS), BF16),
-        grid=(NY,),
-        in_specs=[pl.BlockSpec((None, rows, FF // NY), lambda j: (0, 0, j))],
-        out_specs=pl.BlockSpec((1, NC, NZ, rows, BS), lambda j: (j, 0, 0, 0, 0)),
-        compiler_params=BIG,
-        name="pack",
-    )(pseudo_grads)
-    chip, cut = lax.optimization_barrier((chip, cut))
+    packed = call(
+        pack_kernel, [shape((NZ, rows, BS), BF16)] * (2 * NX), (pos, pseudo_grads), "pack"
+    )
+    spread = list(packed)
+    for n in (NX + 2, 2, NX + 1, NX + 3, 1, 3, NX):
+        flip, step = divmod(n, NX)
+        pairs = [
+            (NC * i + c, NC * ((i + step) % NX) + (c ^ flip)) for i in range(NX) for c in range(NC)
+        ]
+        spread[n] = lax.ppermute(packed[n], ("x", "c"), pairs)
+    *spread, cut = lax.optimization_barrier((*spread, cut))
     cut = lax.ppermute(cut, ("x", "y"), swap)
-    chip = lax.all_to_all(chip.reshape(NY * NC, NZ, rows, BS), ("x", "c"), 0, 0, tiled=True)
-    spread = chip.reshape(NX, NC, NZ, rows, BS)
-    spread, cut = lax.optimization_barrier((spread, cut))
 
     a, b = call(
         exchange_kernel,
         (shape((NX, 4, 96, BS), BF16), shape((NX, 8, 64, BS), BF16)),
-        (pos, spread),
+        (pos, *spread),
         "exchange",
     )
     pair_a, pair_b = [], []
@@ -280,7 +292,7 @@
     coded = call(
         forward_kernel,
         shape((NZ, BS + TAIL, BS), jnp.int16),
-        (pos, cut, spread, a, b, inv_wide, fwd_wide),
+        (pos, cut, *spread, a, b, inv_wide, fwd_wide),
         "forward",
         [pltpu.VMEM((NX, BPO, BS, BS), BF16), pltpu.VMEM((NZ, BS), F32)],
     )

time: 137 us -> 135 us (0.985); the launches traced: 136 us -> 133 us
  waiting for transfers between devices: 46.2 us -> 15.4 us
  blocking collectives: 35.3 us -> 56.2 us
  starting transfers between devices: 41.6 us -> 48.2 us
    ppermute x0 -> x7, starting transfers between devices: none -> 28.4 us  [per_device(): spread[n] = lax.ppermute(packed[n], ('x', 'c'), pairs)]
    all_to_all x2 -> x0, waiting for transfers between devices: 27.8 us -> none  [the longest x1 19.9 us: per_device(): lax.all_to_all(chip.reshape(NY * NC, NZ, rows, BS), ('x', 'c'), 0, 0, til...]
    all_to_all x2 -> x0, starting transfers between devices: 22.1 us -> none  [the longest x1 15.7 us: per_device(): cut = lax.all_to_all(cut, 'z', 0, 0, tiled=True)[:, 0]]
    all_to_all x0 -> x1, blocking collectives: none -> 21.2 us  [per_device(): cut = lax.all_to_all(cut, 'z', 0, 0, tiled=True)[:, 0]]
    pallas_call x3 -> x4, Pallas kernels: 3.55 us -> 5.7 us  [call(): pl.pallas_call(kernel, out_shape=out_shape, in_specs=[SMEM if i.dtype ==...]
    pallas_call x1 -> x0, Pallas kernels: 1.92 us -> none  [per_device(): pl.pallas_call(pack_kernel, out_shape=shape((NY, NC, NZ, rows, BS), BF16)...]
    all_to_all x1, waiting for transfers between devices: 10.2 us -> 8.32 us  [per_device(): norm = lax.all_to_all(norm, ('x', 'y', 'c'), 0, 0, tiled=True)]
  transfers between devices with their start and end apart: 7 -> 12, of which waited for: 4 -> 2; matrix products, arithmetic and copies ran while one was open for 0% -> 0% of each run, Pallas kernels for 1% -> 0%
where the time goes in v7:
time: 135 us; the launch traced here: 133 us
  blocking collectives  56.2 us (42%)
  starting transfers between devices  48.2 us (36%)
  waiting for transfers between devices  15.4 us (11%)
  Pallas kernels  8.93 us (7%)
  local copies, waits for them, and re-layouts  2.54 us (2%)
  between operations  1.52 us (1%)
    all_to_all x1, blocking collectives, per_device(): coded = lax.all_to_all(coded, 'z', 0, 0, tiled=True)  35 us
    ppermute x7, starting transfers between devices, per_device(): spread[n] = lax.ppermute(packed[n], ('x', 'c'), pairs)  28.4 us
    all_to_all x1, blocking collectives, per_device(): cut = lax.all_to_all(cut, 'z', 0, 0, tiled=True)[:, 0]  21.2 us
    all_to_all x1, starting transfers between devices, per_device(): norm = lax.all_to_all(norm, ('x', 'y', 'c'), 0, 0, tiled=True)  14.1 us
    all_to_all x1, waiting for transfers between devices, per_device(): norm = lax.all_to_all(norm, ('x', 'y', 'c'), 0, 0, tiled=True)  8.32 us
    ppermute x1, waiting for transfers between devices, per_device(): a = lax.ppermute(a, 'z', pair_a)  7.01 us
    pallas_call x4, Pallas kernels, call(): pl.pallas_call(kernel, out_shape=out_shape, in_specs=[SMEM if i.dtype ==...  5.7 us
    ppermute x1, starting transfers between devices, per_device(): a = lax.ppermute(a, 'z', pair_a)  3.68 us
  transfers between devices with their start and end apart: 12, of which 2 were waited for; matrix products, arithmetic and copies ran while one was open for 0% of the time, Pallas kernels for 0%

profile of v7, /device:TPU:1, one launch (start us, length us, event | category | flops | bytes accessed | tf_op | source)
XLA Modules:
  0.0 132.9 jit_solution(6686381236875744824)
XLA Ops:
  0.6 0.7 constant_dynamic-slice_fusion
  1.4 0.1 copy.11
  1.5 0.1 copy.12
  1.6 0.1 select_reduce_fusion
  1.6 0.1 copy.13
  1.7 0.1 broadcast_in_dim.27
  1.9 0.1 pad_add_fusion.pos
  1.9 0.0 copy-start
  1.9 1.4 %copy-done = bf16[1,48,16384]{2,1,0:T(8,128)(2,1)S(1)} copy-done((bf16[1,48,16384]{2,1,0:T(8,128)(2,1)S(1)}, bf16[1,48,16384]{2,1,0:T(8,128)(2,1)}, u32[]{:S(2)}) %copy-start) | copy-done | bytes 1572888
  3.3 0.0 copy-start.3
  3.3 0.0 copy-start.5
  3.4 1.0 pack.1
  4.3 3.9 %collective-permute-start = (bf16[16,48,128]{2,1,0:T(8,128)(2,1)S(1)}, bf16[16,48,128]{2,1,0:T(8,128)(2,1)S(1)}, u32[]{:S(2)}, u32[]{:S(2)}) collective-permute-start(bf16[16,48,128]{2,1,0:T(8,128)(2,1)S(1)} %get-tuple-element.27), channel_id=1, source_target_pairs={{0,128},{1,129},{128,256},{129,257},{256,384},{257,385},{384,0},{3... | collective-permute-start | bytes 589832 | tf_op jit(solution)/shard_map/ppermute | solution.py:275
  8.3 4.4 %collective-permute-start.1 = (bf16[16,48,128]{2,1,0:T(8,128)(2,1)S(1)}, bf16[16,48,128]{2,1,0:T(8,128)(2,1)S(1)}, u32[]{:S(2)}, u32[]{:S(2)}) collective-permute-start(bf16[16,48,128]{2,1,0:T(8,128)(2,1)S(1)} %get-tuple-element.28), channel_id=1, source_target_pairs={{0,256},{1,257},{128,384},{129,385},{256,0},{257,1},{384,128},{385... | collective-permute-start | bytes 589832 | tf_op jit(solution)/shard_map/ppermute | solution.py:275
  12.6 3.1 %collective-permute-start.2 = (bf16[16,48,128]{2,1,0:T(8,128)(2,1)S(1)}, bf16[16,48,128]{2,1,0:T(8,128)(2,1)S(1)}, u32[]{:S(2)}, u32[]{:S(2)}) collective-permute-start(bf16[16,48,128]{2,1,0:T(8,128)(2,1)S(1)} %get-tuple-element.29), channel_id=1, source_target_pairs={{0,384},{1,385},{128,0},{129,1},{256,128},{257,129},{384,256},{385... | collective-permute-start | bytes 589832 | tf_op jit(solution)/shard_map/ppermute | solution.py:275
  15.7 6.4 %collective-permute-start.3 = (bf16[16,48,128]{2,1,0:T(8,128)(2,1)S(1)}, bf16[16,48,128]{2,1,0:T(8,128)(2,1)S(1)}, u32[]{:S(2)}, u32[]{:S(2)}) collective-permute-start(bf16[16,48,128]{2,1,0:T(8,128)(2,1)S(1)} %get-tuple-element.30), channel_id=1, source_target_pairs={{0,1},{1,0},{128,129},{129,128},{256,257},{257,256},{384,385},{385... | collective-permute-start | bytes 589832 | tf_op jit(solution)/shard_map/ppermute | solution.py:275
  22.1 2.4 %collective-permute-start.4 = (bf16[16,48,128]{2,1,0:T(8,128)(2,1)S(1)}, bf16[16,48,128]{2,1,0:T(8,128)(2,1)S(1)}, u32[]{:S(2)}, u32[]{:S(2)}) collective-permute-start(bf16[16,48,128]{2,1,0:T(8,128)(2,1)S(1)} %get-tuple-element.31), channel_id=1, source_target_pairs={{0,129},{1,128},{128,257},{129,256},{256,385},{257,384},{384,1},{3... | collective-permute-start | bytes 589832 | tf_op jit(solution)/shard_map/ppermute | solution.py:275
  24.5 0.0 collective-permute-done.refs_1_
  24.5 4.0 %collective-permute-start.5 = (bf16[16,48,128]{2,1,0:T(8,128)(2,1)S(1)}, bf16[16,48,128]{2,1,0:T(8,128)(2,1)S(1)}, u32[]{:S(2)}, u32[]{:S(2)}) collective-permute-start(bf16[16,48,128]{2,1,0:T(8,128)(2,1)S(1)} %get-tuple-element.32), channel_id=1, source_target_pairs={{0,257},{1,256},{128,385},{129,384},{256,1},{257,0},{384,129},{385... | collective-permute-start | bytes 589832 | tf_op jit(solution)/shard_map/ppermute | solution.py:275
  28.5 0.0 collective-permute-done.1.refs_2_
  28.5 4.2 %collective-permute-start.6 = (bf16[16,48,128]{2,1,0:T(8,128)(2,1)S(1)}, bf16[16,48,128]{2,1,0:T(8,128)(2,1)S(1)}, u32[]{:S(2)}, u32[]{:S(2)}) collective-permute-start(bf16[16,48,128]{2,1,0:T(8,128)(2,1)S(1)} %get-tuple-element.33), channel_id=1, source_target_pairs={{0,385},{1,384},{128,1},{129,0},{256,129},{257,128},{384,257},{385... | collective-permute-start | bytes 589832 | tf_op jit(solution)/shard_map/ppermute | solution.py:275
  32.8 21.2 %all_to_all.15 = s32[16,1,128]{2,1,0:T(1,128)S(1)} all-to-all(s32[16,1,128]{2,1,0:T(1,128)S(1)} %pad.4), channel_id=1, replica_groups=mesh['x'=4,'y'=4,'z'=16,'c'=2] {'z'}, dimensions={0} | all-to-all | bytes 16384 | tf_op jit(solution)/shard_map/all_to_all | solution.py:264
  53.9 0.0 collective-permute-done.2.refs_3_
  53.9 0.0 collective-permute-done.3.refs_4_
  53.9 0.0 collective-permute-done.4.refs_5_
  53.9 0.0 collective-permute-done.5.refs_6_
  54.0 0.0 collective-permute-done.6.refs_7_
  54.0 0.6 exchange.1
  54.6 0.7 collective-permute-start.9
  55.3 3.7 %collective-permute-start.8 = (bf16[4,4,96,128]{3,2,1,0:T(8,128)(2,1)S(1)}, bf16[4,4,96,128]{3,2,1,0:T(8,128)(2,1)S(1)}, u32[]{:S(2)}, u32[]{:S(2)}) collective-permute-start(bf16[4,4,96,128]{3,2,1,0:T(8,128)(2,1)S(1)} %get-tuple-element.44), channel_id=1, source_target_pairs={{0,2},{2,0},{4,6},{6,4},{8,10},{10,8},{12,14},{14,12},{16,18},{18,... | collective-permute-start | bytes 1179656 | tf_op jit(solution)/shard_map/ppermute | solution.py:289
  59.0 0.7 collective-permute-start.7
  59.7 0.0 collective-permute-done.7.cut
  59.7 7.0 %collective-permute-done.8.refs_8_ = bf16[4,4,96,128]{3,2,1,0:T(8,128)(2,1)S(1)} collective-permute-done((bf16[4,4,96,128]{3,2,1,0:T(8,128)(2,1)S(1)}, bf16[4,4,96,128]{3,2,1,0:T(8,128)(2,1)S(1)}, u32[]{:S(2)}, u32[]{:S(2)}) %collective-permute-start.8) | collective-permute-done | bytes 393248 | tf_op jit(solution)/shard_map/ppermute | solution.py:289
  66.7 0.0 collective-permute-done.9.refs_9_
  66.7 0.0 copy-done.3
  66.7 0.0 copy-done.5
  66.7 2.9 %forward.1 = s16[16,144,128]{2,1,0:T(8,128)(2,1)S(1)} custom-call(s32[3]{0:T(128)S(1)} %pad_add_fusion.pos, s32[16,128]{1,0:T(8,128)S(1)} %collective-permute-done.7.cut, bf16[16,48,128]{2,1,0:T(8,128)(2,1)S(1)} %get-tuple-element.36.refs_0_, bf16[16,48,128]{2,1,0:T(8,128)(2,1)S(1)} %collective-permute-done.refs_1_, ...), custom_call_target="tpu_custom_call" | custom-call | tf_op jit(solution)/shard_map/forward/pallas_call | solution.py:234
  69.6 0.0 copy-start.1
  69.6 0.0 copy-start.2
  69.6 0.0 copy-start.4
  69.7 35.0 %all_to_all.16.z = s16[16,144,128]{2,1,0:T(8,128)(2,1)S(1)} all-to-all(s16[16,144,128]{2,1,0:T(8,128)(2,1)S(1)} %forward.1), channel_id=1, replica_groups=mesh['x'=4,'y'=4,'z'=16,'c'=2] {'z'}, dimensions={0} | all-to-all | bytes 1179648 | tf_op jit(solution)/shard_map/all_to_all | solution.py:299
  104.7 1.2 compact.1
  105.9 0.7 collective-permute-start.10
  106.6 14.1 %all-to-all-start.2 = ((f32[32,1,128]{2,1,0:T(1,128)}), f32[32,1,128]{2,1,0:T(1,128)S(1)}, u32[]{:S(2)}, u32[]{:S(2)}) async-start(f32[32,1,128]{2,1,0:T(1,128)} %get-tuple-element.47), calls=%async_computation.2 | async-start | bytes 32768 | tf_op jit(solution)/shard_map/all_to_all | solution.py:307
  121.4 8.3 %all-to-all-done.2.norm = f32[32,1,128]{2,1,0:T(1,128)S(1)} async-done(((f32[32,1,128]{2,1,0:T(1,128)}), f32[32,1,128]{2,1,0:T(1,128)S(1)}, u32[]{:S(2)}, u32[]{:S(2)}) %all-to-all-start.2) | async-done | bytes 16416 | tf_op jit(solution)/shard_map/all_to_all | solution.py:307
  129.7 0.0 collective-permute-done.10.code.tail
  129.7 0.0 copy-done.1
  129.7 0.0 copy-done.2
  129.7 0.0 copy-done.4
  129.7 3.2 %update.1 = (f32[1536,128]{1,0:T(8,128)}, f32[1536,128]{1,0:T(8,128)}) custom-call(s16[1552,128]{1,0:T(8,128)(2,1)S(1)} %collective-permute-done.10.code.tail, s16[1552,128]{1,0:T(8,128)(2,1)S(1)} %collective-permute-done.10.code.tail, f32[32,1,128]{2,1,0:T(1,128)S(1)} %all-to-all-done.2.norm, f32[1]{0:T(128)S(6)} %copy.14.clip, f32[1536,128]{1,0:T(8,128)S(1)} %copy-done.1, ...), custom_call_target="tpu_custom_call" | custom-call | tf_op jit(solution)/shard_map/update/pallas_call | solution.py:310
  (2 shorter events, 0.0 us)
Async XLA Ops:
  1.9 1.4 %copy-start = (bf16[1,48,16384]{2,1,0:T(8,128)(2,1)S(1)}, bf16[1,48,16384]{2,1,0:T(8,128)(2,1)}, u32[]{:S(2)}) copy-start(bf16[1,48,16384]{2,1,0:T(8,128)(2,1)} %g) | copy-start | bytes 4718596
  3.3 63.3 %copy-start.3 = (bf16[128,256]{1,0:T(8,128)(2,1)S(1)}, bf16[128,256]{1,0:T(8,128)(2,1)}, u32[]{:S(2)}) copy-start(bf16[128,256]{1,0:T(8,128)(2,1)} %constant.47.clone.refs_10_.wide) | copy-start | bytes 196612
  3.3 63.3 %copy-start.5 = (bf16[128,256]{1,0:T(8,128)(2,1)S(1)}, bf16[128,256]{1,0:T(8,128)(2,1)}, u32[]{:S(2)}) copy-start(bf16[128,256]{1,0:T(8,128)(2,1)} %constant.46.clone.refs_11_) | copy-start | bytes 196612
  4.3 20.2 %collective-permute-start = (bf16[16,48,128]{2,1,0:T(8,128)(2,1)S(1)}, bf16[16,48,128]{2,1,0:T(8,128)(2,1)S(1)}, u32[]{:S(2)}, u32[]{:S(2)}) collective-permute-start(bf16[16,48,128]{2,1,0:T(8,128)(2,1)S(1)} %get-tuple-element.27), channel_id=1, source_target_pairs={{0,128},{1,129},{128,256},{129,257},{256,384},{257,385},{384,0},{3... | collective-permute-start | bytes 589832 | tf_op jit(solution)/shard_map/ppermute | solution.py:275
  8.3 20.2 %collective-permute-start.1 = (bf16[16,48,128]{2,1,0:T(8,128)(2,1)S(1)}, bf16[16,48,128]{2,1,0:T(8,128)(2,1)S(1)}, u32[]{:S(2)}, u32[]{:S(2)}) collective-permute-start(bf16[16,48,128]{2,1,0:T(8,128)(2,1)S(1)} %get-tuple-element.28), channel_id=1, source_target_pairs={{0,256},{1,257},{128,384},{129,385},{256,0},{257,1},{384,128},{385... | collective-permute-start | bytes 589832 | tf_op jit(solution)/shard_map/ppermute | solution.py:275
  12.6 41.3 %collective-permute-start.2 = (bf16[16,48,128]{2,1,0:T(8,128)(2,1)S(1)}, bf16[16,48,128]{2,1,0:T(8,128)(2,1)S(1)}, u32[]{:S(2)}, u32[]{:S(2)}) collective-permute-start(bf16[16,48,128]{2,1,0:T(8,128)(2,1)S(1)} %get-tuple-element.29), channel_id=1, source_target_pairs={{0,384},{1,385},{128,0},{129,1},{256,128},{257,129},{384,256},{385... | collective-permute-start | bytes 589832 | tf_op jit(solution)/shard_map/ppermute | solution.py:275
  15.7 38.2 %collective-permute-start.3 = (bf16[16,48,128]{2,1,0:T(8,128)(2,1)S(1)}, bf16[16,48,128]{2,1,0:T(8,128)(2,1)S(1)}, u32[]{:S(2)}, u32[]{:S(2)}) collective-permute-start(bf16[16,48,128]{2,1,0:T(8,128)(2,1)S(1)} %get-tuple-element.30), channel_id=1, source_target_pairs={{0,1},{1,0},{128,129},{129,128},{256,257},{257,256},{384,385},{385... | collective-permute-start | bytes 589832 | tf_op jit(solution)/shard_map/ppermute | solution.py:275
  22.1 31.8 %collective-permute-start.4 = (bf16[16,48,128]{2,1,0:T(8,128)(2,1)S(1)}, bf16[16,48,128]{2,1,0:T(8,128)(2,1)S(1)}, u32[]{:S(2)}, u32[]{:S(2)}) collective-permute-start(bf16[16,48,128]{2,1,0:T(8,128)(2,1)S(1)} %get-tuple-element.31), channel_id=1, source_target_pairs={{0,129},{1,128},{128,257},{129,256},{256,385},{257,384},{384,1},{3... | collective-permute-start | bytes 589832 | tf_op jit(solution)/shard_map/ppermute | solution.py:275
  24.5 29.4 %collective-permute-start.5 = (bf16[16,48,128]{2,1,0:T(8,128)(2,1)S(1)}, bf16[16,48,128]{2,1,0:T(8,128)(2,1)S(1)}, u32[]{:S(2)}, u32[]{:S(2)}) collective-permute-start(bf16[16,48,128]{2,1,0:T(8,128)(2,1)S(1)} %get-tuple-element.32), channel_id=1, source_target_pairs={{0,257},{1,256},{128,385},{129,384},{256,1},{257,0},{384,129},{385... | collective-permute-start | bytes 589832 | tf_op jit(solution)/shard_map/ppermute | solution.py:275
  28.5 25.4 %collective-permute-start.6 = (bf16[16,48,128]{2,1,0:T(8,128)(2,1)S(1)}, bf16[16,48,128]{2,1,0:T(8,128)(2,1)S(1)}, u32[]{:S(2)}, u32[]{:S(2)}) collective-permute-start(bf16[16,48,128]{2,1,0:T(8,128)(2,1)S(1)} %get-tuple-element.33), channel_id=1, source_target_pairs={{0,385},{1,384},{128,1},{129,0},{256,129},{257,128},{384,257},{385... | collective-permute-start | bytes 589832 | tf_op jit(solution)/shard_map/ppermute | solution.py:275
  54.6 12.1 %collective-permute-start.9 = (bf16[4,8,64,128]{3,2,1,0:T(8,128)(2,1)S(1)}, bf16[4,8,64,128]{3,2,1,0:T(8,128)(2,1)S(1)}, u32[]{:S(2)}, u32[]{:S(2)}) collective-permute-start(bf16[4,8,64,128]{3,2,1,0:T(8,128)(2,1)S(1)} %get-tuple-element.45), channel_id=1, source_target_pairs={{2,4},{4,2},{10,12},{12,10},{18,20},{20,18},{26,28},{28,26},{3,5},... | collective-permute-start | bytes 1572872 | tf_op jit(solution)/shard_map/ppermute | solution.py:290
  55.3 11.4 %collective-permute-start.8 = (bf16[4,4,96,128]{3,2,1,0:T(8,128)(2,1)S(1)}, bf16[4,4,96,128]{3,2,1,0:T(8,128)(2,1)S(1)}, u32[]{:S(2)}, u32[]{:S(2)}) collective-permute-start(bf16[4,4,96,128]{3,2,1,0:T(8,128)(2,1)S(1)} %get-tuple-element.44), channel_id=1, source_target_pairs={{0,2},{2,0},{4,6},{6,4},{8,10},{10,8},{12,14},{14,12},{16,18},{18,... | collective-permute-start | bytes 1179656 | tf_op jit(solution)/shard_map/ppermute | solution.py:289
  59.0 0.7 collective-permute-start.7
  69.6 60.1 %copy-start.1 = (f32[1536,128]{1,0:T(8,128)S(1)}, f32[1536,128]{1,0:T(8,128)}, u32[]{:S(2)}) copy-start(f32[1536,128]{1,0:T(8,128)} %params.1) | copy-start | bytes 2359300
  69.6 60.0 %copy-start.2 = (f32[1536,128]{1,0:T(8,128)S(1)}, f32[1536,128]{1,0:T(8,128)}, u32[]{:S(2)}) copy-start(f32[1536,128]{1,0:T(8,128)} %mom.1) | copy-start | bytes 2359300
  69.6 60.0 %copy-start.4 = (bf16[256,128]{1,0:T(8,128)(2,1)S(1)}, bf16[256,128]{1,0:T(8,128)(2,1)}, u32[]{:S(2)}) copy-start(bf16[256,128]{1,0:T(8,128)(2,1)} %constant.48.clone.tall) | copy-start | bytes 196612
  105.9 23.8 %collective-permute-start.10 = (s16[1552,128]{1,0:T(8,128)(2,1)S(1)}, s16[1552,128]{1,0:T(8,128)(2,1)S(1)}, u32[]{:S(2)}, u32[]{:S(2)}) collective-permute-start(s16[1552,128]{1,0:T(8,128)(2,1)S(1)} %get-tuple-element.46), channel_id=1, source_target_pairs={{0,0},{32,128},{64,256},{96,384},{128,32},{160,160},{192,288},{224... | collective-permute-start | bytes 1191944 | tf_op jit(solution)/shard_map/ppermute | solution.py:306
  106.6 23.1 %all-to-all-start.2 = ((f32[32,1,128]{2,1,0:T(1,128)}), f32[32,1,128]{2,1,0:T(1,128)S(1)}, u32[]{:S(2)}, u32[]{:S(2)}) async-start(f32[32,1,128]{2,1,0:T(1,128)} %get-tuple-element.47), calls=%async_computation.2 | async-start | bytes 32768 | tf_op jit(solution)/shard_map/all_to_all | solution.py:307

commit v8 on v7

--- a/solution.py
+++ b/solution.py
@@ -57,18 +57,24 @@
 def pack_kernel(pos, g, *outs):
     c, x = pos[1], pos[2]
     for s in range(NX):
-        for out, core in ((outs[s], c), (outs[NX + s], 1 - c)):
+        for half, core in enumerate((c, 1 - c)):
             base = NZ * NC * ((x + s) % 4) + core
             for m in range(4):
                 for w in range(4):
                     start = pl.multiple_of((base + 2 * (4 * w + m)) * BS, BS)
-                    out[4 * m + w] = g[0, :, pl.ds(start, BS)]
+                    outs[s][half, 4 * m + w] = g[0, :, pl.ds(start, BS)]
+
+
+def give_kernel(*refs):
+    for s in range(NX):
+        refs[NX][s] = refs[s][1]
 
 
 def by_place(pos, rows, body):
     for p in range(4):
         for c in range(2):
-            mine, other = rows[:NX], rows[NX:]
+            mine = [v.at[0] for v in rows[:NX]]
+            other = [rows[NX].at[s] for s in range(NX)]
             pair = (mine, other) if c == 0 else (other, mine)
             pl.when((pos[0] == p) & (pos[1] == c))(functools.partial(body, p, *pair))
 
@@ -141,8 +147,8 @@
 
 
 def forward_kernel(pos, cut, *refs):
-    a, b, left, wide, out, x, exps = refs[2 * NX :]
-    assemble(pos, refs[: 2 * NX], a, b, x)
+    a, b, left, wide, out, x, exps = refs[NX + 1 :]
+    assemble(pos, refs[: NX + 1], a, b, x)
     p = pos[0]
     freq = lax.broadcasted_iota(jnp.int32, (BS, BS), 0) + lax.broadcasted_iota(jnp.int32, (BS, BS), 1)
     row = lax.broadcasted_iota(jnp.int32, (TAIL, BS), 0)
@@ -263,17 +269,13 @@
     cut, pseudo_grads = lax.optimization_barrier((cut, pseudo_grads))
     cut = lax.all_to_all(cut, "z", 0, 0, tiled=True)[:, 0]
 
-    packed = call(
-        pack_kernel, [shape((NZ, rows, BS), BF16)] * (2 * NX), (pos, pseudo_grads), "pack"
-    )
-    spread = list(packed)
-    for n in (NX + 2, 2, NX + 1, NX + 3, 1, 3, NX):
-        flip, step = divmod(n, NX)
-        pairs = [
-            (NC * i + c, NC * ((i + step) % NX) + (c ^ flip)) for i in range(NX) for c in range(NC)
-        ]
-        spread[n] = lax.ppermute(packed[n], ("x", "c"), pairs)
+    packed = call(pack_kernel, [shape((NC, NZ, rows, BS), BF16)] * NX, (pos, pseudo_grads), "pack")
+    spread = [packed[0]] + [
+        lax.ppermute(packed[n], "x", [(i, (i + n) % NX) for i in range(NX)]) for n in range(1, NX)
+    ]
     *spread, cut = lax.optimization_barrier((*spread, cut))
+    give = call(give_kernel, shape((NX, NZ, rows, BS), BF16), spread, "give")
+    spread.append(lax.ppermute(give, "c", [(0, 1), (1, 0)]))
     cut = lax.ppermute(cut, ("x", "y"), swap)
 
     a, b = call(

time: 135 us -> 131 us (0.970); the launches traced: 133 us -> 130 us
  starting transfers between devices: 48.2 us -> 35.6 us
  blocking collectives: 56.2 us -> 61.2 us
  waiting for transfers between devices: 15.4 us -> 20.3 us
    ppermute x7 -> x4, starting transfers between devices: 28.4 us -> 16.4 us  [the longest x3 11.4 us: per_device(): lax.ppermute(packed[n], 'x', [(i, (i + n) % NX) for i in range(NX)])]
    all_to_all x1, blocking collectives: 21.2 us -> 26 us  [per_device(): cut = lax.all_to_all(cut, 'z', 0, 0, tiled=True)[:, 0]]
    all_to_all x1, waiting for transfers between devices: 8.32 us -> 10.2 us  [per_device(): norm = lax.all_to_all(norm, ('x', 'y', 'c'), 0, 0, tiled=True)]
    ppermute x7 -> x4, waiting for transfers between devices: 0.02 us -> 1.9 us  [the longest x1 1.89 us: per_device(): spread.append(lax.ppermute(give, 'c', [(0, 1), (1, 0)]))]
    pallas_call x4 -> x5, Pallas kernels: 5.7 us -> 5.74 us  [call(): pl.pallas_call(kernel, out_shape=out_shape, in_specs=[SMEM if i.dtype ==...]
  transfers between devices with their start and end apart: 12 -> 9, of which waited for: 2 -> 3; matrix products, arithmetic and copies ran while one was open for 0% -> 0% of each run, Pallas kernels for 0% -> 0%
where the time goes in v8:
time: 131 us; the launch traced here: 130 us
  blocking collectives  61.2 us (47%)
  starting transfers between devices  35.6 us (27%)
  waiting for transfers between devices  20.3 us (15%)
  Pallas kernels  8.98 us (7%)
  local copies, waits for them, and re-layouts  2.55 us (2%)
  between operations  1.49 us (1%)
    all_to_all x1, blocking collectives, per_device(): coded = lax.all_to_all(coded, 'z', 0, 0, tiled=True)  35.2 us
    all_to_all x1, blocking collectives, per_device(): cut = lax.all_to_all(cut, 'z', 0, 0, tiled=True)[:, 0]  26 us
    all_to_all x1, starting transfers between devices, per_device(): norm = lax.all_to_all(norm, ('x', 'y', 'c'), 0, 0, tiled=True)  13.5 us
    ppermute x3, starting transfers between devices, per_device(): lax.ppermute(packed[n], 'x', [(i, (i + n) % NX) for i in range(NX)])  11.4 us
    all_to_all x1, waiting for transfers between devices, per_device(): norm = lax.all_to_all(norm, ('x', 'y', 'c'), 0, 0, tiled=True)  10.2 us
    ppermute x1, waiting for transfers between devices, per_device(): a = lax.ppermute(a, 'z', pair_a)  8.17 us
    pallas_call x5, Pallas kernels, call(): pl.pallas_call(kernel, out_shape=out_shape, in_specs=[SMEM if i.dtype ==...  5.74 us
    ppermute x1, starting transfers between devices, per_device(): spread.append(lax.ppermute(give, 'c', [(0, 1), (1, 0)]))  4.98 us
  transfers between devices with their start and end apart: 9, of which 3 were waited for; matrix products, arithmetic and copies ran while one was open for 0% of the time, Pallas kernels for 0%

profile of v8, /device:TPU:1, one launch (start us, length us, event | category | flops | bytes accessed | tf_op | source)
XLA Modules:
  0.0 130.3 jit_solution(10618080898520296064)
XLA Ops:
  0.6 0.7 constant_dynamic-slice_fusion
  1.4 0.1 copy.11
  1.5 0.1 copy.12
  1.6 0.1 select_reduce_fusion
  1.6 0.1 copy.13
  1.7 0.1 broadcast_in_dim.27
  1.9 0.1 pad_add_fusion.pos
  1.9 0.0 copy-start
  1.9 1.4 %copy-done = bf16[1,48,16384]{2,1,0:T(8,128)(2,1)S(1)} copy-done((bf16[1,48,16384]{2,1,0:T(8,128)(2,1)S(1)}, bf16[1,48,16384]{2,1,0:T(8,128)(2,1)}, u32[]{:S(2)}) %copy-start) | copy-done | bytes 1572888
  3.3 1.0 pack.1
  4.3 3.9 %collective-permute-start = (bf16[2,16,48,128]{3,2,1,0:T(8,128)(2,1)S(1)}, bf16[2,16,48,128]{3,2,1,0:T(8,128)(2,1)S(1)}, u32[]{:S(2)}, u32[]{:S(2)}) collective-permute-start(bf16[2,16,48,128]{3,2,1,0:T(8,128)(2,1)S(1)} %get-tuple-element.19), channel_id=1, source_target_pairs={{0,128},{128,256},{256,384},{384,0},{1,129},{129,257},{257,385},{3... | collective-permute-start | bytes 1179656 | tf_op jit(solution)/shard_map/ppermute | solution.py:274
  8.3 4.4 %collective-permute-start.1 = (bf16[2,16,48,128]{3,2,1,0:T(8,128)(2,1)S(1)}, bf16[2,16,48,128]{3,2,1,0:T(8,128)(2,1)S(1)}, u32[]{:S(2)}, u32[]{:S(2)}) collective-permute-start(bf16[2,16,48,128]{3,2,1,0:T(8,128)(2,1)S(1)} %get-tuple-element.20), channel_id=1, source_target_pairs={{0,256},{128,384},{256,0},{384,128},{1,257},{129,385},{257,1},{385... | collective-permute-start | bytes 1179656 | tf_op jit(solution)/shard_map/ppermute | solution.py:274
  12.6 3.1 %collective-permute-start.2 = (bf16[2,16,48,128]{3,2,1,0:T(8,128)(2,1)S(1)}, bf16[2,16,48,128]{3,2,1,0:T(8,128)(2,1)S(1)}, u32[]{:S(2)}, u32[]{:S(2)}) collective-permute-start(bf16[2,16,48,128]{3,2,1,0:T(8,128)(2,1)S(1)} %get-tuple-element.21), channel_id=1, source_target_pairs={{0,384},{128,0},{256,128},{384,256},{1,385},{129,1},{257,129},{385... | collective-permute-start | bytes 1179656 | tf_op jit(solution)/shard_map/ppermute | solution.py:274
  15.7 26.0 %all_to_all.15 = s32[16,1,128]{2,1,0:T(1,128)S(1)} all-to-all(s32[16,1,128]{2,1,0:T(1,128)S(1)} %pad.4), channel_id=1, replica_groups=mesh['x'=4,'y'=4,'z'=16,'c'=2] {'z'}, dimensions={0} | all-to-all | bytes 16384 | tf_op jit(solution)/shard_map/all_to_all | solution.py:270
  41.7 0.0 collective-permute-done.refs_1_
  41.7 0.0 collective-permute-done.1.refs_2_
  41.7 0.0 collective-permute-done.2.refs_3_
  41.7 0.1 give.1
  41.8 0.0 copy-start.3
  41.8 0.0 copy-start.4
  41.8 5.0 %collective-permute-start.4 = (bf16[4,16,48,128]{3,2,1,0:T(8,128)(2,1)S(1)}, bf16[4,16,48,128]{3,2,1,0:T(8,128)(2,1)S(1)}, u32[]{:S(2)}, u32[]{:S(2)}) collective-permute-start(bf16[4,16,48,128]{3,2,1,0:T(8,128)(2,1)S(1)} %give.1), channel_id=1, source_target_pairs={{0,1},{1,0},{2,3},{3,2},{4,5},{5,4},{6,7},{7,6},{8,9},{9,8},{10,11... | collective-permute-start | bytes 2359304 | tf_op jit(solution)/shard_map/ppermute | solution.py:278
  46.8 1.9 %collective-permute-done.4.refs_4_ = bf16[4,16,48,128]{3,2,1,0:T(8,128)(2,1)S(1)} collective-permute-done((bf16[4,16,48,128]{3,2,1,0:T(8,128)(2,1)S(1)}, bf16[4,16,48,128]{3,2,1,0:T(8,128)(2,1)S(1)}, u32[]{:S(2)}, u32[]{:S(2)}) %collective-permute-start.4) | collective-permute-done | bytes 786464 | tf_op jit(solution)/shard_map/ppermute | solution.py:278
  48.7 0.6 exchange.1
  49.3 0.7 collective-permute-start.6
  50.1 3.7 %collective-permute-start.5 = (bf16[4,4,96,128]{3,2,1,0:T(8,128)(2,1)S(1)}, bf16[4,4,96,128]{3,2,1,0:T(8,128)(2,1)S(1)}, u32[]{:S(2)}, u32[]{:S(2)}) collective-permute-start(bf16[4,4,96,128]{3,2,1,0:T(8,128)(2,1)S(1)} %get-tuple-element.28), channel_id=1, source_target_pairs={{0,2},{2,0},{4,6},{6,4},{8,10},{10,8},{12,14},{14,12},{16,18},{18,... | collective-permute-start | bytes 1179656 | tf_op jit(solution)/shard_map/ppermute | solution.py:291
  53.7 0.7 collective-permute-start.3
  54.4 0.0 collective-permute-done.3.cut
  54.4 8.2 %collective-permute-done.5.refs_5_ = bf16[4,4,96,128]{3,2,1,0:T(8,128)(2,1)S(1)} collective-permute-done((bf16[4,4,96,128]{3,2,1,0:T(8,128)(2,1)S(1)}, bf16[4,4,96,128]{3,2,1,0:T(8,128)(2,1)S(1)}, u32[]{:S(2)}, u32[]{:S(2)}) %collective-permute-start.5) | collective-permute-done | bytes 393248 | tf_op jit(solution)/shard_map/ppermute | solution.py:291
  62.6 0.0 collective-permute-done.6.refs_6_
  62.6 0.0 copy-done.3
  62.6 0.0 copy-done.4
  62.6 2.9 %forward.1 = s16[16,144,128]{2,1,0:T(8,128)(2,1)S(1)} custom-call(s32[3]{0:T(128)S(1)} %pad_add_fusion.pos, s32[16,128]{1,0:T(8,128)S(1)} %collective-permute-done.3.cut, bf16[2,16,48,128]{3,2,1,0:T(8,128)(2,1)S(1)} %get-tuple-element.24.refs_0_, bf16[2,16,48,128]{3,2,1,0:T(8,128)(2,1)S(1)} %collective-permute-done.refs_1_, ...), custom_call_target="tpu_custom_call" | custom-call | tf_op jit(solution)/shard_map/forward/pallas_call | solution.py:240
  65.5 0.0 copy-start.1
  65.5 0.0 copy-start.2
  65.5 0.0 copy-start.5
  65.6 35.2 %all_to_all.16.z = s16[16,144,128]{2,1,0:T(8,128)(2,1)S(1)} all-to-all(s16[16,144,128]{2,1,0:T(8,128)(2,1)S(1)} %forward.1), channel_id=1, replica_groups=mesh['x'=4,'y'=4,'z'=16,'c'=2] {'z'}, dimensions={0} | all-to-all | bytes 1179648 | tf_op jit(solution)/shard_map/all_to_all | solution.py:301
  100.8 1.2 compact.1
  102.0 0.7 collective-permute-start.7
  102.6 13.5 %all-to-all-start.2 = ((f32[32,1,128]{2,1,0:T(1,128)}), f32[32,1,128]{2,1,0:T(1,128)S(1)}, u32[]{:S(2)}, u32[]{:S(2)}) async-start(f32[32,1,128]{2,1,0:T(1,128)} %get-tuple-element.31), calls=%async_computation.2 | async-start | bytes 32768 | tf_op jit(solution)/shard_map/all_to_all | solution.py:309
  116.8 10.2 %all-to-all-done.2.norm = f32[32,1,128]{2,1,0:T(1,128)S(1)} async-done(((f32[32,1,128]{2,1,0:T(1,128)}), f32[32,1,128]{2,1,0:T(1,128)S(1)}, u32[]{:S(2)}, u32[]{:S(2)}) %all-to-all-start.2) | async-done | bytes 16416 | tf_op jit(solution)/shard_map/all_to_all | solution.py:309
  127.1 0.0 collective-permute-done.7.code.tail
  127.1 0.0 copy-done.1
  127.1 0.0 copy-done.2
  127.1 0.0 copy-done.5
  127.1 3.2 %update.1 = (f32[1536,128]{1,0:T(8,128)}, f32[1536,128]{1,0:T(8,128)}) custom-call(s16[1552,128]{1,0:T(8,128)(2,1)S(1)} %collective-permute-done.7.code.tail, s16[1552,128]{1,0:T(8,128)(2,1)S(1)} %collective-permute-done.7.code.tail, f32[32,1,128]{2,1,0:T(1,128)S(1)} %all-to-all-done.2.norm, f32[1]{0:T(128)S(6)} %copy.14.clip, f32[1536,128]{1,0:T(8,128)S(1)} %copy-done.1, ...), custom_call_target="tpu_custom_call" | custom-call | tf_op jit(solution)/shard_map/update/pallas_call | solution.py:312
  (2 shorter events, 0.0 us)
Async XLA Ops:
  1.9 1.4 %copy-start = (bf16[1,48,16384]{2,1,0:T(8,128)(2,1)S(1)}, bf16[1,48,16384]{2,1,0:T(8,128)(2,1)}, u32[]{:S(2)}) copy-start(bf16[1,48,16384]{2,1,0:T(8,128)(2,1)} %g) | copy-start | bytes 4718596
  4.3 37.4 %collective-permute-start = (bf16[2,16,48,128]{3,2,1,0:T(8,128)(2,1)S(1)}, bf16[2,16,48,128]{3,2,1,0:T(8,128)(2,1)S(1)}, u32[]{:S(2)}, u32[]{:S(2)}) collective-permute-start(bf16[2,16,48,128]{3,2,1,0:T(8,128)(2,1)S(1)} %get-tuple-element.19), channel_id=1, source_target_pairs={{0,128},{128,256},{256,384},{384,0},{1,129},{129,257},{257,385},{3... | collective-permute-start | bytes 1179656 | tf_op jit(solution)/shard_map/ppermute | solution.py:274
  8.3 33.5 %collective-permute-start.1 = (bf16[2,16,48,128]{3,2,1,0:T(8,128)(2,1)S(1)}, bf16[2,16,48,128]{3,2,1,0:T(8,128)(2,1)S(1)}, u32[]{:S(2)}, u32[]{:S(2)}) collective-permute-start(bf16[2,16,48,128]{3,2,1,0:T(8,128)(2,1)S(1)} %get-tuple-element.20), channel_id=1, source_target_pairs={{0,256},{128,384},{256,0},{384,128},{1,257},{129,385},{257,1},{385... | collective-permute-start | bytes 1179656 | tf_op jit(solution)/shard_map/ppermute | solution.py:274
  12.6 29.1 %collective-permute-start.2 = (bf16[2,16,48,128]{3,2,1,0:T(8,128)(2,1)S(1)}, bf16[2,16,48,128]{3,2,1,0:T(8,128)(2,1)S(1)}, u32[]{:S(2)}, u32[]{:S(2)}) collective-permute-start(bf16[2,16,48,128]{3,2,1,0:T(8,128)(2,1)S(1)} %get-tuple-element.21), channel_id=1, source_target_pairs={{0,384},{128,0},{256,128},{384,256},{1,385},{129,1},{257,129},{385... | collective-permute-start | bytes 1179656 | tf_op jit(solution)/shard_map/ppermute | solution.py:274
  41.8 20.8 %copy-start.3 = (bf16[128,256]{1,0:T(8,128)(2,1)S(1)}, bf16[128,256]{1,0:T(8,128)(2,1)}, u32[]{:S(2)}) copy-start(bf16[128,256]{1,0:T(8,128)(2,1)} %constant.47.clone.refs_7_.wide) | copy-start | bytes 196612
  41.8 20.8 %copy-start.4 = (bf16[128,256]{1,0:T(8,128)(2,1)S(1)}, bf16[128,256]{1,0:T(8,128)(2,1)}, u32[]{:S(2)}) copy-start(bf16[128,256]{1,0:T(8,128)(2,1)} %constant.46.clone.refs_8_) | copy-start | bytes 196612
  41.8 6.9 %collective-permute-start.4 = (bf16[4,16,48,128]{3,2,1,0:T(8,128)(2,1)S(1)}, bf16[4,16,48,128]{3,2,1,0:T(8,128)(2,1)S(1)}, u32[]{:S(2)}, u32[]{:S(2)}) collective-permute-start(bf16[4,16,48,128]{3,2,1,0:T(8,128)(2,1)S(1)} %give.1), channel_id=1, source_target_pairs={{0,1},{1,0},{2,3},{3,2},{4,5},{5,4},{6,7},{7,6},{8,9},{9,8},{10,11... | collective-permute-start | bytes 2359304 | tf_op jit(solution)/shard_map/ppermute | solution.py:278
  49.3 13.2 %collective-permute-start.6 = (bf16[4,8,64,128]{3,2,1,0:T(8,128)(2,1)S(1)}, bf16[4,8,64,128]{3,2,1,0:T(8,128)(2,1)S(1)}, u32[]{:S(2)}, u32[]{:S(2)}) collective-permute-start(bf16[4,8,64,128]{3,2,1,0:T(8,128)(2,1)S(1)} %get-tuple-element.29), channel_id=1, source_target_pairs={{2,4},{4,2},{10,12},{12,10},{18,20},{20,18},{26,28},{28,26},{3,5},... | collective-permute-start | bytes 1572872 | tf_op jit(solution)/shard_map/ppermute | solution.py:292
  50.1 12.5 %collective-permute-start.5 = (bf16[4,4,96,128]{3,2,1,0:T(8,128)(2,1)S(1)}, bf16[4,4,96,128]{3,2,1,0:T(8,128)(2,1)S(1)}, u32[]{:S(2)}, u32[]{:S(2)}) collective-permute-start(bf16[4,4,96,128]{3,2,1,0:T(8,128)(2,1)S(1)} %get-tuple-element.28), channel_id=1, source_target_pairs={{0,2},{2,0},{4,6},{6,4},{8,10},{10,8},{12,14},{14,12},{16,18},{18,... | collective-permute-start | bytes 1179656 | tf_op jit(solution)/shard_map/ppermute | solution.py:291
  53.7 0.7 collective-permute-start.3
  65.5 61.5 %copy-start.1 = (f32[1536,128]{1,0:T(8,128)S(1)}, f32[1536,128]{1,0:T(8,128)}, u32[]{:S(2)}) copy-start(f32[1536,128]{1,0:T(8,128)} %params.1) | copy-start | bytes 2359300
  65.5 61.5 %copy-start.2 = (f32[1536,128]{1,0:T(8,128)S(1)}, f32[1536,128]{1,0:T(8,128)}, u32[]{:S(2)}) copy-start(f32[1536,128]{1,0:T(8,128)} %mom.1) | copy-start | bytes 2359300
  65.5 61.5 %copy-start.5 = (bf16[256,128]{1,0:T(8,128)(2,1)S(1)}, bf16[256,128]{1,0:T(8,128)(2,1)}, u32[]{:S(2)}) copy-start(bf16[256,128]{1,0:T(8,128)(2,1)} %constant.48.clone.tall) | copy-start | bytes 196612
  102.0 25.1 %collective-permute-start.7 = (s16[1552,128]{1,0:T(8,128)(2,1)S(1)}, s16[1552,128]{1,0:T(8,128)(2,1)S(1)}, u32[]{:S(2)}, u32[]{:S(2)}) collective-permute-start(s16[1552,128]{1,0:T(8,128)(2,1)S(1)} %get-tuple-element.30), channel_id=1, source_target_pairs={{0,0},{32,128},{64,256},{96,384},{128,32},{160,160},{192,288},{224... | collective-permute-start | bytes 1191944 | tf_op jit(solution)/shard_map/ppermute | solution.py:308
  102.6 24.4 %all-to-all-start.2 = ((f32[32,1,128]{2,1,0:T(1,128)}), f32[32,1,128]{2,1,0:T(1,128)S(1)}, u32[]{:S(2)}, u32[]{:S(2)}) async-start(f32[32,1,128]{2,1,0:T(1,128)} %get-tuple-element.31), calls=%async_computation.2 | async-start | bytes 32768 | tf_op jit(solution)/shard_map/all_to_all | solution.py:309

commit v9 on v8

--- a/solution.py
+++ b/solution.py
@@ -147,7 +147,7 @@
 
 
 def forward_kernel(pos, cut, *refs):
-    a, b, left, wide, out, x, exps = refs[NX + 1 :]
+    a, b, left, wide, out, norm, x, exps = refs[NX + 1 :]
     assemble(pos, refs[: NX + 1], a, b, x)
     p = pos[0]
     freq = lax.broadcasted_iota(jnp.int32, (BS, BS), 0) + lax.broadcasted_iota(jnp.int32, (BS, BS), 1)
@@ -184,18 +184,13 @@
     square = jnp.zeros((1, BS), F32)
     for w in range(4):
         square = step(w, square)
-    e = exponent(square)
-    scaled = jnp.minimum(square, F32(3e38)) * jnp.exp2(-0.5 * e) * jnp.exp2(-0.5 * e) * 16384.0
-    d1 = jnp.floor(scaled)
-    d2 = jnp.floor((scaled - d1) * 16384.0)
-    e = jnp.where(square > F32(3e38), 200.0, e)
-    tail = jnp.where(row == 1, e, jnp.where(row == 2, d1, jnp.where(row == 3, d2, 0.0)))
+    norm[...] = square
     for s in range(NZ):
-        mix = jnp.where(row == 0, exps[s : s + 1, :], tail)
-        out[s, BS : BS + TAIL] = mix.astype(jnp.int32).astype(jnp.int16)
-
-
-def compact_kernel(pos, z, out, norm):
+        tail = jnp.where(row == 0, exps[s : s + 1, :], 0.0)
+        out[s, BS : BS + TAIL] = tail.astype(jnp.int32).astype(jnp.int16)
+
+
+def compact_kernel(pos, z, out):
     p = pos[0]
     row = lax.broadcasted_iota(jnp.int32, (TAIL, BS), 0)
     tail = jnp.zeros((TAIL, BS), F32)
@@ -207,12 +202,6 @@
             e = z[src, BS : BS + TAIL].astype(jnp.int32).astype(F32)[0:1]
             tail = jnp.where(row == n, e, tail)
     out[BS * BPO : BS * BPO + TAIL] = tail.astype(jnp.int32).astype(jnp.int16)
-    total = jnp.zeros((1, BS), F32)
-    for s in range(NZ):
-        t = z[s, BS : BS + TAIL].astype(jnp.int32).astype(F32)
-        part = t[2:3] * F32(1.0 / 16384.0) + t[3:4] * F32(1.0 / 16384.0**2)
-        total += part * jnp.exp2(0.5 * t[1:2]) * jnp.exp2(0.5 * t[1:2])
-    norm[...] = jnp.broadcast_to(total[None], norm.shape)
 
 
 def update_kernel(code, tail, norm, clip, params, mom, tall, wide, new_p, new_m):
@@ -266,10 +255,10 @@
     cut = jnp.max(jnp.where(hit, cuts[:, :, None], -1), axis=1)
     cut = jnp.broadcast_to(cut.T.reshape(4, 1, BPO), (4, 4, BPO)).reshape(NZ, 1, BPO)
     cut = jnp.pad(cut, ((0, 0), (0, 0), (0, BS - BPO)))
-    cut, pseudo_grads = lax.optimization_barrier((cut, pseudo_grads))
+
+    packed = call(pack_kernel, [shape((NC, NZ, rows, BS), BF16)] * NX, (pos, pseudo_grads), "pack")
+    *packed, cut = lax.optimization_barrier((*packed, cut))
     cut = lax.all_to_all(cut, "z", 0, 0, tiled=True)[:, 0]
-
-    packed = call(pack_kernel, [shape((NC, NZ, rows, BS), BF16)] * NX, (pos, pseudo_grads), "pack")
     spread = [packed[0]] + [
         lax.ppermute(packed[n], "x", [(i, (i + n) % NX) for i in range(NX)]) for n in range(1, NX)
     ]
@@ -291,22 +280,20 @@
     a = lax.ppermute(a, "z", pair_a)
     b = lax.ppermute(b, "z", pair_b)
 
-    coded = call(
+    coded, square = call(
         forward_kernel,
-        shape((NZ, BS + TAIL, BS), jnp.int16),
+        (shape((NZ, BS + TAIL, BS), jnp.int16), shape((1, BS), F32)),
         (pos, cut, *spread, a, b, inv_wide, fwd_wide),
         "forward",
         [pltpu.VMEM((NX, BPO, BS, BS), BF16), pltpu.VMEM((NZ, BS), F32)],
     )
     coded = lax.all_to_all(coded, "z", 0, 0, tiled=True)
-    coded, norm = call(
-        compact_kernel,
-        (shape((BPO * BS + TAIL, BS), jnp.int16), shape((NX * NY * NC, 1, BS), F32)),
-        (pos, coded),
-        "compact",
-    )
+    for axis, size, bit in (("c", NC, 1), ("x", NX, 1), ("y", NY, 1), ("x", NX, 2), ("y", NY, 2)):
+        square += lax.ppermute(square, axis, [(i, i ^ bit) for i in range(size)])
+    coded, square = lax.optimization_barrier((coded, square))
+    coded = call(compact_kernel, shape((BPO * BS + TAIL, BS), jnp.int16), (pos, coded), "compact")
     coded = lax.ppermute(coded, ("x", "y"), swap)
-    norm = lax.all_to_all(norm, ("x", "y", "c"), 0, 0, tiled=True)
+    norm = lax.all_to_all(jnp.broadcast_to(square[None], (NZ, 1, BS)), "z", 0, 0, tiled=True)
 
     tile = pl.BlockSpec((3 * BS, BS), lambda i: (i, 0))
     return pl.pallas_call(

time: 131 us -> 133 us (1.015)
  the two profiles are of different devices: /device:TPU:1 before, /device:TPU:4 now
where the time goes in v9:
time: 133 us; the launch traced here: 132 us
  starting transfers between devices  67.3 us (51%)
  waiting for transfers between devices  28.6 us (22%)
  blocking collectives  22.1 us (17%)
  Pallas kernels  9.14 us (7%)
  local copies, waits for them, and re-layouts  3.14 us (2%)
  between operations  1.52 us (1%)
    all_to_all x1, blocking collectives, per_device(): cut = lax.all_to_all(cut, 'z', 0, 0, tiled=True)[:, 0]  22.1 us
    ppermute x5, starting transfers between devices, per_device(): square += lax.ppermute(square, axis, [(i, i ^ bit) for i in range(size)])  17.4 us
    ppermute x3, starting transfers between devices, per_device(): lax.ppermute(packed[n], 'x', [(i, (i + n) % NX) for i in range(NX)])  14.2 us
    all_to_all x1, waiting for transfers between devices, per_device(): lax.all_to_all(jnp.broadcast_to(square[None], (NZ, 1, BS)), 'z', 0, 0, ti...  11.7 us
    ppermute x5, waiting for transfers between devices, per_device(): square += lax.ppermute(square, axis, [(i, i ^ bit) for i in range(size)])  10.3 us
    all_to_all x1, starting transfers between devices, per_device(): lax.all_to_all(jnp.broadcast_to(square[None], (NZ, 1, BS)), 'z', 0, 0, ti...  10 us
    ppermute x1, starting transfers between devices, per_device(): cut = lax.ppermute(cut, ('x', 'y'), swap)  7.56 us
    ppermute x1, starting transfers between devices, per_device(): coded = lax.ppermute(coded, ('x', 'y'), swap)  6.19 us
  transfers between devices with their start and end apart: 15, of which 9 were waited for; matrix products, arithmetic and copies ran while one was open for 0% of the time, Pallas kernels for 0%

profile of v9, /device:TPU:4, one launch (start us, length us, event | category | flops | bytes accessed | tf_op | source)
XLA Modules:
  0.0 132.0 jit_solution(16778458596487910282)
XLA Ops:
  0.6 0.7 constant_dynamic-slice_fusion
  1.4 0.1 copy.11
  1.5 0.1 copy.12
  1.6 0.1 select_reduce_fusion
  1.6 0.1 copy.13
  1.7 0.1 broadcast_in_dim.35
  1.9 0.1 pad_add_fusion.pos
  1.9 0.0 copy-start
  1.9 1.4 %copy-done = bf16[1,48,16384]{2,1,0:T(8,128)(2,1)S(1)} copy-done((bf16[1,48,16384]{2,1,0:T(8,128)(2,1)S(1)}, bf16[1,48,16384]{2,1,0:T(8,128)(2,1)}, u32[]{:S(2)}) %copy-start) | copy-done | bytes 1572888
  3.3 1.0 pack.1
  4.3 3.1 %collective-permute-start = (bf16[2,16,48,128]{3,2,1,0:T(8,128)(2,1)S(1)}, bf16[2,16,48,128]{3,2,1,0:T(8,128)(2,1)S(1)}, u32[]{:S(2)}, u32[]{:S(2)}) collective-permute-start(bf16[2,16,48,128]{3,2,1,0:T(8,128)(2,1)S(1)} %get-tuple-element.27), channel_id=1, source_target_pairs={{0,128},{128,256},{256,384},{384,0},{1,129},{129,257},{257,385},{3... | collective-permute-start | bytes 1179656 | tf_op jit(solution)/shard_map/ppermute | solution.py:263
  7.4 6.6 %collective-permute-start.1 = (bf16[2,16,48,128]{3,2,1,0:T(8,128)(2,1)S(1)}, bf16[2,16,48,128]{3,2,1,0:T(8,128)(2,1)S(1)}, u32[]{:S(2)}, u32[]{:S(2)}) collective-permute-start(bf16[2,16,48,128]{3,2,1,0:T(8,128)(2,1)S(1)} %get-tuple-element.28), channel_id=1, source_target_pairs={{0,256},{128,384},{256,0},{384,128},{1,257},{129,385},{257,1},{385... | collective-permute-start | bytes 1179656 | tf_op jit(solution)/shard_map/ppermute | solution.py:263
  14.0 4.5 %collective-permute-start.2 = (bf16[2,16,48,128]{3,2,1,0:T(8,128)(2,1)S(1)}, bf16[2,16,48,128]{3,2,1,0:T(8,128)(2,1)S(1)}, u32[]{:S(2)}, u32[]{:S(2)}) collective-permute-start(bf16[2,16,48,128]{3,2,1,0:T(8,128)(2,1)S(1)} %get-tuple-element.29), channel_id=1, source_target_pairs={{0,384},{128,0},{256,128},{384,256},{1,385},{129,1},{257,129},{385... | collective-permute-start | bytes 1179656 | tf_op jit(solution)/shard_map/ppermute | solution.py:263
  18.6 22.1 %all_to_all.15 = s32[16,1,128]{2,1,0:T(1,128)S(1)} all-to-all(s32[16,1,128]{2,1,0:T(1,128)S(1)} %pad.4), channel_id=1, replica_groups=mesh['x'=4,'y'=4,'z'=16,'c'=2] {'z'}, dimensions={0} | all-to-all | bytes 16384 | tf_op jit(solution)/shard_map/all_to_all | solution.py:261
  40.7 0.0 collective-permute-done.refs_1_
  40.7 0.0 collective-permute-done.1.refs_2_
  40.7 0.0 collective-permute-done.2.refs_3_
  40.7 0.1 give.1
  40.7 0.0 copy-start.3
  40.7 0.0 copy-start.5
  40.8 2.1 %collective-permute-start.4 = (bf16[4,16,48,128]{3,2,1,0:T(8,128)(2,1)S(1)}, bf16[4,16,48,128]{3,2,1,0:T(8,128)(2,1)S(1)}, u32[]{:S(2)}, u32[]{:S(2)}) collective-permute-start(bf16[4,16,48,128]{3,2,1,0:T(8,128)(2,1)S(1)} %give.1), channel_id=1, source_target_pairs={{0,1},{1,0},{2,3},{3,2},{4,5},{5,4},{6,7},{7,6},{8,9},{9,8},{10,11... | collective-permute-start | bytes 2359304 | tf_op jit(solution)/shard_map/ppermute | solution.py:267
  42.8 2.3 %collective-permute-done.4.refs_4_ = bf16[4,16,48,128]{3,2,1,0:T(8,128)(2,1)S(1)} collective-permute-done((bf16[4,16,48,128]{3,2,1,0:T(8,128)(2,1)S(1)}, bf16[4,16,48,128]{3,2,1,0:T(8,128)(2,1)S(1)}, u32[]{:S(2)}, u32[]{:S(2)}) %collective-permute-start.4) | collective-permute-done | bytes 786464 | tf_op jit(solution)/shard_map/ppermute | solution.py:267
  45.1 0.6 exchange.1
  45.7 0.7 collective-permute-start.6
  46.4 4.2 %collective-permute-start.5 = (bf16[4,4,96,128]{3,2,1,0:T(8,128)(2,1)S(1)}, bf16[4,4,96,128]{3,2,1,0:T(8,128)(2,1)S(1)}, u32[]{:S(2)}, u32[]{:S(2)}) collective-permute-start(bf16[4,4,96,128]{3,2,1,0:T(8,128)(2,1)S(1)} %get-tuple-element.36), channel_id=1, source_target_pairs={{0,2},{2,0},{4,6},{6,4},{8,10},{10,8},{12,14},{14,12},{16,18},{18,... | collective-permute-start | bytes 1179656 | tf_op jit(solution)/shard_map/ppermute | solution.py:280
  50.7 7.6 %collective-permute-start.3 = (s32[16,128]{1,0:T(8,128)S(1)}, s32[16,128]{1,0:T(8,128)S(1)}, u32[]{:S(2)}, u32[]{:S(2)}) collective-permute-start(s32[16,128]{1,0:T(8,128)S(1)} %bitcast.13), channel_id=1, source_target_pairs={{0,0},{32,128},{64,256},{96,384},{128,32},{160,160},{192,288},{224... | collective-permute-start | bytes 24584 | tf_op jit(solution)/shard_map/ppermute | solution.py:268
  58.2 1.9 %collective-permute-done.3.cut = s32[16,128]{1,0:T(8,128)S(1)} collective-permute-done((s32[16,128]{1,0:T(8,128)S(1)}, s32[16,128]{1,0:T(8,128)S(1)}, u32[]{:S(2)}, u32[]{:S(2)}) %collective-permute-start.3) | collective-permute-done | bytes 8224 | tf_op jit(solution)/shard_map/ppermute | solution.py:268
  60.1 0.0 collective-permute-done.5.refs_5_
  60.1 0.0 collective-permute-done.6.refs_6_
  60.1 0.0 copy-done.3
  60.1 0.0 copy-done.5
  60.1 3.7 %forward.1 = (s16[16,144,128]{2,1,0:T(8,128)(2,1)}, f32[1,128]{1,0:T(1,128)S(1)}) custom-call(s32[3]{0:T(128)S(1)} %pad_add_fusion.pos, s32[16,128]{1,0:T(8,128)S(1)} %collective-permute-done.3.cut, bf16[2,16,48,128]{3,2,1,0:T(8,128)(2,1)S(1)} %get-tuple-element.32.refs_0_, bf16[2,16,48,128]{3,2,1,0:T(8,128)(2,1)S(1)} %collective-permute-done.refs_1_, ...), custom_call_target="tpu_custom_call" | custom-call | tf_op jit(solution)/shard_map/forward/pallas_call | solution.py:229
  63.9 0.0 copy-start.1
  63.9 0.0 copy-start.2
  63.9 0.0 copy-start.4
  63.9 4.9 %all-to-all-start.1 = ((s16[16,144,128]{2,1,0:T(8,128)(2,1)}), s16[16,144,128]{2,1,0:T(8,128)(2,1)S(1)}, u32[]{:S(2)}, u32[]{:S(2)}) async-start(s16[16,144,128]{2,1,0:T(8,128)(2,1)} %get-tuple-element.38), calls=%async_computation.1 | async-start | bytes 1179648 | tf_op jit(solution)/shard_map/all_to_all | solution.py:290
  68.8 1.9 %collective-permute-start.7 = (f32[1,128]{1,0:T(1,128)S(1)}, f32[1,128]{1,0:T(1,128)S(1)}, u32[]{:S(2)}, u32[]{:S(2)}) collective-permute-start(f32[1,128]{1,0:T(1,128)S(1)} %get-tuple-element.39), channel_id=1, source_target_pairs={{0,1},{1,0},{2,3},{3,2},{4,5},{5,4},{6,7},{7,6},{8,9},{9,8},{10,11... | collective-permute-start | bytes 1544 | tf_op jit(solution)/shard_map/ppermute | solution.py:292
  70.7 1.1 collective-permute-done.7
  71.8 3.0 %collective-permute-start.8 = (f32[1,128]{1,0:T(1,128)S(1)}, f32[1,128]{1,0:T(1,128)S(1)}, u32[]{:S(2)}, u32[]{:S(2)}) collective-permute-start(f32[1,128]{1,0:T(1,128)S(1)} %add.28), channel_id=1, source_target_pairs={{0,128},{128,0},{256,384},{384,256},{1,129},{129,1},{257,385},{385... | collective-permute-start | bytes 1544 | tf_op jit(solution)/shard_map/ppermute | solution.py:292
  74.8 2.5 %collective-permute-done.8 = f32[1,128]{1,0:T(1,128)S(1)} collective-permute-done((f32[1,128]{1,0:T(1,128)S(1)}, f32[1,128]{1,0:T(1,128)S(1)}, u32[]{:S(2)}, u32[]{:S(2)}) %collective-permute-start.8) | collective-permute-done | bytes 544 | tf_op jit(solution)/shard_map/ppermute | solution.py:292
  77.2 3.5 %collective-permute-start.9 = (f32[1,128]{1,0:T(1,128)S(1)}, f32[1,128]{1,0:T(1,128)S(1)}, u32[]{:S(2)}, u32[]{:S(2)}) collective-permute-start(f32[1,128]{1,0:T(1,128)S(1)} %add.29), channel_id=1, source_target_pairs={{0,32},{32,0},{64,96},{96,64},{1,33},{33,1},{65,97},{97,65},{2,34}... | collective-permute-start | bytes 1544 | tf_op jit(solution)/shard_map/ppermute | solution.py:292
  80.7 1.9 %collective-permute-done.9 = f32[1,128]{1,0:T(1,128)S(1)} collective-permute-done((f32[1,128]{1,0:T(1,128)S(1)}, f32[1,128]{1,0:T(1,128)S(1)}, u32[]{:S(2)}, u32[]{:S(2)}) %collective-permute-start.9) | collective-permute-done | bytes 544 | tf_op jit(solution)/shard_map/ppermute | solution.py:292
  82.7 3.9 %collective-permute-start.10 = (f32[1,128]{1,0:T(1,128)S(1)}, f32[1,128]{1,0:T(1,128)S(1)}, u32[]{:S(2)}, u32[]{:S(2)}) collective-permute-start(f32[1,128]{1,0:T(1,128)S(1)} %add.30), channel_id=1, source_target_pairs={{0,256},{128,384},{256,0},{384,128},{1,257},{129,385},{257,1},{385... | collective-permute-start | bytes 1544 | tf_op jit(solution)/shard_map/ppermute | solution.py:292
  86.6 3.0 %collective-permute-done.10 = f32[1,128]{1,0:T(1,128)S(1)} collective-permute-done((f32[1,128]{1,0:T(1,128)S(1)}, f32[1,128]{1,0:T(1,128)S(1)}, u32[]{:S(2)}, u32[]{:S(2)}) %collective-permute-start.10) | collective-permute-done | bytes 544 | tf_op jit(solution)/shard_map/ppermute | solution.py:292
  89.6 5.1 %collective-permute-start.11 = (f32[1,128]{1,0:T(1,128)S(1)}, f32[1,128]{1,0:T(1,128)S(1)}, u32[]{:S(2)}, u32[]{:S(2)}) collective-permute-start(f32[1,128]{1,0:T(1,128)S(1)} %add.31), channel_id=1, source_target_pairs={{0,64},{32,96},{64,0},{96,32},{1,65},{33,97},{65,1},{97,33},{2,66}... | collective-permute-start | bytes 1544 | tf_op jit(solution)/shard_map/ppermute | solution.py:292
  94.7 1.8 %collective-permute-done.11 = f32[1,128]{1,0:T(1,128)S(1)} collective-permute-done((f32[1,128]{1,0:T(1,128)S(1)}, f32[1,128]{1,0:T(1,128)S(1)}, u32[]{:S(2)}, u32[]{:S(2)}) %collective-permute-start.11) | collective-permute-done | bytes 544 | tf_op jit(solution)/shard_map/ppermute | solution.py:292
  96.5 2.5 %all-to-all-done.1.z = s16[16,144,128]{2,1,0:T(8,128)(2,1)S(1)} async-done(((s16[16,144,128]{2,1,0:T(8,128)(2,1)}), s16[16,144,128]{2,1,0:T(8,128)(2,1)S(1)}, u32[]{:S(2)}, u32[]{:S(2)}) %all-to-all-start.1) | async-done | bytes 589856 | tf_op jit(solution)/shard_map/all_to_all | solution.py:290
  99.0 0.6 compact.1
  99.6 6.2 %collective-permute-start.12 = (s16[1552,128]{1,0:T(8,128)(2,1)S(1)}, s16[1552,128]{1,0:T(8,128)(2,1)S(1)}, u32[]{:S(2)}, u32[]{:S(2)}) collective-permute-start(s16[1552,128]{1,0:T(8,128)(2,1)S(1)} %compact.1), channel_id=1, source_target_pairs={{0,0},{32,128},{64,256},{96,384},{128,32},{160,160},{192,288},{224... | collective-permute-start | bytes 1191944 | tf_op jit(solution)/shard_map/ppermute | solution.py:295
  105.8 0.6 broadcast_in_dim.38
  106.4 10.0 %all-to-all-start.2 = ((f32[16,1,128]{2,1,0:T(1,128)}), f32[16,1,128]{2,1,0:T(1,128)S(1)}, u32[]{:S(2)}, u32[]{:S(2)}) async-start(f32[16,1,128]{2,1,0:T(1,128)} %broadcast_in_dim.38), calls=%async_computation.2 | async-start | bytes 16384 | tf_op jit(solution)/shard_map/all_to_all | solution.py:296
  117.0 11.7 %all-to-all-done.2.norm = f32[16,1,128]{2,1,0:T(1,128)S(1)} async-done(((f32[16,1,128]{2,1,0:T(1,128)}), f32[16,1,128]{2,1,0:T(1,128)S(1)}, u32[]{:S(2)}, u32[]{:S(2)}) %all-to-all-start.2) | async-done | bytes 8224 | tf_op jit(solution)/shard_map/all_to_all | solution.py:296
  128.8 0.0 collective-permute-done.12.code.tail
  128.8 0.0 copy-done.1
  128.8 0.0 copy-done.2
  128.8 0.0 copy-done.4
  128.8 3.2 %update.1 = (f32[1536,128]{1,0:T(8,128)}, f32[1536,128]{1,0:T(8,128)}) custom-call(s16[1552,128]{1,0:T(8,128)(2,1)S(1)} %collective-permute-done.12.code.tail, s16[1552,128]{1,0:T(8,128)(2,1)S(1)} %collective-permute-done.12.code.tail, f32[16,1,128]{2,1,0:T(1,128)S(1)} %all-to-all-done.2.norm, f32[1]{0:T(128)S(6)} %copy.14.clip, f32[1536,128]{1,0:T(8,128)S(1)} %copy-done.1, ...), custom_call_target="tpu_custom_call" | custom-call | tf_op jit(solution)/shard_map/update/pallas_call | solution.py:299
  (7 shorter events, 0.0 us)
Async XLA Ops:
  1.9 1.4 %copy-start = (bf16[1,48,16384]{2,1,0:T(8,128)(2,1)S(1)}, bf16[1,48,16384]{2,1,0:T(8,128)(2,1)}, u32[]{:S(2)}) copy-start(bf16[1,48,16384]{2,1,0:T(8,128)(2,1)} %g.1) | copy-start | bytes 4718596
  4.3 36.3 %collective-permute-start = (bf16[2,16,48,128]{3,2,1,0:T(8,128)(2,1)S(1)}, bf16[2,16,48,128]{3,2,1,0:T(8,128)(2,1)S(1)}, u32[]{:S(2)}, u32[]{:S(2)}) collective-permute-start(bf16[2,16,48,128]{3,2,1,0:T(8,128)(2,1)S(1)} %get-tuple-element.27), channel_id=1, source_target_pairs={{0,128},{128,256},{256,384},{384,0},{1,129},{129,257},{257,385},{3... | collective-permute-start | bytes 1179656 | tf_op jit(solution)/shard_map/ppermute | solution.py:263
  7.4 33.2 %collective-permute-start.1 = (bf16[2,16,48,128]{3,2,1,0:T(8,128)(2,1)S(1)}, bf16[2,16,48,128]{3,2,1,0:T(8,128)(2,1)S(1)}, u32[]{:S(2)}, u32[]{:S(2)}) collective-permute-start(bf16[2,16,48,128]{3,2,1,0:T(8,128)(2,1)S(1)} %get-tuple-element.28), channel_id=1, source_target_pairs={{0,256},{128,384},{256,0},{384,128},{1,257},{129,385},{257,1},{385... | collective-permute-start | bytes 1179656 | tf_op jit(solution)/shard_map/ppermute | solution.py:263
  14.0 26.6 %collective-permute-start.2 = (bf16[2,16,48,128]{3,2,1,0:T(8,128)(2,1)S(1)}, bf16[2,16,48,128]{3,2,1,0:T(8,128)(2,1)S(1)}, u32[]{:S(2)}, u32[]{:S(2)}) collective-permute-start(bf16[2,16,48,128]{3,2,1,0:T(8,128)(2,1)S(1)} %get-tuple-element.29), channel_id=1, source_target_pairs={{0,384},{128,0},{256,128},{384,256},{1,385},{129,1},{257,129},{385... | collective-permute-start | bytes 1179656 | tf_op jit(solution)/shard_map/ppermute | solution.py:263
  40.7 19.4 %copy-start.3 = (bf16[128,256]{1,0:T(8,128)(2,1)S(1)}, bf16[128,256]{1,0:T(8,128)(2,1)}, u32[]{:S(2)}) copy-start(bf16[128,256]{1,0:T(8,128)(2,1)} %constant.47.clone.refs_7_.wide) | copy-start | bytes 196612
  40.7 19.4 %copy-start.5 = (bf16[128,256]{1,0:T(8,128)(2,1)S(1)}, bf16[128,256]{1,0:T(8,128)(2,1)}, u32[]{:S(2)}) copy-start(bf16[128,256]{1,0:T(8,128)(2,1)} %constant.46.clone.refs_8_) | copy-start | bytes 196612
  40.8 4.3 %collective-permute-start.4 = (bf16[4,16,48,128]{3,2,1,0:T(8,128)(2,1)S(1)}, bf16[4,16,48,128]{3,2,1,0:T(8,128)(2,1)S(1)}, u32[]{:S(2)}, u32[]{:S(2)}) collective-permute-start(bf16[4,16,48,128]{3,2,1,0:T(8,128)(2,1)S(1)} %give.1), channel_id=1, source_target_pairs={{0,1},{1,0},{2,3},{3,2},{4,5},{5,4},{6,7},{7,6},{8,9},{9,8},{10,11... | collective-permute-start | bytes 2359304 | tf_op jit(solution)/shard_map/ppermute | solution.py:267
  45.7 14.4 %collective-permute-start.6 = (bf16[4,8,64,128]{3,2,1,0:T(8,128)(2,1)S(1)}, bf16[4,8,64,128]{3,2,1,0:T(8,128)(2,1)S(1)}, u32[]{:S(2)}, u32[]{:S(2)}) collective-permute-start(bf16[4,8,64,128]{3,2,1,0:T(8,128)(2,1)S(1)} %get-tuple-element.37), channel_id=1, source_target_pairs={{2,4},{4,2},{10,12},{12,10},{18,20},{20,18},{26,28},{28,26},{3,5},... | collective-permute-start | bytes 1572872 | tf_op jit(solution)/shard_map/ppermute | solution.py:281
  46.4 13.7 %collective-permute-start.5 = (bf16[4,4,96,128]{3,2,1,0:T(8,128)(2,1)S(1)}, bf16[4,4,96,128]{3,2,1,0:T(8,128)(2,1)S(1)}, u32[]{:S(2)}, u32[]{:S(2)}) collective-permute-start(bf16[4,4,96,128]{3,2,1,0:T(8,128)(2,1)S(1)} %get-tuple-element.36), channel_id=1, source_target_pairs={{0,2},{2,0},{4,6},{6,4},{8,10},{10,8},{12,14},{14,12},{16,18},{18,... | collective-permute-start | bytes 1179656 | tf_op jit(solution)/shard_map/ppermute | solution.py:280
  50.7 9.5 %collective-permute-start.3 = (s32[16,128]{1,0:T(8,128)S(1)}, s32[16,128]{1,0:T(8,128)S(1)}, u32[]{:S(2)}, u32[]{:S(2)}) collective-permute-start(s32[16,128]{1,0:T(8,128)S(1)} %bitcast.13), channel_id=1, source_target_pairs={{0,0},{32,128},{64,256},{96,384},{128,32},{160,160},{192,288},{224... | collective-permute-start | bytes 24584 | tf_op jit(solution)/shard_map/ppermute | solution.py:268
  63.9 64.9 %copy-start.1 = (f32[1536,128]{1,0:T(8,128)S(1)}, f32[1536,128]{1,0:T(8,128)}, u32[]{:S(2)}) copy-start(f32[1536,128]{1,0:T(8,128)} %params.1) | copy-start | bytes 2359300
  63.9 64.9 %copy-start.2 = (f32[1536,128]{1,0:T(8,128)S(1)}, f32[1536,128]{1,0:T(8,128)}, u32[]{:S(2)}) copy-start(f32[1536,128]{1,0:T(8,128)} %mom.1) | copy-start | bytes 2359300
  63.9 64.9 %copy-start.4 = (bf16[256,128]{1,0:T(8,128)(2,1)S(1)}, bf16[256,128]{1,0:T(8,128)(2,1)}, u32[]{:S(2)}) copy-start(bf16[256,128]{1,0:T(8,128)(2,1)} %constant.48.clone.tall) | copy-start | bytes 196612
  63.9 35.1 %all-to-all-start.1 = ((s16[16,144,128]{2,1,0:T(8,128)(2,1)}), s16[16,144,128]{2,1,0:T(8,128)(2,1)S(1)}, u32[]{:S(2)}, u32[]{:S(2)}) async-start(s16[16,144,128]{2,1,0:T(8,128)(2,1)} %get-tuple-element.38), calls=%async_computation.1 | async-start | bytes 1179648 | tf_op jit(solution)/shard_map/all_to_all | solution.py:290
  68.8 3.0 %collective-permute-start.7 = (f32[1,128]{1,0:T(1,128)S(1)}, f32[1,128]{1,0:T(1,128)S(1)}, u32[]{:S(2)}, u32[]{:S(2)}) collective-permute-start(f32[1,128]{1,0:T(1,128)S(1)} %get-tuple-element.39), channel_id=1, source_target_pairs={{0,1},{1,0},{2,3},{3,2},{4,5},{5,4},{6,7},{7,6},{8,9},{9,8},{10,11... | collective-permute-start | bytes 1544 | tf_op jit(solution)/shard_map/ppermute | solution.py:292
  71.8 5.4 %collective-permute-start.8 = (f32[1,128]{1,0:T(1,128)S(1)}, f32[1,128]{1,0:T(1,128)S(1)}, u32[]{:S(2)}, u32[]{:S(2)}) collective-permute-start(f32[1,128]{1,0:T(1,128)S(1)} %add.28), channel_id=1, source_target_pairs={{0,128},{128,0},{256,384},{384,256},{1,129},{129,1},{257,385},{385... | collective-permute-start | bytes 1544 | tf_op jit(solution)/shard_map/ppermute | solution.py:292
  77.2 5.4 %collective-permute-start.9 = (f32[1,128]{1,0:T(1,128)S(1)}, f32[1,128]{1,0:T(1,128)S(1)}, u32[]{:S(2)}, u32[]{:S(2)}) collective-permute-start(f32[1,128]{1,0:T(1,128)S(1)} %add.29), channel_id=1, source_target_pairs={{0,32},{32,0},{64,96},{96,64},{1,33},{33,1},{65,97},{97,65},{2,34}... | collective-permute-start | bytes 1544 | tf_op jit(solution)/shard_map/ppermute | solution.py:292
  82.7 6.9 %collective-permute-start.10 = (f32[1,128]{1,0:T(1,128)S(1)}, f32[1,128]{1,0:T(1,128)S(1)}, u32[]{:S(2)}, u32[]{:S(2)}) collective-permute-start(f32[1,128]{1,0:T(1,128)S(1)} %add.30), channel_id=1, source_target_pairs={{0,256},{128,384},{256,0},{384,128},{1,257},{129,385},{257,1},{385... | collective-permute-start | bytes 1544 | tf_op jit(solution)/shard_map/ppermute | solution.py:292
  89.6 6.9 %collective-permute-start.11 = (f32[1,128]{1,0:T(1,128)S(1)}, f32[1,128]{1,0:T(1,128)S(1)}, u32[]{:S(2)}, u32[]{:S(2)}) collective-permute-start(f32[1,128]{1,0:T(1,128)S(1)} %add.31), channel_id=1, source_target_pairs={{0,64},{32,96},{64,0},{96,32},{1,65},{33,97},{65,1},{97,33},{2,66}... | collective-permute-start | bytes 1544 | tf_op jit(solution)/shard_map/ppermute | solution.py:292
  99.6 29.2 %collective-permute-start.12 = (s16[1552,128]{1,0:T(8,128)(2,1)S(1)}, s16[1552,128]{1,0:T(8,128)(2,1)S(1)}, u32[]{:S(2)}, u32[]{:S(2)}) collective-permute-start(s16[1552,128]{1,0:T(8,128)(2,1)S(1)} %compact.1), channel_id=1, source_target_pairs={{0,0},{32,128},{64,256},{96,384},{128,32},{160,160},{192,288},{224... | collective-permute-start | bytes 1191944 | tf_op jit(solution)/shard_map/ppermute | solution.py:295
  106.4 22.4 %all-to-all-start.2 = ((f32[16,1,128]{2,1,0:T(1,128)}), f32[16,1,128]{2,1,0:T(1,128)S(1)}, u32[]{:S(2)}, u32[]{:S(2)}) async-start(f32[16,1,128]{2,1,0:T(1,128)} %broadcast_in_dim.38), calls=%async_computation.2 | async-start | bytes 16384 | tf_op jit(solution)/shard_map/all_to_all | solution.py:296

commit v10 on v8

--- a/solution.py
+++ b/solution.py
@@ -42,16 +42,15 @@
     return hi, (v - hi.astype(F32)).astype(BF16)
 
 
-def times_wide(v, wide):
+def add_halves(both):
+    return both[:, :BS] + both[:, BS:]
+
+
+def left_times(left, v):
     hi, lo = split(v)
-    both = dot(hi, wide)
-    return both[:, :BS] + both[:, BS:] + dot(lo, wide[:, :BS])
-
-
-def tall_times(tall, v):
-    hi, lo = split(v)
-    both = dot(tall, hi)
-    return both[:BS] + both[BS:] + dot(tall[:BS], lo)
+    top = jnp.concatenate([hi, lo], axis=1)
+    low = jnp.concatenate([hi, jnp.zeros_like(lo)], axis=1)
+    return add_halves(dot(left, jnp.concatenate([top, low], axis=0)))
 
 
 def pack_kernel(pos, g, *outs):
@@ -162,17 +161,7 @@
             blk = p - (p > m).astype(jnp.int32)
             total = jnp.zeros((BS, BS), F32)
             for r in range(NX):
-                both = dot(x[r, 4 * k + w], wide[...])
-                hi, lo = split(both[:, :BS] + both[:, BS:])
-                pairs = jnp.concatenate(
-                    [
-                        jnp.concatenate([hi, lo], axis=1),
-                        jnp.concatenate([hi, jnp.zeros_like(lo)], axis=1),
-                    ],
-                    axis=0,
-                )
-                both = dot(left[...], pairs)
-                coef = both[:, :BS] + both[:, BS:]
+                coef = left_times(left[...], add_halves(dot(x[r, 4 * k + w], wide[...])))
                 total += jnp.where(freq <= cut[4 * w + m, 4 * blk + (pos[2] + 4 - r) % 4], coef, 0.0)
             e = exponent(jnp.max(jnp.abs(total), axis=0, keepdims=True))
             code = jnp.clip(jnp.floor(total * jnp.exp2(15.0 - e) + 0.5), -32767.0, 32767.0)
@@ -215,7 +204,7 @@
     norm[...] = jnp.broadcast_to(total[None], norm.shape)
 
 
-def update_kernel(code, tail, norm, clip, params, mom, tall, wide, new_p, new_m):
+def update_kernel(code, tail, norm, clip, params, mom, left, full, new_p, new_m):
     i = pl.program_id(0)
     total = jnp.sum(jnp.sum(norm[...], axis=0), axis=1, keepdims=True)
     factor = jnp.minimum(F32(1.0), clip[0] * F32(math.sqrt(D * FF)) / (jnp.sqrt(total) + F32(EPSILON)))
@@ -225,7 +214,8 @@
         e = jnp.sum(jnp.where(row == 3 * i + n, exps, 0.0), axis=0, keepdims=True)
         d = slice(BS * n, BS * n + BS)
         coef = code[d].astype(jnp.int32).astype(F32) * (jnp.exp2(e - 15.0) * factor)
-        upd = tall_times(tall[...], times_wide(coef, wide[...]))
+        right = add_halves(dot(jnp.concatenate(split(coef), axis=1), full[...]))
+        upd = left_times(left[...], right)
         nm = NESTEROV * mom[d] + upd
         new_m[d] = nm
         new_p[d] = params[d] - OUTER_RATE * (upd + NESTEROV * nm)
@@ -253,8 +243,8 @@
     pos = jnp.stack([z % 4, lax.axis_index("c"), lax.axis_index("x")]).astype(jnp.int32)
     hi, lo = table_parts()
     fwd_wide = jnp.asarray(np.concatenate([hi.T, lo.T], axis=1))
-    inv_wide = jnp.asarray(np.concatenate([hi, lo], axis=1))
-    inv_tall = jnp.asarray(np.concatenate([hi.T, lo.T], axis=0))
+    left = jnp.asarray(np.concatenate([hi, lo], axis=1))
+    inv_full = jnp.asarray(np.block([[hi, lo], [hi, np.zeros_like(lo)]]))
     rows = pseudo_grads.shape[1]
     swap = [(NY * i + j, NX * j + i) for i in range(NX) for j in range(NY)]
     shape = jax.ShapeDtypeStruct
@@ -265,7 +255,7 @@
     hit = picks[:, :, None] == jnp.arange(BPO, dtype=jnp.int32)
     cut = jnp.max(jnp.where(hit, cuts[:, :, None], -1), axis=1)
     cut = jnp.broadcast_to(cut.T.reshape(4, 1, BPO), (4, 4, BPO)).reshape(NZ, 1, BPO)
-    cut = jnp.pad(cut, ((0, 0), (0, 0), (0, BS - BPO)))
+    cut = jnp.broadcast_to(jnp.pad(cut, ((0, 0), (0, 0), (0, BS - BPO))), (NZ, 16, BS))
     cut, pseudo_grads = lax.optimization_barrier((cut, pseudo_grads))
     cut = lax.all_to_all(cut, "z", 0, 0, tiled=True)[:, 0]
 
@@ -294,7 +284,7 @@
     coded = call(
         forward_kernel,
         shape((NZ, BS + TAIL, BS), jnp.int16),
-        (pos, cut, *spread, a, b, inv_wide, fwd_wide),
+        (pos, cut, *spread, a, b, left, fwd_wide),
         "forward",
         [pltpu.VMEM((NX, BPO, BS, BS), BF16), pltpu.VMEM((NZ, BS), F32)],
     )
@@ -326,7 +316,7 @@
         out_specs=(tile, tile),
         compiler_params=BIG,
         name="update",
-    )(coded, coded, norm, clip_level, outer_params, momentum, inv_tall, inv_wide)
+    )(coded, coded, norm, clip_level, outer_params, momentum, fwd_wide, inv_full)
 
 
 def solution(mesh):

time: 131 us -> 143 us (1.092)
  blocking collectives: 61.2 us -> 42.1 us
  starting transfers between devices: 35.6 us -> 52.2 us
  waiting for transfers between devices: 20.3 us -> 33.6 us
    all_to_all x1 -> x0, blocking collectives: 26 us -> none  [per_device(): cut = lax.all_to_all(cut, 'z', 0, 0, tiled=True)[:, 0]]
    all_to_all x0 -> x1, starting transfers between devices: none -> 15.7 us  [per_device(): cut = lax.all_to_all(cut, 'z', 0, 0, tiled=True)[:, 0]]
    ppermute x3, waiting for transfers between devices: 0.01 us -> 13.5 us  [per_device(): lax.ppermute(packed[n], 'x', [(i, (i + n) % NX) for i in range(NX)])]
    all_to_all x1, blocking collectives: 35.2 us -> 42.1 us  [per_device(): coded = lax.all_to_all(coded, 'z', 0, 0, tiled=True)]
    ppermute x1, starting transfers between devices: 3.68 us -> 5.69 us  [per_device(): a = lax.ppermute(a, 'z', pair_a)]
  transfers between devices with their start and end apart: 9 -> 10, of which waited for: 3 -> 6; matrix products, arithmetic and copies ran while one was open for 0% -> 0% of each run, Pallas kernels for 0% -> 1%
where the time goes in v10:
time: 143 us; the launch traced here: 142 us
  starting transfers between devices  52.2 us (37%)
  blocking collectives  42.1 us (29%)
  waiting for transfers between devices  33.6 us (23%)
  Pallas kernels  8.84 us (6%)
  local copies, waits for them, and re-layouts  3.22 us (2%)
  between operations  1.49 us (1%)
    all_to_all x1, blocking collectives, per_device(): coded = lax.all_to_all(coded, 'z', 0, 0, tiled=True)  42.1 us
    all_to_all x1, starting transfers between devices, per_device(): cut = lax.all_to_all(cut, 'z', 0, 0, tiled=True)[:, 0]  15.7 us
    all_to_all x1, starting transfers between devices, per_device(): norm = lax.all_to_all(norm, ('x', 'y', 'c'), 0, 0, tiled=True)  14.6 us
    ppermute x3, waiting for transfers between devices, per_device(): lax.ppermute(packed[n], 'x', [(i, (i + n) % NX) for i in range(NX)])  13.5 us
    ppermute x3, starting transfers between devices, per_device(): lax.ppermute(packed[n], 'x', [(i, (i + n) % NX) for i in range(NX)])  10.5 us
    all_to_all x1, waiting for transfers between devices, per_device(): norm = lax.all_to_all(norm, ('x', 'y', 'c'), 0, 0, tiled=True)  10.1 us
    ppermute x1, waiting for transfers between devices, per_device(): a = lax.ppermute(a, 'z', pair_a)  8.17 us
    pallas_call x5, Pallas kernels, call(): pl.pallas_call(kernel, out_shape=out_shape, in_specs=[SMEM if i.dtype ==...  5.74 us
  transfers between devices with their start and end apart: 10, of which 6 were waited for; matrix products, arithmetic and copies ran while one was open for 0% of the time, Pallas kernels for 1%

profile of v10, /device:TPU:1, one launch (start us, length us, event | category | flops | bytes accessed | tf_op | source)
XLA Modules:
  0.0 141.7 jit_solution(11073824364630454498)
XLA Ops:
  0.6 0.7 constant_dynamic-slice_fusion
  1.4 0.1 copy.12
  1.5 0.1 copy.13
  1.5 0.1 select_reduce_fusion
  1.6 0.1 copy.14
  1.7 0.1 broadcast_in_dim.34
  1.8 0.7 broadcast_in_dim.37
  2.5 15.7 %all-to-all-start = ((s32[16,16,128]{2,1,0:T(8,128)}), s32[16,16,128]{2,1,0:T(8,128)S(1)}, u32[]{:S(2)}, u32[]{:S(2)}) async-start(s32[16,16,128]{2,1,0:T(8,128)} %broadcast_in_dim.37), calls=%async_computation | async-start | bytes 262144 | tf_op jit(solution)/shard_map/all_to_all | solution.py:260
  18.3 0.1 pad_add_fusion.pos
  18.3 0.0 copy-start
  18.3 1.4 copy-done
  19.8 1.0 pack.1
  20.7 3.1 %collective-permute-start = (bf16[2,16,48,128]{3,2,1,0:T(8,128)(2,1)S(1)}, bf16[2,16,48,128]{3,2,1,0:T(8,128)(2,1)S(1)}, u32[]{:S(2)}, u32[]{:S(2)}) collective-permute-start(bf16[2,16,48,128]{3,2,1,0:T(8,128)(2,1)S(1)} %get-tuple-element.19), channel_id=1, source_target_pairs={{0,128},{128,256},{256,384},{384,0},{1,129},{129,257},{257,385},{3... | collective-permute-start | bytes 1179656 | tf_op jit(solution)/shard_map/ppermute | solution.py:264
  23.9 4.4 %collective-permute-start.1 = (bf16[2,16,48,128]{3,2,1,0:T(8,128)(2,1)S(1)}, bf16[2,16,48,128]{3,2,1,0:T(8,128)(2,1)S(1)}, u32[]{:S(2)}, u32[]{:S(2)}) collective-permute-start(bf16[2,16,48,128]{3,2,1,0:T(8,128)(2,1)S(1)} %get-tuple-element.20), channel_id=1, source_target_pairs={{0,256},{128,384},{256,0},{384,128},{1,257},{129,385},{257,1},{385... | collective-permute-start | bytes 1179656 | tf_op jit(solution)/shard_map/ppermute | solution.py:264
  28.2 3.1 %collective-permute-start.2 = (bf16[2,16,48,128]{3,2,1,0:T(8,128)(2,1)S(1)}, bf16[2,16,48,128]{3,2,1,0:T(8,128)(2,1)S(1)}, u32[]{:S(2)}, u32[]{:S(2)}) collective-permute-start(bf16[2,16,48,128]{3,2,1,0:T(8,128)(2,1)S(1)} %get-tuple-element.21), channel_id=1, source_target_pairs={{0,384},{128,0},{256,128},{384,256},{1,385},{129,1},{257,129},{385... | collective-permute-start | bytes 1179656 | tf_op jit(solution)/shard_map/ppermute | solution.py:264
  31.3 0.0 all-to-all-done
  31.3 2.2 %collective-permute-done.refs_1_ = bf16[2,16,48,128]{3,2,1,0:T(8,128)(2,1)S(1)} collective-permute-done((bf16[2,16,48,128]{3,2,1,0:T(8,128)(2,1)S(1)}, bf16[2,16,48,128]{3,2,1,0:T(8,128)(2,1)S(1)}, u32[]{:S(2)}, u32[]{:S(2)}) %collective-permute-start) | collective-permute-done | bytes 393248 | tf_op jit(solution)/shard_map/ppermute | solution.py:264
  33.5 9.4 %collective-permute-done.1.refs_2_ = bf16[2,16,48,128]{3,2,1,0:T(8,128)(2,1)S(1)} collective-permute-done((bf16[2,16,48,128]{3,2,1,0:T(8,128)(2,1)S(1)}, bf16[2,16,48,128]{3,2,1,0:T(8,128)(2,1)S(1)}, u32[]{:S(2)}, u32[]{:S(2)}) %collective-permute-start.1) | collective-permute-done | bytes 393248 | tf_op jit(solution)/shard_map/ppermute | solution.py:264
  42.9 1.9 %collective-permute-done.2.refs_3_ = bf16[2,16,48,128]{3,2,1,0:T(8,128)(2,1)S(1)} collective-permute-done((bf16[2,16,48,128]{3,2,1,0:T(8,128)(2,1)S(1)}, bf16[2,16,48,128]{3,2,1,0:T(8,128)(2,1)S(1)}, u32[]{:S(2)}, u32[]{:S(2)}) %collective-permute-start.2) | collective-permute-done | bytes 393248 | tf_op jit(solution)/shard_map/ppermute | solution.py:264
  44.8 0.1 give.1
  44.8 0.0 copy-start.3
  44.8 0.0 copy-start.5
  44.9 3.6 %collective-permute-start.4 = (bf16[4,16,48,128]{3,2,1,0:T(8,128)(2,1)S(1)}, bf16[4,16,48,128]{3,2,1,0:T(8,128)(2,1)S(1)}, u32[]{:S(2)}, u32[]{:S(2)}) collective-permute-start(bf16[4,16,48,128]{3,2,1,0:T(8,128)(2,1)S(1)} %give.1), channel_id=1, source_target_pairs={{0,1},{1,0},{2,3},{3,2},{4,5},{5,4},{6,7},{7,6},{8,9},{9,8},{10,11... | collective-permute-start | bytes 2359304 | tf_op jit(solution)/shard_map/ppermute | solution.py:268
  48.5 1.9 %collective-permute-done.4.refs_4_ = bf16[4,16,48,128]{3,2,1,0:T(8,128)(2,1)S(1)} collective-permute-done((bf16[4,16,48,128]{3,2,1,0:T(8,128)(2,1)S(1)}, bf16[4,16,48,128]{3,2,1,0:T(8,128)(2,1)S(1)}, u32[]{:S(2)}, u32[]{:S(2)}) %collective-permute-start.4) | collective-permute-done | bytes 786464 | tf_op jit(solution)/shard_map/ppermute | solution.py:268
  50.3 0.6 exchange.1
  51.0 0.7 collective-permute-start.6
  51.7 5.7 %collective-permute-start.5 = (bf16[4,4,96,128]{3,2,1,0:T(8,128)(2,1)S(1)}, bf16[4,4,96,128]{3,2,1,0:T(8,128)(2,1)S(1)}, u32[]{:S(2)}, u32[]{:S(2)}) collective-permute-start(bf16[4,4,96,128]{3,2,1,0:T(8,128)(2,1)S(1)} %get-tuple-element.28), channel_id=1, source_target_pairs={{0,2},{2,0},{4,6},{6,4},{8,10},{10,8},{12,14},{14,12},{16,18},{18,... | collective-permute-start | bytes 1179656 | tf_op jit(solution)/shard_map/ppermute | solution.py:281
  57.4 0.7 collective-permute-start.3
  58.0 0.0 collective-permute-done.3.cut
  58.1 8.2 %collective-permute-done.5.refs_5_ = bf16[4,4,96,128]{3,2,1,0:T(8,128)(2,1)S(1)} collective-permute-done((bf16[4,4,96,128]{3,2,1,0:T(8,128)(2,1)S(1)}, bf16[4,4,96,128]{3,2,1,0:T(8,128)(2,1)S(1)}, u32[]{:S(2)}, u32[]{:S(2)}) %collective-permute-start.5) | collective-permute-done | bytes 393248 | tf_op jit(solution)/shard_map/ppermute | solution.py:281
  66.2 0.0 collective-permute-done.6.refs_6_
  66.2 0.0 copy-done.3
  66.2 0.0 copy-done.5
  66.2 2.9 %forward.1 = s16[16,144,128]{2,1,0:T(8,128)(2,1)S(1)} custom-call(s32[3]{0:T(128)S(1)} %pad_add_fusion.pos, s32[16,128]{1,0:T(8,128)S(1)} %collective-permute-done.3.cut, bf16[2,16,48,128]{3,2,1,0:T(8,128)(2,1)S(1)} %get-tuple-element.24.refs_0_, bf16[2,16,48,128]{3,2,1,0:T(8,128)(2,1)S(1)} %collective-permute-done.refs_1_, ...), custom_call_target="tpu_custom_call" | custom-call | tf_op jit(solution)/shard_map/forward/pallas_call | solution.py:230
  69.2 0.0 copy-start.1
  69.2 0.0 copy-start.2
  69.2 0.0 copy-start.4
  69.2 42.1 %all_to_all.15.z = s16[16,144,128]{2,1,0:T(8,128)(2,1)S(1)} all-to-all(s16[16,144,128]{2,1,0:T(8,128)(2,1)S(1)} %forward.1), channel_id=1, replica_groups=mesh['x'=4,'y'=4,'z'=16,'c'=2] {'z'}, dimensions={0} | all-to-all | bytes 1179648 | tf_op jit(solution)/shard_map/all_to_all | solution.py:291
  111.3 1.2 compact.1
  112.5 0.7 collective-permute-start.7
  113.2 14.6 %all-to-all-start.2 = ((f32[32,1,128]{2,1,0:T(1,128)}), f32[32,1,128]{2,1,0:T(1,128)S(1)}, u32[]{:S(2)}, u32[]{:S(2)}) async-start(f32[32,1,128]{2,1,0:T(1,128)} %get-tuple-element.31), calls=%async_computation.2 | async-start | bytes 32768 | tf_op jit(solution)/shard_map/all_to_all | solution.py:299
  128.5 10.1 %all-to-all-done.2.norm = f32[32,1,128]{2,1,0:T(1,128)S(1)} async-done(((f32[32,1,128]{2,1,0:T(1,128)}), f32[32,1,128]{2,1,0:T(1,128)S(1)}, u32[]{:S(2)}, u32[]{:S(2)}) %all-to-all-start.2) | async-done | bytes 16416 | tf_op jit(solution)/shard_map/all_to_all | solution.py:299
  138.6 0.0 collective-permute-done.7.code.tail
  138.6 0.0 copy-done.1
  138.6 0.0 copy-done.2
  138.6 0.0 copy-done.4
  138.6 3.1 %update.1 = (f32[1536,128]{1,0:T(8,128)}, f32[1536,128]{1,0:T(8,128)}) custom-call(s16[1552,128]{1,0:T(8,128)(2,1)S(1)} %collective-permute-done.7.code.tail, s16[1552,128]{1,0:T(8,128)(2,1)S(1)} %collective-permute-done.7.code.tail, f32[32,1,128]{2,1,0:T(1,128)S(1)} %all-to-all-done.2.norm, f32[1]{0:T(128)S(6)} %copy.17.clip, f32[1536,128]{1,0:T(8,128)S(1)} %copy-done.1, ...), custom_call_target="tpu_custom_call" | custom-call | tf_op jit(solution)/shard_map/update/pallas_call | solution.py:302
  (3 shorter events, 0.0 us)
Async XLA Ops:
  2.5 28.8 %all-to-all-start = ((s32[16,16,128]{2,1,0:T(8,128)}), s32[16,16,128]{2,1,0:T(8,128)S(1)}, u32[]{:S(2)}, u32[]{:S(2)}) async-start(s32[16,16,128]{2,1,0:T(8,128)} %broadcast_in_dim.37), calls=%async_computation | async-start | bytes 262144 | tf_op jit(solution)/shard_map/all_to_all | solution.py:260
  18.3 1.4 copy-start
  20.7 12.8 %collective-permute-start = (bf16[2,16,48,128]{3,2,1,0:T(8,128)(2,1)S(1)}, bf16[2,16,48,128]{3,2,1,0:T(8,128)(2,1)S(1)}, u32[]{:S(2)}, u32[]{:S(2)}) collective-permute-start(bf16[2,16,48,128]{3,2,1,0:T(8,128)(2,1)S(1)} %get-tuple-element.19), channel_id=1, source_target_pairs={{0,128},{128,256},{256,384},{384,0},{1,129},{129,257},{257,385},{3... | collective-permute-start | bytes 1179656 | tf_op jit(solution)/shard_map/ppermute | solution.py:264
  23.9 19.1 %collective-permute-start.1 = (bf16[2,16,48,128]{3,2,1,0:T(8,128)(2,1)S(1)}, bf16[2,16,48,128]{3,2,1,0:T(8,128)(2,1)S(1)}, u32[]{:S(2)}, u32[]{:S(2)}) collective-permute-start(bf16[2,16,48,128]{3,2,1,0:T(8,128)(2,1)S(1)} %get-tuple-element.20), channel_id=1, source_target_pairs={{0,256},{128,384},{256,0},{384,128},{1,257},{129,385},{257,1},{385... | collective-permute-start | bytes 1179656 | tf_op jit(solution)/shard_map/ppermute | solution.py:264
  28.2 16.5 %collective-permute-start.2 = (bf16[2,16,48,128]{3,2,1,0:T(8,128)(2,1)S(1)}, bf16[2,16,48,128]{3,2,1,0:T(8,128)(2,1)S(1)}, u32[]{:S(2)}, u32[]{:S(2)}) collective-permute-start(bf16[2,16,48,128]{3,2,1,0:T(8,128)(2,1)S(1)} %get-tuple-element.21), channel_id=1, source_target_pairs={{0,384},{128,0},{256,128},{384,256},{1,385},{129,1},{257,129},{385... | collective-permute-start | bytes 1179656 | tf_op jit(solution)/shard_map/ppermute | solution.py:264
  44.8 21.4 %copy-start.3 = (bf16[128,256]{1,0:T(8,128)(2,1)S(1)}, bf16[128,256]{1,0:T(8,128)(2,1)}, u32[]{:S(2)}) copy-start(bf16[128,256]{1,0:T(8,128)(2,1)} %constant.46.clone.refs_8_.left) | copy-start | bytes 196612
  44.8 21.4 %copy-start.5 = (bf16[128,256]{1,0:T(8,128)(2,1)S(1)}, bf16[128,256]{1,0:T(8,128)(2,1)}, u32[]{:S(2)}) copy-start(bf16[128,256]{1,0:T(8,128)(2,1)} %constant.47.clone.refs_7_) | copy-start | bytes 196612
  44.9 5.5 %collective-permute-start.4 = (bf16[4,16,48,128]{3,2,1,0:T(8,128)(2,1)S(1)}, bf16[4,16,48,128]{3,2,1,0:T(8,128)(2,1)S(1)}, u32[]{:S(2)}, u32[]{:S(2)}) collective-permute-start(bf16[4,16,48,128]{3,2,1,0:T(8,128)(2,1)S(1)} %give.1), channel_id=1, source_target_pairs={{0,1},{1,0},{2,3},{3,2},{4,5},{5,4},{6,7},{7,6},{8,9},{9,8},{10,11... | collective-permute-start | bytes 2359304 | tf_op jit(solution)/shard_map/ppermute | solution.py:268
  51.0 15.3 %collective-permute-start.6 = (bf16[4,8,64,128]{3,2,1,0:T(8,128)(2,1)S(1)}, bf16[4,8,64,128]{3,2,1,0:T(8,128)(2,1)S(1)}, u32[]{:S(2)}, u32[]{:S(2)}) collective-permute-start(bf16[4,8,64,128]{3,2,1,0:T(8,128)(2,1)S(1)} %get-tuple-element.29), channel_id=1, source_target_pairs={{2,4},{4,2},{10,12},{12,10},{18,20},{20,18},{26,28},{28,26},{3,5},... | collective-permute-start | bytes 1572872 | tf_op jit(solution)/shard_map/ppermute | solution.py:282
  51.7 14.6 %collective-permute-start.5 = (bf16[4,4,96,128]{3,2,1,0:T(8,128)(2,1)S(1)}, bf16[4,4,96,128]{3,2,1,0:T(8,128)(2,1)S(1)}, u32[]{:S(2)}, u32[]{:S(2)}) collective-permute-start(bf16[4,4,96,128]{3,2,1,0:T(8,128)(2,1)S(1)} %get-tuple-element.28), channel_id=1, source_target_pairs={{0,2},{2,0},{4,6},{6,4},{8,10},{10,8},{12,14},{14,12},{16,18},{18,... | collective-permute-start | bytes 1179656 | tf_op jit(solution)/shard_map/ppermute | solution.py:281
  57.4 0.7 collective-permute-start.3
  69.2 69.4 %copy-start.1 = (f32[1536,128]{1,0:T(8,128)S(1)}, f32[1536,128]{1,0:T(8,128)}, u32[]{:S(2)}) copy-start(f32[1536,128]{1,0:T(8,128)} %params.1) | copy-start | bytes 2359300
  69.2 69.4 %copy-start.2 = (f32[1536,128]{1,0:T(8,128)S(1)}, f32[1536,128]{1,0:T(8,128)}, u32[]{:S(2)}) copy-start(f32[1536,128]{1,0:T(8,128)} %mom.1) | copy-start | bytes 2359300
  69.2 69.4 %copy-start.4 = (bf16[256,256]{1,0:T(8,128)(2,1)S(1)}, bf16[256,256]{1,0:T(8,128)(2,1)}, u32[]{:S(2)}) copy-start(bf16[256,256]{1,0:T(8,128)(2,1)} %constant.48.clone.full) | copy-start | bytes 393220
  112.5 26.1 %collective-permute-start.7 = (s16[1552,128]{1,0:T(8,128)(2,1)S(1)}, s16[1552,128]{1,0:T(8,128)(2,1)S(1)}, u32[]{:S(2)}, u32[]{:S(2)}) collective-permute-start(s16[1552,128]{1,0:T(8,128)(2,1)S(1)} %get-tuple-element.30), channel_id=1, source_target_pairs={{0,0},{32,128},{64,256},{96,384},{128,32},{160,160},{192,288},{224... | collective-permute-start | bytes 1191944 | tf_op jit(solution)/shard_map/ppermute | solution.py:298
  113.2 25.4 %all-to-all-start.2 = ((f32[32,1,128]{2,1,0:T(1,128)}), f32[32,1,128]{2,1,0:T(1,128)S(1)}, u32[]{:S(2)}, u32[]{:S(2)}) async-start(f32[32,1,128]{2,1,0:T(1,128)} %get-tuple-element.31), calls=%async_computation.2 | async-start | bytes 32768 | tf_op jit(solution)/shard_map/all_to_all | solution.py:299

commit v11 on v8

--- a/solution.py
+++ b/solution.py
@@ -54,8 +54,17 @@
     return both[:BS] + both[BS:] + dot(tall[:BS], lo)
 
 
-def pack_kernel(pos, g, *outs):
+def pack_kernel(pos, picks, cuts, g, *outs):
     c, x = pos[1], pos[2]
+    lane = lax.broadcasted_iota(jnp.int32, (1, BS), 1)
+    for grp in range(4):
+        row = jnp.full((1, BS), -1, jnp.int32)
+        for r in range(NX):
+            for s in range(picks.shape[3]):
+                at = 4 * picks[r, 0, x, s] + r - 12 * grp
+                row = jnp.where(lane == at, jnp.maximum(row, cuts[r, 0, x, s]), row)
+        for n in range(4):
+            outs[NX][4 * grp + n] = row
     for s in range(NX):
         for half, core in enumerate((c, 1 - c)):
             base = NZ * NC * ((x + s) % 4) + core
@@ -259,17 +268,13 @@
     swap = [(NY * i + j, NX * j + i) for i in range(NX) for j in range(NY)]
     shape = jax.ShapeDtypeStruct
 
-    picks, cuts = (
-        lax.dynamic_index_in_dim(v[:, 0], lax.axis_index("x"), 1, keepdims=False) for v in (block_picks, cutoffs)
+    *packed, cut = call(
+        pack_kernel,
+        [shape((NC, NZ, rows, BS), BF16)] * NX + [shape((NZ, 1, BS), jnp.int32)],
+        (pos, block_picks, cutoffs, pseudo_grads),
+        "pack",
     )
-    hit = picks[:, :, None] == jnp.arange(BPO, dtype=jnp.int32)
-    cut = jnp.max(jnp.where(hit, cuts[:, :, None], -1), axis=1)
-    cut = jnp.broadcast_to(cut.T.reshape(4, 1, BPO), (4, 4, BPO)).reshape(NZ, 1, BPO)
-    cut = jnp.pad(cut, ((0, 0), (0, 0), (0, BS - BPO)))
-    cut, pseudo_grads = lax.optimization_barrier((cut, pseudo_grads))
     cut = lax.all_to_all(cut, "z", 0, 0, tiled=True)[:, 0]
-
-    packed = call(pack_kernel, [shape((NC, NZ, rows, BS), BF16)] * NX, (pos, pseudo_grads), "pack")
     spread = [packed[0]] + [
         lax.ppermute(packed[n], "x", [(i, (i + n) % NX) for i in range(NX)]) for n in range(1, NX)
     ]

time: 131 us -> 132 us (level)
    unnamed x12 -> x16, local copies, waits for them, and re-layouts: 1.44 us -> 2.84 us
where the time goes in v11:
time: 132 us; the launch traced here: 131 us
  blocking collectives  61.2 us (46%)
  starting transfers between devices  35.6 us (27%)
  waiting for transfers between devices  20.3 us (15%)
  Pallas kernels  9.37 us (7%)
  local copies, waits for them, and re-layouts  2.84 us (2%)
  between operations  1.47 us (1%)
    all_to_all x1, blocking collectives, per_device(): coded = lax.all_to_all(coded, 'z', 0, 0, tiled=True)  35.2 us
    all_to_all x1, blocking collectives, per_device(): cut = lax.all_to_all(cut, 'z', 0, 0, tiled=True)[:, 0]  26 us
    all_to_all x1, starting transfers between devices, per_device(): norm = lax.all_to_all(norm, ('x', 'y', 'c'), 0, 0, tiled=True)  13.6 us
    ppermute x3, starting transfers between devices, per_device(): lax.ppermute(packed[n], 'x', [(i, (i + n) % NX) for i in range(NX)])  11.4 us
    all_to_all x1, waiting for transfers between devices, per_device(): norm = lax.all_to_all(norm, ('x', 'y', 'c'), 0, 0, tiled=True)  10.2 us
    ppermute x1, waiting for transfers between devices, per_device(): a = lax.ppermute(a, 'z', pair_a)  8.17 us
    pallas_call x5, Pallas kernels, call(): pl.pallas_call(kernel, out_shape=out_shape, in_specs=[SMEM if i.dtype ==...  6.14 us
    ppermute x1, starting transfers between devices, per_device(): spread.append(lax.ppermute(give, 'c', [(0, 1), (1, 0)]))  4.98 us
  transfers between devices with their start and end apart: 9, of which 3 were waited for; matrix products, arithmetic and copies ran while one was open for 0% of the time, Pallas kernels for 0%

profile of v11, /device:TPU:1, one launch (start us, length us, event | category | flops | bytes accessed | tf_op | source)
XLA Modules:
  0.0 130.9 jit_solution(8054254145966710506)
XLA Ops:
  0.6 0.1 pad_add_fusion.pos
  0.7 0.0 copy-start
  0.7 1.4 %copy-done = bf16[1,48,16384]{2,1,0:T(8,128)(2,1)S(1)} copy-done((bf16[1,48,16384]{2,1,0:T(8,128)(2,1)S(1)}, bf16[1,48,16384]{2,1,0:T(8,128)(2,1)}, u32[]{:S(2)}) %copy-start) | copy-done | bytes 1572888
  2.1 0.0 copy-start.6
  2.1 0.7 copy-done.6
  2.8 0.0 copy-start.7
  2.8 0.7 copy-done.7
  3.5 1.4 %pack.1 = (bf16[2,16,48,128]{3,2,1,0:T(8,128)(2,1)S(1)}, bf16[2,16,48,128]{3,2,1,0:T(8,128)(2,1)S(1)}, bf16[2,16,48,128]{3,2,1,0:T(8,128)(2,1)S(1)}, bf16[2,16,4...) custom-call(s32[3]{0:T(128)S(1)} %pad_add_fusion.pos, s32[4,1,4,6]{3,2,1,0:T(4,128)S(1)} %copy-done.6, ...), custom_call_target="tpu_custom_call" | custom-call | tf_op jit(solution)/shard_map/pack/pallas_call | solution.py:249
  4.9 3.9 %collective-permute-start = (bf16[2,16,48,128]{3,2,1,0:T(8,128)(2,1)S(1)}, bf16[2,16,48,128]{3,2,1,0:T(8,128)(2,1)S(1)}, u32[]{:S(2)}, u32[]{:S(2)}) collective-permute-start(bf16[2,16,48,128]{3,2,1,0:T(8,128)(2,1)S(1)} %get-tuple-element.17), channel_id=1, source_target_pairs={{0,128},{128,256},{256,384},{384,0},{1,129},{129,257},{257,385},{3... | collective-permute-start | bytes 1179656 | tf_op jit(solution)/shard_map/ppermute | solution.py:279
  8.9 4.4 %collective-permute-start.1 = (bf16[2,16,48,128]{3,2,1,0:T(8,128)(2,1)S(1)}, bf16[2,16,48,128]{3,2,1,0:T(8,128)(2,1)S(1)}, u32[]{:S(2)}, u32[]{:S(2)}) collective-permute-start(bf16[2,16,48,128]{3,2,1,0:T(8,128)(2,1)S(1)} %get-tuple-element.18), channel_id=1, source_target_pairs={{0,256},{128,384},{256,0},{384,128},{1,257},{129,385},{257,1},{385... | collective-permute-start | bytes 1179656 | tf_op jit(solution)/shard_map/ppermute | solution.py:279
  13.2 3.1 %collective-permute-start.2 = (bf16[2,16,48,128]{3,2,1,0:T(8,128)(2,1)S(1)}, bf16[2,16,48,128]{3,2,1,0:T(8,128)(2,1)S(1)}, u32[]{:S(2)}, u32[]{:S(2)}) collective-permute-start(bf16[2,16,48,128]{3,2,1,0:T(8,128)(2,1)S(1)} %get-tuple-element.19), channel_id=1, source_target_pairs={{0,384},{128,0},{256,128},{384,256},{1,385},{129,1},{257,129},{385... | collective-permute-start | bytes 1179656 | tf_op jit(solution)/shard_map/ppermute | solution.py:279
  16.3 26.0 %all_to_all.15 = s32[16,1,128]{2,1,0:T(1,128)S(1)} all-to-all(s32[16,1,128]{2,1,0:T(1,128)S(1)} %get-tuple-element.20), channel_id=1, replica_groups=mesh['x'=4,'y'=4,'z'=16,'c'=2] {'z'}, dimensions={0} | all-to-all | bytes 16384 | tf_op jit(solution)/shard_map/all_to_all | solution.py:277
  42.3 0.0 collective-permute-done.refs_1_
  42.3 0.0 collective-permute-done.1.refs_2_
  42.3 0.0 collective-permute-done.2.refs_3_
  42.3 0.1 give.1
  42.4 0.0 copy-start.3
  42.4 0.0 copy-start.4
  42.4 5.0 %collective-permute-start.4 = (bf16[4,16,48,128]{3,2,1,0:T(8,128)(2,1)S(1)}, bf16[4,16,48,128]{3,2,1,0:T(8,128)(2,1)S(1)}, u32[]{:S(2)}, u32[]{:S(2)}) collective-permute-start(bf16[4,16,48,128]{3,2,1,0:T(8,128)(2,1)S(1)} %give.1), channel_id=1, source_target_pairs={{0,1},{1,0},{2,3},{3,2},{4,5},{5,4},{6,7},{7,6},{8,9},{9,8},{10,11... | collective-permute-start | bytes 2359304 | tf_op jit(solution)/shard_map/ppermute | solution.py:283
  47.4 1.9 %collective-permute-done.4.refs_4_ = bf16[4,16,48,128]{3,2,1,0:T(8,128)(2,1)S(1)} collective-permute-done((bf16[4,16,48,128]{3,2,1,0:T(8,128)(2,1)S(1)}, bf16[4,16,48,128]{3,2,1,0:T(8,128)(2,1)S(1)}, u32[]{:S(2)}, u32[]{:S(2)}) %collective-permute-start.4) | collective-permute-done | bytes 786464 | tf_op jit(solution)/shard_map/ppermute | solution.py:283
  49.3 0.6 exchange.1
  49.9 0.7 collective-permute-start.6
  50.6 3.7 %collective-permute-start.5 = (bf16[4,4,96,128]{3,2,1,0:T(8,128)(2,1)S(1)}, bf16[4,4,96,128]{3,2,1,0:T(8,128)(2,1)S(1)}, u32[]{:S(2)}, u32[]{:S(2)}) collective-permute-start(bf16[4,4,96,128]{3,2,1,0:T(8,128)(2,1)S(1)} %get-tuple-element.26), channel_id=1, source_target_pairs={{0,2},{2,0},{4,6},{6,4},{8,10},{10,8},{12,14},{14,12},{16,18},{18,... | collective-permute-start | bytes 1179656 | tf_op jit(solution)/shard_map/ppermute | solution.py:296
  54.3 0.7 collective-permute-start.3
  55.0 0.0 collective-permute-done.3.cut
  55.0 8.2 %collective-permute-done.5.refs_5_ = bf16[4,4,96,128]{3,2,1,0:T(8,128)(2,1)S(1)} collective-permute-done((bf16[4,4,96,128]{3,2,1,0:T(8,128)(2,1)S(1)}, bf16[4,4,96,128]{3,2,1,0:T(8,128)(2,1)S(1)}, u32[]{:S(2)}, u32[]{:S(2)}) %collective-permute-start.5) | collective-permute-done | bytes 393248 | tf_op jit(solution)/shard_map/ppermute | solution.py:296
  63.2 0.0 collective-permute-done.6.refs_6_
  63.2 0.0 copy-done.3
  63.2 0.0 copy-done.4
  63.2 2.9 %forward.1 = s16[16,144,128]{2,1,0:T(8,128)(2,1)S(1)} custom-call(s32[3]{0:T(128)S(1)} %pad_add_fusion.pos, s32[16,128]{1,0:T(8,128)S(1)} %collective-permute-done.3.cut, bf16[2,16,48,128]{3,2,1,0:T(8,128)(2,1)S(1)} %get-tuple-element.22.refs_0_, bf16[2,16,48,128]{3,2,1,0:T(8,128)(2,1)S(1)} %collective-permute-done.refs_1_, ...), custom_call_target="tpu_custom_call" | custom-call | tf_op jit(solution)/shard_map/forward/pallas_call | solution.py:249
  66.1 0.0 copy-start.1
  66.1 0.0 copy-start.2
  66.1 0.0 copy-start.5
  66.1 35.2 %all_to_all.16.z = s16[16,144,128]{2,1,0:T(8,128)(2,1)S(1)} all-to-all(s16[16,144,128]{2,1,0:T(8,128)(2,1)S(1)} %forward.1), channel_id=1, replica_groups=mesh['x'=4,'y'=4,'z'=16,'c'=2] {'z'}, dimensions={0} | all-to-all | bytes 1179648 | tf_op jit(solution)/shard_map/all_to_all | solution.py:306
  101.3 1.2 compact.1
  102.5 0.7 collective-permute-start.7
  103.2 13.6 %all-to-all-start.2 = ((f32[32,1,128]{2,1,0:T(1,128)}), f32[32,1,128]{2,1,0:T(1,128)S(1)}, u32[]{:S(2)}, u32[]{:S(2)}) async-start(f32[32,1,128]{2,1,0:T(1,128)} %get-tuple-element.29), calls=%async_computation.2 | async-start | bytes 32768 | tf_op jit(solution)/shard_map/all_to_all | solution.py:314
  117.4 10.2 %all-to-all-done.2.norm = f32[32,1,128]{2,1,0:T(1,128)S(1)} async-done(((f32[32,1,128]{2,1,0:T(1,128)}), f32[32,1,128]{2,1,0:T(1,128)S(1)}, u32[]{:S(2)}, u32[]{:S(2)}) %all-to-all-start.2) | async-done | bytes 16416 | tf_op jit(solution)/shard_map/all_to_all | solution.py:314
  127.6 0.0 collective-permute-done.7.code.tail
  127.6 0.0 copy-done.1
  127.6 0.0 copy-done.2
  127.6 0.0 copy-done.5
  127.7 3.2 %update.1 = (f32[1536,128]{1,0:T(8,128)}, f32[1536,128]{1,0:T(8,128)}) custom-call(s16[1552,128]{1,0:T(8,128)(2,1)S(1)} %collective-permute-done.7.code.tail, s16[1552,128]{1,0:T(8,128)(2,1)S(1)} %collective-permute-done.7.code.tail, f32[32,1,128]{2,1,0:T(1,128)S(1)} %all-to-all-done.2.norm, f32[1]{0:T(128)S(6)} %copy.12.clip, f32[1536,128]{1,0:T(8,128)S(1)} %copy-done.1, ...), custom_call_target="tpu_custom_call" | custom-call | tf_op jit(solution)/shard_map/update/pallas_call | solution.py:317
Async XLA Ops:
  0.7 1.4 %copy-start = (bf16[1,48,16384]{2,1,0:T(8,128)(2,1)S(1)}, bf16[1,48,16384]{2,1,0:T(8,128)(2,1)}, u32[]{:S(2)}) copy-start(bf16[1,48,16384]{2,1,0:T(8,128)(2,1)} %g.1) | copy-start | bytes 4718596
  2.1 0.7 copy-start.6
  2.8 0.7 copy-start.7
  4.9 37.4 %collective-permute-start = (bf16[2,16,48,128]{3,2,1,0:T(8,128)(2,1)S(1)}, bf16[2,16,48,128]{3,2,1,0:T(8,128)(2,1)S(1)}, u32[]{:S(2)}, u32[]{:S(2)}) collective-permute-start(bf16[2,16,48,128]{3,2,1,0:T(8,128)(2,1)S(1)} %get-tuple-element.17), channel_id=1, source_target_pairs={{0,128},{128,256},{256,384},{384,0},{1,129},{129,257},{257,385},{3... | collective-permute-start | bytes 1179656 | tf_op jit(solution)/shard_map/ppermute | solution.py:279
  8.9 33.5 %collective-permute-start.1 = (bf16[2,16,48,128]{3,2,1,0:T(8,128)(2,1)S(1)}, bf16[2,16,48,128]{3,2,1,0:T(8,128)(2,1)S(1)}, u32[]{:S(2)}, u32[]{:S(2)}) collective-permute-start(bf16[2,16,48,128]{3,2,1,0:T(8,128)(2,1)S(1)} %get-tuple-element.18), channel_id=1, source_target_pairs={{0,256},{128,384},{256,0},{384,128},{1,257},{129,385},{257,1},{385... | collective-permute-start | bytes 1179656 | tf_op jit(solution)/shard_map/ppermute | solution.py:279
  13.2 29.1 %collective-permute-start.2 = (bf16[2,16,48,128]{3,2,1,0:T(8,128)(2,1)S(1)}, bf16[2,16,48,128]{3,2,1,0:T(8,128)(2,1)S(1)}, u32[]{:S(2)}, u32[]{:S(2)}) collective-permute-start(bf16[2,16,48,128]{3,2,1,0:T(8,128)(2,1)S(1)} %get-tuple-element.19), channel_id=1, source_target_pairs={{0,384},{128,0},{256,128},{384,256},{1,385},{129,1},{257,129},{385... | collective-permute-start | bytes 1179656 | tf_op jit(solution)/shard_map/ppermute | solution.py:279
  42.4 20.8 %copy-start.3 = (bf16[128,256]{1,0:T(8,128)(2,1)S(1)}, bf16[128,256]{1,0:T(8,128)(2,1)}, u32[]{:S(2)}) copy-start(bf16[128,256]{1,0:T(8,128)(2,1)} %constant.34.clone.refs_7_.wide) | copy-start | bytes 196612
  42.4 20.8 %copy-start.4 = (bf16[128,256]{1,0:T(8,128)(2,1)S(1)}, bf16[128,256]{1,0:T(8,128)(2,1)}, u32[]{:S(2)}) copy-start(bf16[128,256]{1,0:T(8,128)(2,1)} %constant.33.clone.refs_8_) | copy-start | bytes 196612
  42.4 6.9 %collective-permute-start.4 = (bf16[4,16,48,128]{3,2,1,0:T(8,128)(2,1)S(1)}, bf16[4,16,48,128]{3,2,1,0:T(8,128)(2,1)S(1)}, u32[]{:S(2)}, u32[]{:S(2)}) collective-permute-start(bf16[4,16,48,128]{3,2,1,0:T(8,128)(2,1)S(1)} %give.1), channel_id=1, source_target_pairs={{0,1},{1,0},{2,3},{3,2},{4,5},{5,4},{6,7},{7,6},{8,9},{9,8},{10,11... | collective-permute-start | bytes 2359304 | tf_op jit(solution)/shard_map/ppermute | solution.py:283
  49.9 13.2 %collective-permute-start.6 = (bf16[4,8,64,128]{3,2,1,0:T(8,128)(2,1)S(1)}, bf16[4,8,64,128]{3,2,1,0:T(8,128)(2,1)S(1)}, u32[]{:S(2)}, u32[]{:S(2)}) collective-permute-start(bf16[4,8,64,128]{3,2,1,0:T(8,128)(2,1)S(1)} %get-tuple-element.27), channel_id=1, source_target_pairs={{2,4},{4,2},{10,12},{12,10},{18,20},{20,18},{26,28},{28,26},{3,5},... | collective-permute-start | bytes 1572872 | tf_op jit(solution)/shard_map/ppermute | solution.py:297
  50.6 12.5 %collective-permute-start.5 = (bf16[4,4,96,128]{3,2,1,0:T(8,128)(2,1)S(1)}, bf16[4,4,96,128]{3,2,1,0:T(8,128)(2,1)S(1)}, u32[]{:S(2)}, u32[]{:S(2)}) collective-permute-start(bf16[4,4,96,128]{3,2,1,0:T(8,128)(2,1)S(1)} %get-tuple-element.26), channel_id=1, source_target_pairs={{0,2},{2,0},{4,6},{6,4},{8,10},{10,8},{12,14},{14,12},{16,18},{18,... | collective-permute-start | bytes 1179656 | tf_op jit(solution)/shard_map/ppermute | solution.py:296
  54.3 0.7 collective-permute-start.3
  66.1 61.5 %copy-start.1 = (f32[1536,128]{1,0:T(8,128)S(1)}, f32[1536,128]{1,0:T(8,128)}, u32[]{:S(2)}) copy-start(f32[1536,128]{1,0:T(8,128)} %params.1) | copy-start | bytes 2359300
  66.1 61.5 %copy-start.2 = (f32[1536,128]{1,0:T(8,128)S(1)}, f32[1536,128]{1,0:T(8,128)}, u32[]{:S(2)}) copy-start(f32[1536,128]{1,0:T(8,128)} %mom.1) | copy-start | bytes 2359300
  66.1 61.5 %copy-start.5 = (bf16[256,128]{1,0:T(8,128)(2,1)S(1)}, bf16[256,128]{1,0:T(8,128)(2,1)}, u32[]{:S(2)}) copy-start(bf16[256,128]{1,0:T(8,128)(2,1)} %constant.35.clone.tall) | copy-start | bytes 196612
  102.5 25.1 %collective-permute-start.7 = (s16[1552,128]{1,0:T(8,128)(2,1)S(1)}, s16[1552,128]{1,0:T(8,128)(2,1)S(1)}, u32[]{:S(2)}, u32[]{:S(2)}) collective-permute-start(s16[1552,128]{1,0:T(8,128)(2,1)S(1)} %get-tuple-element.28), channel_id=1, source_target_pairs={{0,0},{32,128},{64,256},{96,384},{128,32},{160,160},{192,288},{224... | collective-permute-start | bytes 1191944 | tf_op jit(solution)/shard_map/ppermute | solution.py:313
  103.2 24.4 %all-to-all-start.2 = ((f32[32,1,128]{2,1,0:T(1,128)}), f32[32,1,128]{2,1,0:T(1,128)S(1)}, u32[]{:S(2)}, u32[]{:S(2)}) async-start(f32[32,1,128]{2,1,0:T(1,128)} %get-tuple-element.29), calls=%async_computation.2 | async-start | bytes 32768 | tf_op jit(solution)/shard_map/all_to_all | solution.py:314

commit v12 on v10

--- a/solution.py
+++ b/solution.py
@@ -53,8 +53,17 @@
     return add_halves(dot(left, jnp.concatenate([top, low], axis=0)))
 
 
-def pack_kernel(pos, g, *outs):
+def pack_kernel(pos, picks, cuts, g, *outs):
     c, x = pos[1], pos[2]
+    lane = lax.broadcasted_iota(jnp.int32, (1, BS), 1)
+    for grp in range(4):
+        row = jnp.full((1, BS), -1, jnp.int32)
+        for r in range(NX):
+            for s in range(picks.shape[3]):
+                at = 4 * picks[r, 0, x, s] + r - 12 * grp
+                row = jnp.where(lane == at, jnp.maximum(row, cuts[r, 0, x, s]), row)
+        for n in range(4):
+            outs[NX][4 * grp + n] = row
     for s in range(NX):
         for half, core in enumerate((c, 1 - c)):
             base = NZ * NC * ((x + s) % 4) + core
@@ -249,17 +258,13 @@
     swap = [(NY * i + j, NX * j + i) for i in range(NX) for j in range(NY)]
     shape = jax.ShapeDtypeStruct
 
-    picks, cuts = (
-        lax.dynamic_index_in_dim(v[:, 0], lax.axis_index("x"), 1, keepdims=False) for v in (block_picks, cutoffs)
+    *packed, cut = call(
+        pack_kernel,
+        [shape((NC, NZ, rows, BS), BF16)] * NX + [shape((NZ, 1, BS), jnp.int32)],
+        (pos, block_picks, cutoffs, pseudo_grads),
+        "pack",
     )
-    hit = picks[:, :, None] == jnp.arange(BPO, dtype=jnp.int32)
-    cut = jnp.max(jnp.where(hit, cuts[:, :, None], -1), axis=1)
-    cut = jnp.broadcast_to(cut.T.reshape(4, 1, BPO), (4, 4, BPO)).reshape(NZ, 1, BPO)
-    cut = jnp.broadcast_to(jnp.pad(cut, ((0, 0), (0, 0), (0, BS - BPO))), (NZ, 16, BS))
-    cut, pseudo_grads = lax.optimization_barrier((cut, pseudo_grads))
     cut = lax.all_to_all(cut, "z", 0, 0, tiled=True)[:, 0]
-
-    packed = call(pack_kernel, [shape((NC, NZ, rows, BS), BF16)] * NX, (pos, pseudo_grads), "pack")
     spread = [packed[0]] + [
         lax.ppermute(packed[n], "x", [(i, (i + n) % NX) for i in range(NX)]) for n in range(1, NX)
     ]

time: 143 us -> 132 us (0.923)
  blocking collectives: 42.1 us -> 61.2 us
  starting transfers between devices: 52.2 us -> 35.6 us
  waiting for transfers between devices: 33.6 us -> 20.3 us
    all_to_all x0 -> x1, blocking collectives: none -> 26 us  [per_device(): cut = lax.all_to_all(cut, 'z', 0, 0, tiled=True)[:, 0]]
    all_to_all x1 -> x0, starting transfers between devices: 15.7 us -> none  [per_device(): cut = lax.all_to_all(cut, 'z', 0, 0, tiled=True)[:, 0]]
    ppermute x3, waiting for transfers between devices: 13.5 us -> 0.01 us  [per_device(): lax.ppermute(packed[n], 'x', [(i, (i + n) % NX) for i in range(NX)])]
    all_to_all x1, blocking collectives: 42.1 us -> 35.2 us  [per_device(): coded = lax.all_to_all(coded, 'z', 0, 0, tiled=True)]
    ppermute x1, starting transfers between devices: 5.69 us -> 3.68 us  [per_device(): a = lax.ppermute(a, 'z', pair_a)]
  transfers between devices with their start and end apart: 10 -> 9, of which waited for: 6 -> 3; matrix products, arithmetic and copies ran while one was open for 0% -> 0% of each run, Pallas kernels for 1% -> 0%
where the time goes in v12:
time: 132 us; the launch traced here: 131 us
  blocking collectives  61.2 us (46%)
  starting transfers between devices  35.6 us (27%)
  waiting for transfers between devices  20.3 us (15%)
  Pallas kernels  9.24 us (7%)
  local copies, waits for them, and re-layouts  2.84 us (2%)
  between operations  1.47 us (1%)
    all_to_all x1, blocking collectives, per_device(): coded = lax.all_to_all(coded, 'z', 0, 0, tiled=True)  35.2 us
    all_to_all x1, blocking collectives, per_device(): cut = lax.all_to_all(cut, 'z', 0, 0, tiled=True)[:, 0]  26 us
    all_to_all x1, starting transfers between devices, per_device(): norm = lax.all_to_all(norm, ('x', 'y', 'c'), 0, 0, tiled=True)  13.6 us
    ppermute x3, starting transfers between devices, per_device(): lax.ppermute(packed[n], 'x', [(i, (i + n) % NX) for i in range(NX)])  11.4 us
    all_to_all x1, waiting for transfers between devices, per_device(): norm = lax.all_to_all(norm, ('x', 'y', 'c'), 0, 0, tiled=True)  10.2 us
    ppermute x1, waiting for transfers between devices, per_device(): a = lax.ppermute(a, 'z', pair_a)  8.17 us
    pallas_call x5, Pallas kernels, call(): pl.pallas_call(kernel, out_shape=out_shape, in_specs=[SMEM if i.dtype ==...  6.14 us
    ppermute x1, starting transfers between devices, per_device(): spread.append(lax.ppermute(give, 'c', [(0, 1), (1, 0)]))  4.98 us
  transfers between devices with their start and end apart: 9, of which 3 were waited for; matrix products, arithmetic and copies ran while one was open for 0% of the time, Pallas kernels for 0%

profile of v12, /device:TPU:1, one launch (start us, length us, event | category | flops | bytes accessed | tf_op | source)
XLA Modules:
  0.0 130.8 jit_solution(11316934582085945900)
XLA Ops:
  0.6 0.1 pad_add_fusion.pos
  0.7 0.0 copy-start
  0.7 1.4 %copy-done = bf16[1,48,16384]{2,1,0:T(8,128)(2,1)S(1)} copy-done((bf16[1,48,16384]{2,1,0:T(8,128)(2,1)S(1)}, bf16[1,48,16384]{2,1,0:T(8,128)(2,1)}, u32[]{:S(2)}) %copy-start) | copy-done | bytes 1572888
  2.1 0.0 copy-start.6
  2.1 0.7 copy-done.6
  2.8 0.0 copy-start.7
  2.8 0.7 copy-done.7
  3.5 1.4 %pack.1 = (bf16[2,16,48,128]{3,2,1,0:T(8,128)(2,1)S(1)}, bf16[2,16,48,128]{3,2,1,0:T(8,128)(2,1)S(1)}, bf16[2,16,48,128]{3,2,1,0:T(8,128)(2,1)S(1)}, bf16[2,16,4...) custom-call(s32[3]{0:T(128)S(1)} %pad_add_fusion.pos, s32[4,1,4,6]{3,2,1,0:T(4,128)S(1)} %copy-done.6, ...), custom_call_target="tpu_custom_call" | custom-call | tf_op jit(solution)/shard_map/pack/pallas_call | solution.py:239
  4.9 3.9 %collective-permute-start = (bf16[2,16,48,128]{3,2,1,0:T(8,128)(2,1)S(1)}, bf16[2,16,48,128]{3,2,1,0:T(8,128)(2,1)S(1)}, u32[]{:S(2)}, u32[]{:S(2)}) collective-permute-start(bf16[2,16,48,128]{3,2,1,0:T(8,128)(2,1)S(1)} %get-tuple-element.17), channel_id=1, source_target_pairs={{0,128},{128,256},{256,384},{384,0},{1,129},{129,257},{257,385},{3... | collective-permute-start | bytes 1179656 | tf_op jit(solution)/shard_map/ppermute | solution.py:269
  8.9 4.4 %collective-permute-start.1 = (bf16[2,16,48,128]{3,2,1,0:T(8,128)(2,1)S(1)}, bf16[2,16,48,128]{3,2,1,0:T(8,128)(2,1)S(1)}, u32[]{:S(2)}, u32[]{:S(2)}) collective-permute-start(bf16[2,16,48,128]{3,2,1,0:T(8,128)(2,1)S(1)} %get-tuple-element.18), channel_id=1, source_target_pairs={{0,256},{128,384},{256,0},{384,128},{1,257},{129,385},{257,1},{385... | collective-permute-start | bytes 1179656 | tf_op jit(solution)/shard_map/ppermute | solution.py:269
  13.2 3.1 %collective-permute-start.2 = (bf16[2,16,48,128]{3,2,1,0:T(8,128)(2,1)S(1)}, bf16[2,16,48,128]{3,2,1,0:T(8,128)(2,1)S(1)}, u32[]{:S(2)}, u32[]{:S(2)}) collective-permute-start(bf16[2,16,48,128]{3,2,1,0:T(8,128)(2,1)S(1)} %get-tuple-element.19), channel_id=1, source_target_pairs={{0,384},{128,0},{256,128},{384,256},{1,385},{129,1},{257,129},{385... | collective-permute-start | bytes 1179656 | tf_op jit(solution)/shard_map/ppermute | solution.py:269
  16.3 26.0 %all_to_all.15 = s32[16,1,128]{2,1,0:T(1,128)S(1)} all-to-all(s32[16,1,128]{2,1,0:T(1,128)S(1)} %get-tuple-element.20), channel_id=1, replica_groups=mesh['x'=4,'y'=4,'z'=16,'c'=2] {'z'}, dimensions={0} | all-to-all | bytes 16384 | tf_op jit(solution)/shard_map/all_to_all | solution.py:267
  42.3 0.0 collective-permute-done.refs_1_
  42.3 0.0 collective-permute-done.1.refs_2_
  42.3 0.0 collective-permute-done.2.refs_3_
  42.3 0.1 give.1
  42.4 0.0 copy-start.3
  42.4 0.0 copy-start.5
  42.4 5.0 %collective-permute-start.4 = (bf16[4,16,48,128]{3,2,1,0:T(8,128)(2,1)S(1)}, bf16[4,16,48,128]{3,2,1,0:T(8,128)(2,1)S(1)}, u32[]{:S(2)}, u32[]{:S(2)}) collective-permute-start(bf16[4,16,48,128]{3,2,1,0:T(8,128)(2,1)S(1)} %give.1), channel_id=1, source_target_pairs={{0,1},{1,0},{2,3},{3,2},{4,5},{5,4},{6,7},{7,6},{8,9},{9,8},{10,11... | collective-permute-start | bytes 2359304 | tf_op jit(solution)/shard_map/ppermute | solution.py:273
  47.4 1.9 %collective-permute-done.4.refs_4_ = bf16[4,16,48,128]{3,2,1,0:T(8,128)(2,1)S(1)} collective-permute-done((bf16[4,16,48,128]{3,2,1,0:T(8,128)(2,1)S(1)}, bf16[4,16,48,128]{3,2,1,0:T(8,128)(2,1)S(1)}, u32[]{:S(2)}, u32[]{:S(2)}) %collective-permute-start.4) | collective-permute-done | bytes 786464 | tf_op jit(solution)/shard_map/ppermute | solution.py:273
  49.3 0.6 exchange.1
  49.9 0.7 collective-permute-start.6
  50.6 3.7 %collective-permute-start.5 = (bf16[4,4,96,128]{3,2,1,0:T(8,128)(2,1)S(1)}, bf16[4,4,96,128]{3,2,1,0:T(8,128)(2,1)S(1)}, u32[]{:S(2)}, u32[]{:S(2)}) collective-permute-start(bf16[4,4,96,128]{3,2,1,0:T(8,128)(2,1)S(1)} %get-tuple-element.26), channel_id=1, source_target_pairs={{0,2},{2,0},{4,6},{6,4},{8,10},{10,8},{12,14},{14,12},{16,18},{18,... | collective-permute-start | bytes 1179656 | tf_op jit(solution)/shard_map/ppermute | solution.py:286
  54.3 0.7 collective-permute-start.3
  55.0 0.0 collective-permute-done.3.cut
  55.0 8.2 %collective-permute-done.5.refs_5_ = bf16[4,4,96,128]{3,2,1,0:T(8,128)(2,1)S(1)} collective-permute-done((bf16[4,4,96,128]{3,2,1,0:T(8,128)(2,1)S(1)}, bf16[4,4,96,128]{3,2,1,0:T(8,128)(2,1)S(1)}, u32[]{:S(2)}, u32[]{:S(2)}) %collective-permute-start.5) | collective-permute-done | bytes 393248 | tf_op jit(solution)/shard_map/ppermute | solution.py:286
  63.2 0.0 collective-permute-done.6.refs_6_
  63.2 0.0 copy-done.3
  63.2 0.0 copy-done.5
  63.2 2.9 %forward.1 = s16[16,144,128]{2,1,0:T(8,128)(2,1)S(1)} custom-call(s32[3]{0:T(128)S(1)} %pad_add_fusion.pos, s32[16,128]{1,0:T(8,128)S(1)} %collective-permute-done.3.cut, bf16[2,16,48,128]{3,2,1,0:T(8,128)(2,1)S(1)} %get-tuple-element.22.refs_0_, bf16[2,16,48,128]{3,2,1,0:T(8,128)(2,1)S(1)} %collective-permute-done.refs_1_, ...), custom_call_target="tpu_custom_call" | custom-call | tf_op jit(solution)/shard_map/forward/pallas_call | solution.py:239
  66.1 0.0 copy-start.1
  66.1 0.0 copy-start.2
  66.1 0.0 copy-start.4
  66.1 35.2 %all_to_all.16.z = s16[16,144,128]{2,1,0:T(8,128)(2,1)S(1)} all-to-all(s16[16,144,128]{2,1,0:T(8,128)(2,1)S(1)} %forward.1), channel_id=1, replica_groups=mesh['x'=4,'y'=4,'z'=16,'c'=2] {'z'}, dimensions={0} | all-to-all | bytes 1179648 | tf_op jit(solution)/shard_map/all_to_all | solution.py:296
  101.3 1.2 compact.1
  102.5 0.7 collective-permute-start.7
  103.2 13.6 %all-to-all-start.2 = ((f32[32,1,128]{2,1,0:T(1,128)}), f32[32,1,128]{2,1,0:T(1,128)S(1)}, u32[]{:S(2)}, u32[]{:S(2)}) async-start(f32[32,1,128]{2,1,0:T(1,128)} %get-tuple-element.29), calls=%async_computation.2 | async-start | bytes 32768 | tf_op jit(solution)/shard_map/all_to_all | solution.py:304
  117.4 10.2 %all-to-all-done.2.norm = f32[32,1,128]{2,1,0:T(1,128)S(1)} async-done(((f32[32,1,128]{2,1,0:T(1,128)}), f32[32,1,128]{2,1,0:T(1,128)S(1)}, u32[]{:S(2)}, u32[]{:S(2)}) %all-to-all-start.2) | async-done | bytes 16416 | tf_op jit(solution)/shard_map/all_to_all | solution.py:304
  127.6 0.0 collective-permute-done.7.code.tail
  127.6 0.0 copy-done.1
  127.6 0.0 copy-done.2
  127.6 0.0 copy-done.4
  127.7 3.1 %update.1 = (f32[1536,128]{1,0:T(8,128)}, f32[1536,128]{1,0:T(8,128)}) custom-call(s16[1552,128]{1,0:T(8,128)(2,1)S(1)} %collective-permute-done.7.code.tail, s16[1552,128]{1,0:T(8,128)(2,1)S(1)} %collective-permute-done.7.code.tail, f32[32,1,128]{2,1,0:T(1,128)S(1)} %all-to-all-done.2.norm, f32[1]{0:T(128)S(6)} %copy.12.clip, f32[1536,128]{1,0:T(8,128)S(1)} %copy-done.1, ...), custom_call_target="tpu_custom_call" | custom-call | tf_op jit(solution)/shard_map/update/pallas_call | solution.py:307
Async XLA Ops:
  0.7 1.4 %copy-start = (bf16[1,48,16384]{2,1,0:T(8,128)(2,1)S(1)}, bf16[1,48,16384]{2,1,0:T(8,128)(2,1)}, u32[]{:S(2)}) copy-start(bf16[1,48,16384]{2,1,0:T(8,128)(2,1)} %g.1) | copy-start | bytes 4718596
  2.1 0.7 copy-start.6
  2.8 0.7 copy-start.7
  4.9 37.4 %collective-permute-start = (bf16[2,16,48,128]{3,2,1,0:T(8,128)(2,1)S(1)}, bf16[2,16,48,128]{3,2,1,0:T(8,128)(2,1)S(1)}, u32[]{:S(2)}, u32[]{:S(2)}) collective-permute-start(bf16[2,16,48,128]{3,2,1,0:T(8,128)(2,1)S(1)} %get-tuple-element.17), channel_id=1, source_target_pairs={{0,128},{128,256},{256,384},{384,0},{1,129},{129,257},{257,385},{3... | collective-permute-start | bytes 1179656 | tf_op jit(solution)/shard_map/ppermute | solution.py:269
  8.9 33.5 %collective-permute-start.1 = (bf16[2,16,48,128]{3,2,1,0:T(8,128)(2,1)S(1)}, bf16[2,16,48,128]{3,2,1,0:T(8,128)(2,1)S(1)}, u32[]{:S(2)}, u32[]{:S(2)}) collective-permute-start(bf16[2,16,48,128]{3,2,1,0:T(8,128)(2,1)S(1)} %get-tuple-element.18), channel_id=1, source_target_pairs={{0,256},{128,384},{256,0},{384,128},{1,257},{129,385},{257,1},{385... | collective-permute-start | bytes 1179656 | tf_op jit(solution)/shard_map/ppermute | solution.py:269
  13.2 29.1 %collective-permute-start.2 = (bf16[2,16,48,128]{3,2,1,0:T(8,128)(2,1)S(1)}, bf16[2,16,48,128]{3,2,1,0:T(8,128)(2,1)S(1)}, u32[]{:S(2)}, u32[]{:S(2)}) collective-permute-start(bf16[2,16,48,128]{3,2,1,0:T(8,128)(2,1)S(1)} %get-tuple-element.19), channel_id=1, source_target_pairs={{0,384},{128,0},{256,128},{384,256},{1,385},{129,1},{257,129},{385... | collective-permute-start | bytes 1179656 | tf_op jit(solution)/shard_map/ppermute | solution.py:269
  42.4 20.8 %copy-start.3 = (bf16[128,256]{1,0:T(8,128)(2,1)S(1)}, bf16[128,256]{1,0:T(8,128)(2,1)}, u32[]{:S(2)}) copy-start(bf16[128,256]{1,0:T(8,128)(2,1)} %constant.33.clone.refs_8_.left) | copy-start | bytes 196612
  42.4 20.8 %copy-start.5 = (bf16[128,256]{1,0:T(8,128)(2,1)S(1)}, bf16[128,256]{1,0:T(8,128)(2,1)}, u32[]{:S(2)}) copy-start(bf16[128,256]{1,0:T(8,128)(2,1)} %constant.34.clone.refs_7_) | copy-start | bytes 196612
  42.4 6.9 %collective-permute-start.4 = (bf16[4,16,48,128]{3,2,1,0:T(8,128)(2,1)S(1)}, bf16[4,16,48,128]{3,2,1,0:T(8,128)(2,1)S(1)}, u32[]{:S(2)}, u32[]{:S(2)}) collective-permute-start(bf16[4,16,48,128]{3,2,1,0:T(8,128)(2,1)S(1)} %give.1), channel_id=1, source_target_pairs={{0,1},{1,0},{2,3},{3,2},{4,5},{5,4},{6,7},{7,6},{8,9},{9,8},{10,11... | collective-permute-start | bytes 2359304 | tf_op jit(solution)/shard_map/ppermute | solution.py:273
  49.9 13.2 %collective-permute-start.6 = (bf16[4,8,64,128]{3,2,1,0:T(8,128)(2,1)S(1)}, bf16[4,8,64,128]{3,2,1,0:T(8,128)(2,1)S(1)}, u32[]{:S(2)}, u32[]{:S(2)}) collective-permute-start(bf16[4,8,64,128]{3,2,1,0:T(8,128)(2,1)S(1)} %get-tuple-element.27), channel_id=1, source_target_pairs={{2,4},{4,2},{10,12},{12,10},{18,20},{20,18},{26,28},{28,26},{3,5},... | collective-permute-start | bytes 1572872 | tf_op jit(solution)/shard_map/ppermute | solution.py:287
  50.6 12.5 %collective-permute-start.5 = (bf16[4,4,96,128]{3,2,1,0:T(8,128)(2,1)S(1)}, bf16[4,4,96,128]{3,2,1,0:T(8,128)(2,1)S(1)}, u32[]{:S(2)}, u32[]{:S(2)}) collective-permute-start(bf16[4,4,96,128]{3,2,1,0:T(8,128)(2,1)S(1)} %get-tuple-element.26), channel_id=1, source_target_pairs={{0,2},{2,0},{4,6},{6,4},{8,10},{10,8},{12,14},{14,12},{16,18},{18,... | collective-permute-start | bytes 1179656 | tf_op jit(solution)/shard_map/ppermute | solution.py:286
  54.3 0.7 collective-permute-start.3
  66.1 61.5 %copy-start.1 = (f32[1536,128]{1,0:T(8,128)S(1)}, f32[1536,128]{1,0:T(8,128)}, u32[]{:S(2)}) copy-start(f32[1536,128]{1,0:T(8,128)} %params.1) | copy-start | bytes 2359300
  66.1 61.5 %copy-start.2 = (f32[1536,128]{1,0:T(8,128)S(1)}, f32[1536,128]{1,0:T(8,128)}, u32[]{:S(2)}) copy-start(f32[1536,128]{1,0:T(8,128)} %mom.1) | copy-start | bytes 2359300
  66.1 61.5 %copy-start.4 = (bf16[256,256]{1,0:T(8,128)(2,1)S(1)}, bf16[256,256]{1,0:T(8,128)(2,1)}, u32[]{:S(2)}) copy-start(bf16[256,256]{1,0:T(8,128)(2,1)} %constant.35.clone.full) | copy-start | bytes 393220
  102.5 25.1 %collective-permute-start.7 = (s16[1552,128]{1,0:T(8,128)(2,1)S(1)}, s16[1552,128]{1,0:T(8,128)(2,1)S(1)}, u32[]{:S(2)}, u32[]{:S(2)}) collective-permute-start(s16[1552,128]{1,0:T(8,128)(2,1)S(1)} %get-tuple-element.28), channel_id=1, source_target_pairs={{0,0},{32,128},{64,256},{96,384},{128,32},{160,160},{192,288},{224... | collective-permute-start | bytes 1191944 | tf_op jit(solution)/shard_map/ppermute | solution.py:303
  103.2 24.4 %all-to-all-start.2 = ((f32[32,1,128]{2,1,0:T(1,128)}), f32[32,1,128]{2,1,0:T(1,128)S(1)}, u32[]{:S(2)}, u32[]{:S(2)}) async-start(f32[32,1,128]{2,1,0:T(1,128)} %get-tuple-element.29), calls=%async_computation.2 | async-start | bytes 32768 | tf_op jit(solution)/shard_map/all_to_all | solution.py:304
